TPU v7x, 256 devices: a whole 4x4x8 slice. The times are simulated.
256 devices in a mesh: section: 16 (over z, y_lo), fsdp: 16 (over y_hi, x, core).
Axes of the slice: x: 4, y: 4 (y_hi: 2, y_lo: 2; y = y_hi * 2 + y_lo), z: 8, core: 2. Of those that a mesh axis runs over, the one named last changes fastest.
Arguments:
- inputs: bfloat16 [8, 512, 6144], P(None, 'fsdp'), may hold values from -6 to 6
- out_grad: bfloat16 [8, 512, 6144], P(None, 'fsdp'), may hold values from -0.119628906 to 0.119628906
- down_proj: bfloat16 [16, 6144, 128], P('section', 'fsdp'), may hold values from -0.078125 to 0.078125
- gain: bfloat16 [16, 6144], P('section', 'fsdp'), may hold values from 0.5 to 1.5
- up_proj: bfloat16 [16, 128, 6144], P('section', None, 'fsdp'), may hold values from -0.5 to 0.5
Outputs:
- grad_down: float32 [16, 6144, 128], P('section', 'fsdp')
- grad_gain: float32 [16, 6144], P('section', 'fsdp')
- grad_up: float32 [16, 128, 6144], P('section', None, 'fsdp')
All inputs are finite; a program needn't handle non-finite values.
Results may differ from a plain program's by a relative error of at most 0.04.
Values may be sent and summed in bfloat16 or wider, within the bound.
No kernel may reach another device: no remote copies, remote signals or barrier semaphores. Data moves between devices by JAX's collectives and lax.ppermute only.
A program may use at most 64 MiB of HBM per device.

v0:
```python
import functools

import jax
import jax.numpy as jnp
from jax import lax
from jax.experimental import pallas as pl
from jax.experimental.pallas import tpu as pltpu
from jax.sharding import PartitionSpec as P

F32 = jnp.float32
BF16 = jnp.bfloat16
NN = ((1,), (0,))
NT = ((1,), (1,))
TN = ((0,), (0,))
MIB = 2**20


def dot(a, b, dims):
    return lax.dot_general(a, b, (dims, ((), ())), preferred_element_type=F32)


def hop(block, axis, stride, count, offset):
    route = []
    for i in range(lax.axis_size(axis)):
        place = (i // stride) % count
        route.append((i, i + ((place + offset) % count - place) * stride))
    return lax.ppermute(block, axis, route)


def swap(block):
    return hop(block, "fsdp", 1, 2, 1)


def across(block):
    route = []
    for section in range(16):
        for group in range(16):
            to = (section ^ 1) * 16 + (group ^ 8)
            route.append((section * 16 + group, to))
    return lax.ppermute(block, ("section", "fsdp"), route)


def gather_pieces(shard):
    left = hop(shard, "fsdp", 2, 4, 1)
    right = hop(shard, "fsdp", 2, 4, -1)
    other = hop(shard, "fsdp", 8, 2, 1)
    far = hop(left, "fsdp", 2, 4, 1)
    other_left = hop(other, "fsdp", 2, 4, 1)
    other_right = hop(other, "fsdp", 2, 4, -1)
    other_far = hop(other_right, "fsdp", 2, 4, -1)
    near = [shard, left, right, other, far, other_left, other_right, other_far]
    return near + [swap(piece) for piece in near]


def gather_table(slab):
    half = slab.shape[0] // 2
    slab_swap = swap(slab)
    left = hop(slab, "fsdp", 2, 4, 1)
    right = hop(slab, "fsdp", 2, 4, -1)
    other = across(slab)
    far_a = hop(left[:half], "fsdp", 2, 4, 1)
    far_b = hop(right[half:], "fsdp", 2, 4, -1)
    other, slab_swap = lax.optimization_barrier((other, slab_swap))
    other_left = hop(other, "fsdp", 2, 4, 1)
    other_right = hop(other, "fsdp", 2, 4, -1)
    early = [swap(left), swap(right), swap(other)]
    far_a, far_b, early = lax.optimization_barrier((far_a, far_b, early))
    other_far = [across(far_a), across(far_b)]
    near = [slab, left, right, other, far_a, far_b, other_left, other_right] + other_far
    late = [swap(piece) for piece in near[4:]]
    return near + [slab_swap] + early + late


def places():
    me = lax.axis_index("fsdp")
    y, x, core = me // 8, (me // 2) % 4, me % 2
    steps = ((0, 0), (0, 3), (0, 1), (1, 0), (0, 2), (1, 3), (1, 1), (1, 2))
    found = []
    for c in (core, 1 - core):
        for i, o in steps:
            found.append(jnp.where(i == 0, y, 1 - y) * 8 + ((x + o) % 4) * 2 + c)
    return jnp.stack(found).astype(jnp.int32)


def gather_section(block):
    return lax.all_to_all(
        jnp.broadcast_to(block[None], (16,) + block.shape), "section", 0, 0, tiled=True
    )


def along_y(block):
    mate = hop(block, "section", 1, 2, 1)
    even = lax.axis_index("section") % 2 == 0
    return jnp.stack([jnp.where(even, block, mate), jnp.where(even, mate, block)])


def along_z(pair):
    planes = [list(range(y, 16, 2)) for y in range(2)]
    whole = lax.all_gather(pair, "section", axis=0, axis_index_groups=planes)
    return whole.reshape((16,) + pair.shape[1:])


def add(keep, got):
    return (keep.astype(F32) + got.astype(F32)).astype(BF16)


def among_chips(chunks):
    chips = [list(range(core, 16, 2)) for core in range(2)]
    return lax.all_to_all(chunks, "fsdp", 0, 0, tiled=True, axis_index_groups=chips)


def project(place_ref, x_ref, y_ref, *rest):
    pieces = rest[:16]
    out_ref, w_ref, xv_ref, yv_ref, sem = rest[16:]
    size, rank = pieces[0].shape[0], pieces[0].shape[1] // 2
    copies = [pltpu.make_async_copy(x_ref, xv_ref, sem.at[16])]
    for at, piece in enumerate(pieces):
        span = pl.ds(pl.multiple_of(place_ref[at] * size, size), size)
        copies.append(pltpu.make_async_copy(piece, w_ref.at[span, :], sem.at[at]))
    last = pltpu.make_async_copy(y_ref, yv_ref, sem.at[17])
    for copy in copies + [last]:
        copy.start()
    for copy in copies:
        copy.wait()
    out_ref[:, : 2 * rank] = dot(xv_ref[...], w_ref[...], NN).astype(BF16)
    last.wait()
    out_ref[:, 2 * rank :] = dot(yv_ref[...], w_ref[:, rank:], NN).astype(BF16)


def chain(width, s_ref, place_ref, a_hbm, norm_ref, *rest):
    pieces = rest[:20]
    pick_ref, keep_ref, send_ref = rest[20:23]
    z_ref, a_ref, w_ref, lift_ref, act_ref, slope_ref, inv_ref = rest[23:30]
    q_ref, p_ref, sq_ref, sums_ref, sem = rest[30:]
    layers = a_ref.shape[0]
    rank = z_ref.shape[2]
    cut = [slice(rank * i, rank * (i + 1)) for i in range(layers)]
    parts, many = 4, layers // 4
    first = pltpu.make_async_copy(a_hbm, a_ref, sem.at[parts, 0])
    first.start()
    copies = []
    for part in range(parts):
        some = pl.ds(part * many, many)
        for at, whole in enumerate((0, 1, 2, 3, None, 6, 7, None) * 2):
            first_of = 10 * (at // 8)
            if whole is not None:
                piece = pieces[first_of + whole].at[some]
            else:
                half = first_of + (4 if at % 8 == 4 else 8) + part // 2
                piece = pieces[half].at[pl.ds(part % 2 * many, many)]
            span = pl.ds(pl.multiple_of(place_ref[at] * rank, rank), rank)
            copy = pltpu.make_async_copy(piece, z_ref.at[some, span, :], sem.at[part, at])
            copy.start()
            copies.append(copy)
    first.wait()
    for s in range(layers):
        w_ref[s] = a_ref[s, :, cut[1]].astype(F32)
        lift_ref[s] = a_ref[s, :, cut[2]].astype(F32)
    scale = 1.0 / width
    total = norm_ref[...]
    for s in range(layers):
        if s % many == 0:
            for copy in copies[16 * (s // many) : 16 * (s // many) + 16]:
                copy.wait()
        inverse = lax.rsqrt(jnp.maximum(total, 0.0) * scale + 1e-05)
        raw = a_ref[s, :, cut[0]].astype(F32)
        if s > 0:
            raw = raw + dot(q_ref[:, : rank * s], z_ref[s, : rank * s, :], NN)
        act = raw * inverse
        sigma = jax.nn.sigmoid(act)
        now = (act * sigma).astype(BF16)
        q_ref[:, cut[s]] = now
        slope_ref[s] = sigma * (1.0 + act * (1.0 - sigma))
        act_ref[s] = act
        inv_ref[s] = jnp.broadcast_to(inverse, act.shape)
        wide = now.astype(F32)
        ahead = dot(now, z_ref[s, rank * s :, :], NT)
        own = ahead[:, :rank]
        here = w_ref[s]
        total = total + jnp.sum(wide * (2.0 * here + own), axis=1, keepdims=True)
        w_ref[s] = here + own
        for k in range(s + 1, layers):
            w_ref[k] += ahead[:, cut[k - s]]
    shrink = jnp.zeros_like(total)
    for s in range(layers - 1, -1, -1):
        up = lift_ref[s]
        if s + 1 < layers:
            up = up - shrink * w_ref[s]
            up = up - dot(sq_ref[:, rank * (s + 1) :], z_ref[s, rank * (s + 1) :, :], NN)
        grad = (up * slope_ref[s]).astype(BF16).astype(F32)
        inverse = inv_ref[s]
        now = (grad * inverse).astype(BF16)
        p_ref[:, cut[s]] = now
        sq_ref[:, cut[s]] = (shrink * q_ref[:, cut[s]].astype(F32)).astype(BF16)
        if s > 0:
            back = dot(now, z_ref[s, : rank * s, :], NT)
            for k in range(s):
                lift_ref[k] += back[:, cut[k]]
        mean = jnp.sum(grad * act_ref[s] * inverse * inverse, axis=1, keepdims=True) * scale
        shrink = shrink + mean
    here = pl.ds(pl.multiple_of(s_ref[0] * rank, rank), rank)
    p_t, q_t, sq_t = p_ref[:, here].T, q_ref[:, here].T, sq_ref[:, here].T
    both = jnp.concatenate([p_t, -sq_t], axis=0)
    pick_ref[: 2 * rank] = both
    pick_ref[2 * rank :] = q_t
    for j in range(layers):

        @pl.when(j < s_ref[0])
        def _():
            sums_ref[...] = dot(both, q_ref[:, cut[j]], NN).astype(BF16)

        @pl.when(j >= s_ref[0])
        def _():
            first = dot(q_t, p_ref[:, cut[j]], NN)
            first = jnp.where(j == s_ref[0], 0.0, first)
            sums_ref[:rank] = first.astype(BF16)
            sums_ref[rank:] = (-dot(q_t, sq_ref[:, cut[j]], NN)).astype(BF16)

        @pl.when(s_ref[1] == j % 2)
        def _():
            keep_ref[j // 2] = sums_ref[...]

        @pl.when(s_ref[1] != j % 2)
        def _():
            send_ref[j // 2] = sums_ref[...]


def chain_call(width, here, place, projected, norm, table):
    sections, tokens, wide = projected.shape
    rank = wide // 3
    smem = pl.BlockSpec(memory_space=pltpu.SMEM)
    vmem = pl.BlockSpec(memory_space=pltpu.VMEM)
    in_hbm = pl.BlockSpec(memory_space=pltpu.HBM)
    big = pltpu.VMEM((sections, tokens, rank), F32)
    flat = pltpu.VMEM((tokens, sections * rank), BF16)
    return pl.pallas_call(
        functools.partial(chain, width),
        out_shape=(
            jax.ShapeDtypeStruct((3 * rank, tokens), BF16),
            jax.ShapeDtypeStruct((8, 2 * rank, rank), BF16),
            jax.ShapeDtypeStruct((8, 2 * rank, rank), BF16),
        ),
        in_specs=[smem, smem, in_hbm, vmem] + [in_hbm] * 20,
        out_specs=(vmem,) * 3,
        scratch_shapes=[pltpu.VMEM((sections, sections * rank, rank), BF16)]
        + [pltpu.VMEM((sections, tokens, wide), BF16)]
        + [big] * 5
        + [flat] * 3
        + [pltpu.VMEM((2 * rank, rank), BF16), pltpu.SemaphoreType.DMA((5, 16))],
        compiler_params=pltpu.CompilerParams(vmem_limit_bytes=57 * MIB),
        cost_estimate=pl.CostEstimate(
            flops=2 * 10**10, bytes_accessed=12 * MIB, transcendentals=10**6
        ),
        name="chain",
    )(here, place, projected, norm, *table)


def outer(s_ref, pick_ref, x_hbm, y_hbm, keep_ref, send_ref, x_ref, y_ref, sem):
    rank = pick_ref.shape[0] // 3
    half, _, piece = keep_ref.shape
    first = s_ref[1] == 0
    copies = []
    for i in range(half):
        span = pl.ds(2 * piece * i, 2 * piece)
        for k, (far, near) in enumerate(((x_hbm, x_ref), (y_hbm, y_ref))):
            copies.append(pltpu.make_async_copy(far.at[:, span], near.at[:, span], sem.at[k, i]))
            copies[-1].start()
    for i in range(half):
        span = slice(2 * piece * i, 2 * piece * (i + 1))
        copies[2 * i].wait()
        copies[2 * i + 1].wait()
        from_x = dot(pick_ref[: 2 * rank], x_ref[:, span], NN)
        from_y = dot(pick_ref[2 * rank :], y_ref[:, span], NN)
        both = jnp.concatenate([from_x[:rank], from_x[rank:] + from_y], axis=0).astype(BF16)
        even, odd = both[:, :piece], both[:, piece:]
        keep_ref[i] = jnp.where(first, even, odd)
        send_ref[i] = jnp.where(first, odd, even)


def finish(s_ref, part_ref, mate_ref, up_hbm, down_hbm, own_ref, gain_ref, *rest):
    down_out, gain_out, up_out, up_ref, down_ref, sem = rest
    copies = [
        pltpu.make_async_copy(up_hbm, up_ref, sem.at[0]),
        pltpu.make_async_copy(down_hbm, down_ref, sem.at[1]),
    ]
    for copy in copies:
        copy.start()
    layers, rank, piece = up_ref.shape
    held = part_ref[0, :, :piece].astype(F32)
    for k in range(1, part_ref.shape[0]):
        held = held + part_ref[k, :, :piece].astype(F32)
    first = s_ref[1] == 0
    zero = jnp.zeros((rank, rank), BF16)
    masked, after = [], []
    for j in range(layers):
        ours, theirs = part_ref[j // 2, :, piece:], mate_ref[j // 2]
        sums = jnp.where(first == (j % 2 == 0), ours, theirs)
        before = jnp.where(j < s_ref[0], sums[:rank], zero)
        masked.append(jnp.concatenate([before, sums[rank:]], axis=0))
        after.append(jnp.where(j > s_ref[0], sums[:rank], zero))
    for copy in copies:
        copy.wait()
    held = held + dot(jnp.concatenate(masked, axis=1), up_ref[...].reshape(-1, piece), NN)
    held_up = held[rank:]
    for k in range(layers):
        held_up = held_up + dot(after[k], down_ref[k], NT)
    up_out[...] = held_up
    held_down = held[:rank]
    down_out[...] = (held_down * gain_ref[...]).T
    gain_out[...] = jnp.sum(own_ref[...].astype(F32).T * held_down, axis=0, keepdims=True)


def on_device(inputs, out_grad, down_proj, gain, up_proj):
    sections, groups = lax.axis_size("section"), lax.axis_size("fsdp")
    s = lax.axis_index("section")
    here = jnp.stack([s, lax.axis_index("fsdp") % 2]).astype(jnp.int32)
    place = places()
    width = inputs.shape[2]
    x = inputs.reshape(-1, width)
    y = out_grad.reshape(-1, width)
    tokens = x.shape[0]
    down, gain_row, up = down_proj[0], gain[0].astype(F32), up_proj[0]
    piece, rank = down.shape
    smem = pl.BlockSpec(memory_space=pltpu.SMEM)
    vmem = pl.BlockSpec(memory_space=pltpu.VMEM)
    in_hbm = pl.BlockSpec(memory_space=pltpu.HBM)

    scaled_down = (down.astype(F32) * gain_row[:, None]).astype(BF16)
    weights = jnp.concatenate([scaled_down, up.T], axis=1)
    up_all = along_z(along_y(up))

    projected = pl.pallas_call(
        project,
        out_shape=jax.ShapeDtypeStruct((tokens, 3 * rank), BF16),
        in_specs=[smem] + [in_hbm] * 18,
        out_specs=vmem,
        scratch_shapes=[
            pltpu.VMEM((width, 2 * rank), BF16),
            pltpu.VMEM(x.shape, BF16),
            pltpu.VMEM(y.shape, BF16),
            pltpu.SemaphoreType.DMA((18,)),
        ],
        compiler_params=pltpu.CompilerParams(vmem_limit_bytes=57 * MIB),
        name="project",
    )(place, x, y, *gather_pieces(weights))
    up_all, projected, late = lax.optimization_barrier(
        (up_all, projected, along_y(scaled_down))
    )
    projected = along_z(along_y(projected))
    norm = jnp.sum(jnp.square(x.astype(F32)), axis=1, keepdims=True)

    pairs = dot(up_all.reshape(sections * rank, piece), weights, NN)
    layer = lax.broadcasted_iota(jnp.int32, (sections * rank, 1), 0) // rank
    chosen = jnp.where(layer < s, pairs[:, :rank], pairs[:, rank:]).astype(BF16)
    chosen = lax.all_to_all(chosen.reshape(groups, rank, rank), "fsdp", 0, 0, tiled=True)
    block = jnp.sum(chosen.astype(F32), axis=0).astype(BF16)
    table = gather_table(gather_section(block))
    late, _ = lax.optimization_barrier((late, block))
    down_all = along_z(late)

    pick, cross, cross_out = chain_call(width, here, place, projected, norm, table)
    cross = add(cross, swap(cross_out))
    cross, pick = lax.optimization_barrier((cross, pick))
    cross = among_chips(cross)
    half = groups // 2
    part, part_out = pl.pallas_call(
        outer,
        out_shape=(jax.ShapeDtypeStruct((half, 2 * rank, piece), BF16),) * 2,
        in_specs=[smem, vmem, in_hbm, in_hbm],
        out_specs=(vmem,) * 2,
        scratch_shapes=[
            pltpu.VMEM(x.shape, BF16),
            pltpu.VMEM(y.shape, BF16),
            pltpu.SemaphoreType.DMA((2, half)),
        ],
        compiler_params=pltpu.CompilerParams(vmem_limit_bytes=57 * MIB),
        cost_estimate=pl.CostEstimate(
            flops=7 * 10**9, bytes_accessed=9 * MIB, transcendentals=0
        ),
        name="outer",
    )(here, pick, x, y)
    part_got = swap(part_out)
    cross = jnp.sum(cross.astype(F32), axis=0).astype(BF16)
    cross = jnp.broadcast_to(cross[None], (half, 2 * rank, rank))
    part = among_chips(jnp.concatenate([add(part, part_got), cross], axis=2))
    mate = swap(part[:, :, piece:])

    grad_down, grad_gain, grad_up = pl.pallas_call(
        finish,
        out_shape=(
            jax.ShapeDtypeStruct((piece, rank), F32),
            jax.ShapeDtypeStruct((1, piece), F32),
            jax.ShapeDtypeStruct((rank, piece), F32),
        ),
        in_specs=[smem, vmem, vmem, in_hbm, in_hbm, vmem, vmem],
        out_specs=(vmem,) * 3,
        scratch_shapes=[
            pltpu.VMEM(up_all.shape, BF16),
            pltpu.VMEM(down_all.shape, BF16),
            pltpu.SemaphoreType.DMA((2,)),
        ],
        compiler_params=pltpu.CompilerParams(vmem_limit_bytes=57 * MIB),
        name="finish",
    )(here, part, mate, up_all, down_all, down, gain_row[None])
    return (grad_down[None], grad_gain, grad_up[None])


def solution(mesh):
    placed = (
        P(None, "fsdp", None),
        P(None, "fsdp", None),
        P("section", "fsdp", None),
        P("section", "fsdp"),
        P("section", None, "fsdp"),
    )
    return jax.shard_map(
        on_device,
        mesh=mesh,
        in_specs=placed,
        out_specs=(P("section", "fsdp", None), P("section", "fsdp"), P("section", None, "fsdp")),
        check_vma=False,
    )
```

profile of v0, /device:TPU:1, one launch (start us, length us, event | category | flops | bytes accessed | tf_op | source)
XLA Modules:
  0.0 261.5 jit_solution(10261111459054775225)
XLA Ops:
  8.2 2.2 collective-permute-start
  10.4 2.0 collective-permute-done
  15.2 3.2 %collective-permute-start.3 = (bf16[384,256]{1,0:T(8,128)(2,1)S(1)}, bf16[384,256]{1,0:T(8,128)(2,1)S(1)}, u32[]{:S(2)}, u32[]{:S(2)}) collective-permute-start(bf16[384,256]{1,0:T(8,128)(2,1)S(1)} %pad_maximum_fusion.3.rest_0_), channel_id=1, source_target_pairs={{0,8},{1,9},{2,10},{3,11},{4,12},{5,13},{6,14},{7,15},{8,0},{9,1},... | collective-permute-start | bytes 589832 | tf_op jit(solution)/shard_map/ppermute | solution.py:27
  21.0 2.7 %collective-permute-start.8 = (bf16[384,256]{1,0:T(8,128)(2,1)S(1)}, bf16[384,256]{1,0:T(8,128)(2,1)S(1)}, u32[]{:S(2)}, u32[]{:S(2)}) collective-permute-start(bf16[384,256]{1,0:T(8,128)(2,1)S(1)} %pad_maximum_fusion.3.rest_0_), channel_id=1, source_target_pairs={{0,1},{1,0},{2,3},{3,2},{4,5},{5,4},{6,7},{7,6},{8,9},{9,8},{10,11... | collective-permute-start | bytes 589832 | tf_op jit(solution)/shard_map/ppermute | solution.py:27
  25.3 3.1 %collective-permute-done.16 = bf16[384,128]{1,0:T(8,128)(2,1)S(1)} collective-permute-done((bf16[384,128]{1,0:T(8,128)(2,1)S(1)}, bf16[384,128]{1,0:T(8,128)(2,1)S(1)}, u32[]{:S(2)}, u32[]{:S(2)}) %collective-permute-start.16) | collective-permute-done | bytes 98336 | tf_op jit(solution)/shard_map/ppermute | solution.py:27
  29.0 3.9 %collective-permute-start.11 = (bf16[384,256]{1,0:T(8,128)(2,1)S(1)}, bf16[384,256]{1,0:T(8,128)(2,1)S(1)}, u32[]{:S(2)}, u32[]{:S(2)}) collective-permute-start(bf16[384,256]{1,0:T(8,128)(2,1)S(1)} %collective-permute-done.3.rest_3_), channel_id=1, source_target_pairs={{0,1},{1,0},{2,3},{3,2},{4,5},{5,4},{6,7},{7,6},{8,9},{9,8},{10,11... | collective-permute-start | bytes 589832 | tf_op jit(solution)/shard_map/ppermute | solution.py:27
  33.0 2.8 %collective-permute-start.7 = (bf16[384,256]{1,0:T(8,128)(2,1)S(1)}, bf16[384,256]{1,0:T(8,128)(2,1)S(1)}, u32[]{:S(2)}, u32[]{:S(2)}) collective-permute-start(bf16[384,256]{1,0:T(8,128)(2,1)S(1)} %collective-permute-done.6.rest_6_), channel_id=1, source_target_pairs={{0,6},{1,7},{2,0},{3,1},{4,2},{5,3},{6,4},{7,5},{8,14},{9,15},{10,... | collective-permute-start | bytes 589832 | tf_op jit(solution)/shard_map/ppermute | solution.py:27
  36.5 2.5 collective-permute-start.10
  39.1 2.1 collective-permute-start.14
  41.7 11.9 %collective-permute-start.15 = (bf16[384,256]{1,0:T(8,128)(2,1)S(1)}, bf16[384,256]{1,0:T(8,128)(2,1)}, u32[]{:S(2)}, u32[]{:S(2)}) collective-permute-start(bf16[384,256]{1,0:T(8,128)(2,1)S(1)} %collective-permute-done.7.rest_7_), channel_id=1, source_target_pairs={{0,1},{1,0},{2,3},{3,2},{4,5},{5,4},{6,7},{7,6},{8,9},{9,8},{10,11... | collective-permute-start | bytes 589832 | tf_op jit(solution)/shard_map/ppermute | solution.py:27
  55.2 7.8 %project.1 = bf16[256,384]{1,0:T(8,128)(2,1)} custom-call(s32[16]{0:T(128)} %stack.106.place_ref, bf16[256,6144]{1,0:T(8,128)(2,1)} %bitcast.46, bf16[256,6144]{1,0:T(8,128)(2,1)} %bitcast.49, bf16[384,256]{1,0:T(8,128)(2,1)} %copy-done.5, bf16[384,256]{1,0:T(8,128)(2,1)} %copy-done.9, bf16[384,256]{1,0:T(8,128)(2,1)} %copy-done.10, ...), custom_call_target="tpu_custom_call" | custom-call | tf_op jit(solution)/shard_map/project/pallas_call | solution.py:332
  64.1 5.6 %collective-permute-done.17 = bf16[256,384]{1,0:T(8,128)(2,1)S(1)} collective-permute-done((bf16[256,384]{1,0:T(8,128)(2,1)}, bf16[256,384]{1,0:T(8,128)(2,1)S(1)}, u32[]{:S(2)}, u32[]{:S(2)}) %collective-permute-start.17) | collective-permute-done | bytes 196640 | tf_op jit(solution)/shard_map/ppermute | solution.py:27
  72.8 18.3 %all_to_all.20 = bf16[16,128,128]{2,1,0:T(8,128)(2,1)} all-to-all(bf16[16,128,128]{2,1,0:T(8,128)(2,1)S(1)} %bitcast.51), channel_id=1, replica_groups=mesh['section'=16,'fsdp'=16] {'fsdp'}, dimensions={0} | all-to-all | bytes 1048576 | tf_op jit(solution)/shard_map/all_to_all | solution.py:355
  92.3 30.2 %all_to_all.21.rest_0_ = bf16[16,128,128]{2,1,0:T(8,128)(2,1)S(1)} all-to-all(bf16[16,128,128]{2,1,0:T(8,128)(2,1)S(1)} %broadcast_in_dim.33), channel_id=1, replica_groups=mesh['section'=16,'fsdp'=16] {'section'}, dimensions={0} | all-to-all | bytes 1048576 | tf_op jit(solution)/shard_map/all_to_all | solution.py:86
  123.1 2.0 collective-permute-start.19
  126.3 2.5 collective-permute-start.21
  128.8 5.7 %collective-permute-done.18.rest_1_ = bf16[16,128,128]{2,1,0:T(8,128)(2,1)S(1)} collective-permute-done((bf16[16,128,128]{2,1,0:T(8,128)(2,1)S(1)}, bf16[16,128,128]{2,1,0:T(8,128)(2,1)S(1)}, u32[]{:S(2)}, u32[]{:S(2)}) %collective-permute-start.18) | collective-permute-done | bytes 524320 | tf_op jit(solution)/shard_map/ppermute | solution.py:27
  135.4 2.1 collective-permute-start.23
  137.5 4.1 %collective-permute-start.26 = (bf16[16,128,128]{2,1,0:T(8,128)(2,1)S(1)}, bf16[16,128,128]{2,1,0:T(8,128)(2,1)S(1)}, u32[]{:S(2)}, u32[]{:S(2)}) collective-permute-start(bf16[16,128,128]{2,1,0:T(8,128)(2,1)S(1)} %collective-permute-done.20.rest_3_), channel_id=1, source_target_pairs={{0,1},{1,0},{2,3},{3,2},{4,5},{5,4},{6,7},{7,6},{8,9},{9,8},{10,11... | collective-permute-start | bytes 1572872 | tf_op jit(solution)/shard_map/ppermute | solution.py:27
  142.1 2.7 %collective-permute-start.28 = (bf16[16,128,128]{2,1,0:T(8,128)(2,1)S(1)}, bf16[16,128,128]{2,1,0:T(8,128)(2,1)}, u32[]{:S(2)}, u32[]{:S(2)}) collective-permute-start(bf16[16,128,128]{2,1,0:T(8,128)(2,1)S(1)} %collective-permute-done.20.rest_3_), channel_id=1, source_target_pairs={{0,6},{1,7},{2,0},{3,1},{4,2},{5,3},{6,4},{7,5},{8,14},{9,15},{10,... | collective-permute-start | bytes 1572872 | tf_op jit(solution)/shard_map/ppermute | solution.py:27
  147.6 4.9 %collective-permute-start.31 = (bf16[8,128,128]{2,1,0:T(8,128)(2,1)S(1)}, bf16[8,128,128]{2,1,0:T(8,128)(2,1)S(1)}, u32[]{:S(2)}, u32[]{:S(2)}) collective-permute-start(bf16[8,128,128]{2,1,0:T(8,128)(2,1)S(1)} %collective-permute-done.22.rest_4_), channel_id=1, source_target_pairs={{0,1},{1,0},{2,3},{3,2},{4,5},{5,4},{6,7},{7,6},{8,9},{9,8},{10,11... | collective-permute-start | bytes 786440 | tf_op jit(solution)/shard_map/ppermute | solution.py:27
  153.2 4.5 %collective-permute-start.33 = (bf16[16,128,128]{2,1,0:T(8,128)(2,1)}, bf16[16,128,128]{2,1,0:T(8,128)(2,1)}, u32[]{:S(2)}, u32[]{:S(2)}) collective-permute-start(bf16[16,128,128]{2,1,0:T(8,128)(2,1)} %collective-permute-done.27.rest_6_), channel_id=1, source_target_pairs={{0,1},{1,0},{2,3},{3,2},{4,5},{5,4},{6,7},{7,6},{8,9},{9,8},{10,11... | collective-permute-start | bytes 1572872 | tf_op jit(solution)/shard_map/ppermute | solution.py:27
  158.3 2.3 collective-permute-start.35
  163.9 21.6 %chain.1 = (bf16[384,256]{1,0:T(8,128)(2,1)}, bf16[8,256,128]{2,1,0:T(8,128)(2,1)}, bf16[8,256,128]{2,1,0:T(8,128)(2,1)}) custom-call(s32[2]{0:T(128)} %pad_add_fusion.s_ref, s32[16]{0:T(128)} %stack.106.place_ref, bf16[16,256,384]{2,1,0:T(8,128)(2,1)} %all-gather.9.cloned.1.call-done.a_hbm, f32[256,1]{1,0:T(8,128)} %broadcast_in_dim.37.norm_ref, ...), custom_call_target="tpu_custom_call" | custom-call | flops 20000000000 | bytes 12582912 | tf_op jit(solution)/shard_map/chain/pallas_call | solution.py:236
  187.7 2.0 add_convert_fusion.1
  189.7 6.9 %outer.1 = (bf16[8,256,384]{2,1,0:T(8,128)(2,1)}, bf16[8,256,384]{2,1,0:T(8,128)(2,1)}) custom-call(s32[2]{0:T(128)} %pad_add_fusion.s_ref, bf16[384,256]{1,0:T(8,128)(2,1)} %get-tuple-element.36.pick_ref, bf16[256,6144]{1,0:T(8,128)(2,1)} %bitcast.47, bf16[256,6144]{1,0:T(8,128)(2,1)} %bitcast.50), custom_call_target="tpu_custom_call" | custom-call | flops 7000000000 | bytes 9437184 | tf_op jit(solution)/shard_map/outer/pallas_call | solution.py:366
  197.1 3.6 %all-to-all-start.2 = ((bf16[8,256,128]{2,1,0:T(8,128)(2,1)}), bf16[8,256,128]{2,1,0:T(8,128)(2,1)S(1)}, u32[]{:S(2)}, u32[]{:S(2)}) async-start(bf16[8,256,128]{2,1,0:T(8,128)(2,1)} %add_convert_fusion.1), calls=%async_computation.2 | async-start | bytes 1048576 | tf_op jit(solution)/shard_map/all_to_all | solution.py:109
  201.5 11.0 %all-to-all-done.2 = bf16[8,256,128]{2,1,0:T(8,128)(2,1)S(1)} async-done(((bf16[8,256,128]{2,1,0:T(8,128)(2,1)}), bf16[8,256,128]{2,1,0:T(8,128)(2,1)S(1)}, u32[]{:S(2)}, u32[]{:S(2)}) %all-to-all-start.2) | async-done | bytes 524320 | tf_op jit(solution)/shard_map/all_to_all | solution.py:109
  212.6 1.8 add_convert_fusion
  214.7 30.1 %all_to_all.22.part_ref = bf16[8,256,512]{2,1,0:T(8,128)(2,1)S(1)} all-to-all(bf16[8,256,512]{2,1,0:T(8,128)(2,1)S(1)} %pad_maximum_fusion), channel_id=1, replica_groups={{0,2,4,6,8,10,12,14},{1,3,5,7,9,11,13,15},{16,18,20,22,24,26,28,30},{17..., dimensions={0} | all-to-all | bytes 4194304 | tf_op jit(solution)/shard_map/all_to_all | solution.py:109
  244.9 1.8 collective-permute-start.39
  249.1 5.7 %finish.1 = (f32[384,128]{1,0:T(8,128)}, f32[1,384]{1,0:T(1,128)}, f32[128,384]{1,0:T(8,128)}) custom-call(s32[2]{0:T(128)} %pad_add_fusion.s_ref, bf16[8,256,512]{2,1,0:T(8,128)(2,1)} %copy-done.1, bf16[8,256,128]{2,1,0:T(8,128)(2,1)} %copy-done.7, bf16[16,128,384]{2,1,0:T(8,128)(2,1)} %all-gather.7.cloned.1.call-done.up_hbm, ...), custom_call_target="tpu_custom_call" | custom-call | tf_op jit(solution)/shard_map/finish/pallas_call | solution.py:388
  (159 shorter events, 33.3 us)
Async XLA Ops:
  7.2 55.9 %all-gather.7.cloned.1.call-start = ((), (), s32[]{:S(2)}) async-start(), calls=%async_computation.4 | async-start | bytes 1769472 | tf_op jit(solution)/shard_map/all_gather | solution.py:99
  13.4 150.5 %all-gather.9.cloned.1.call-start = ((), (), s32[]{:S(2)}) async-start(), calls=%async_computation.5 | async-start | bytes 3538944 | tf_op jit(solution)/shard_map/all_gather | solution.py:99
  15.2 8.5 %collective-permute-start.3 = (bf16[384,256]{1,0:T(8,128)(2,1)S(1)}, bf16[384,256]{1,0:T(8,128)(2,1)S(1)}, u32[]{:S(2)}, u32[]{:S(2)}) collective-permute-start(bf16[384,256]{1,0:T(8,128)(2,1)S(1)} %pad_maximum_fusion.3.rest_0_), channel_id=1, source_target_pairs={{0,8},{1,9},{2,10},{3,11},{4,12},{5,13},{6,14},{7,15},{8,0},{9,1},... | collective-permute-start | bytes 589832 | tf_op jit(solution)/shard_map/ppermute | solution.py:27
  18.3 10.6 %collective-permute-start.1 = (bf16[384,256]{1,0:T(8,128)(2,1)S(1)}, bf16[384,256]{1,0:T(8,128)(2,1)S(1)}, u32[]{:S(2)}, u32[]{:S(2)}) collective-permute-start(bf16[384,256]{1,0:T(8,128)(2,1)S(1)} %pad_maximum_fusion.3.rest_0_), channel_id=1, source_target_pairs={{0,2},{1,3},{2,4},{3,5},{4,6},{5,7},{6,0},{7,1},{8,10},{9,11},{10,... | collective-permute-start | bytes 589832 | tf_op jit(solution)/shard_map/ppermute | solution.py:27
  19.5 9.5 %collective-permute-start.2 = (bf16[384,256]{1,0:T(8,128)(2,1)S(1)}, bf16[384,256]{1,0:T(8,128)(2,1)S(1)}, u32[]{:S(2)}, u32[]{:S(2)}) collective-permute-start(bf16[384,256]{1,0:T(8,128)(2,1)S(1)} %pad_maximum_fusion.3.rest_0_), channel_id=1, source_target_pairs={{0,6},{1,7},{2,0},{3,1},{4,2},{5,3},{6,4},{7,5},{8,14},{9,15},{10,... | collective-permute-start | bytes 589832 | tf_op jit(solution)/shard_map/ppermute | solution.py:27
  21.0 11.9 %collective-permute-start.8 = (bf16[384,256]{1,0:T(8,128)(2,1)S(1)}, bf16[384,256]{1,0:T(8,128)(2,1)S(1)}, u32[]{:S(2)}, u32[]{:S(2)}) collective-permute-start(bf16[384,256]{1,0:T(8,128)(2,1)S(1)} %pad_maximum_fusion.3.rest_0_), channel_id=1, source_target_pairs={{0,1},{1,0},{2,3},{3,2},{4,5},{5,4},{6,7},{7,6},{8,9},{9,8},{10,11... | collective-permute-start | bytes 589832 | tf_op jit(solution)/shard_map/ppermute | solution.py:27
  23.7 9.4 %collective-permute-start.6 = (bf16[384,256]{1,0:T(8,128)(2,1)S(1)}, bf16[384,256]{1,0:T(8,128)(2,1)S(1)}, u32[]{:S(2)}, u32[]{:S(2)}) collective-permute-start(bf16[384,256]{1,0:T(8,128)(2,1)S(1)} %collective-permute-done.3.rest_3_), channel_id=1, source_target_pairs={{0,6},{1,7},{2,0},{3,1},{4,2},{5,3},{6,4},{7,5},{8,14},{9,15},{10,... | collective-permute-start | bytes 589832 | tf_op jit(solution)/shard_map/ppermute | solution.py:27
  28.4 8.1 %collective-permute-start.5 = (bf16[384,256]{1,0:T(8,128)(2,1)S(1)}, bf16[384,256]{1,0:T(8,128)(2,1)S(1)}, u32[]{:S(2)}, u32[]{:S(2)}) collective-permute-start(bf16[384,256]{1,0:T(8,128)(2,1)S(1)} %collective-permute-done.3.rest_3_), channel_id=1, source_target_pairs={{0,2},{1,3},{2,4},{3,5},{4,6},{5,7},{6,0},{7,1},{8,10},{9,11},{10,... | collective-permute-start | bytes 589832 | tf_op jit(solution)/shard_map/ppermute | solution.py:27
  28.9 10.1 %collective-permute-start.4 = (bf16[384,256]{1,0:T(8,128)(2,1)S(1)}, bf16[384,256]{1,0:T(8,128)(2,1)S(1)}, u32[]{:S(2)}, u32[]{:S(2)}) collective-permute-start(bf16[384,256]{1,0:T(8,128)(2,1)S(1)} %collective-permute-done.1.rest_1_), channel_id=1, source_target_pairs={{0,2},{1,3},{2,4},{3,5},{4,6},{5,7},{6,0},{7,1},{8,10},{9,11},{10,... | collective-permute-start | bytes 589832 | tf_op jit(solution)/shard_map/ppermute | solution.py:27
  29.0 12.2 %collective-permute-start.11 = (bf16[384,256]{1,0:T(8,128)(2,1)S(1)}, bf16[384,256]{1,0:T(8,128)(2,1)S(1)}, u32[]{:S(2)}, u32[]{:S(2)}) collective-permute-start(bf16[384,256]{1,0:T(8,128)(2,1)S(1)} %collective-permute-done.3.rest_3_), channel_id=1, source_target_pairs={{0,1},{1,0},{2,3},{3,2},{4,5},{5,4},{6,7},{7,6},{8,9},{9,8},{10,11... | collective-permute-start | bytes 589832 | tf_op jit(solution)/shard_map/ppermute | solution.py:27
  32.9 8.3 %collective-permute-start.9 = (bf16[384,256]{1,0:T(8,128)(2,1)S(1)}, bf16[384,256]{1,0:T(8,128)(2,1)S(1)}, u32[]{:S(2)}, u32[]{:S(2)}) collective-permute-start(bf16[384,256]{1,0:T(8,128)(2,1)S(1)} %collective-permute-done.1.rest_1_), channel_id=1, source_target_pairs={{0,1},{1,0},{2,3},{3,2},{4,5},{5,4},{6,7},{7,6},{8,9},{9,8},{10,11... | collective-permute-start | bytes 589832 | tf_op jit(solution)/shard_map/ppermute | solution.py:27
  33.0 8.6 %collective-permute-start.7 = (bf16[384,256]{1,0:T(8,128)(2,1)S(1)}, bf16[384,256]{1,0:T(8,128)(2,1)S(1)}, u32[]{:S(2)}, u32[]{:S(2)}) collective-permute-start(bf16[384,256]{1,0:T(8,128)(2,1)S(1)} %collective-permute-done.6.rest_6_), channel_id=1, source_target_pairs={{0,6},{1,7},{2,0},{3,1},{4,2},{5,3},{6,4},{7,5},{8,14},{9,15},{10,... | collective-permute-start | bytes 589832 | tf_op jit(solution)/shard_map/ppermute | solution.py:27
  36.5 17.9 %collective-permute-start.10 = (bf16[384,256]{1,0:T(8,128)(2,1)S(1)}, bf16[384,256]{1,0:T(8,128)(2,1)S(1)}, u32[]{:S(2)}, u32[]{:S(2)}) collective-permute-start(bf16[384,256]{1,0:T(8,128)(2,1)S(1)} %collective-permute-done.2.rest_2_), channel_id=1, source_target_pairs={{0,1},{1,0},{2,3},{3,2},{4,5},{5,4},{6,7},{7,6},{8,9},{9,8},{10,11... | collective-permute-start | bytes 589832 | tf_op jit(solution)/shard_map/ppermute | solution.py:27
  39.1 15.3 %collective-permute-start.14 = (bf16[384,256]{1,0:T(8,128)(2,1)S(1)}, bf16[384,256]{1,0:T(8,128)(2,1)S(1)}, u32[]{:S(2)}, u32[]{:S(2)}) collective-permute-start(bf16[384,256]{1,0:T(8,128)(2,1)S(1)} %collective-permute-done.6.rest_6_), channel_id=1, source_target_pairs={{0,1},{1,0},{2,3},{3,2},{4,5},{5,4},{6,7},{7,6},{8,9},{9,8},{10,11... | collective-permute-start | bytes 589832 | tf_op jit(solution)/shard_map/ppermute | solution.py:27
  41.2 13.2 %collective-permute-start.13 = (bf16[384,256]{1,0:T(8,128)(2,1)S(1)}, bf16[384,256]{1,0:T(8,128)(2,1)S(1)}, u32[]{:S(2)}, u32[]{:S(2)}) collective-permute-start(bf16[384,256]{1,0:T(8,128)(2,1)S(1)} %collective-permute-done.5.rest_5_), channel_id=1, source_target_pairs={{0,1},{1,0},{2,3},{3,2},{4,5},{5,4},{6,7},{7,6},{8,9},{9,8},{10,11... | collective-permute-start | bytes 589832 | tf_op jit(solution)/shard_map/ppermute | solution.py:27
  41.3 13.1 %collective-permute-start.12 = (bf16[384,256]{1,0:T(8,128)(2,1)S(1)}, bf16[384,256]{1,0:T(8,128)(2,1)S(1)}, u32[]{:S(2)}, u32[]{:S(2)}) collective-permute-start(bf16[384,256]{1,0:T(8,128)(2,1)S(1)} %collective-permute-done.4.rest_4_), channel_id=1, source_target_pairs={{0,1},{1,0},{2,3},{3,2},{4,5},{5,4},{6,7},{7,6},{8,9},{9,8},{10,11... | collective-permute-start | bytes 589832 | tf_op jit(solution)/shard_map/ppermute | solution.py:27
  41.7 13.1 %collective-permute-start.15 = (bf16[384,256]{1,0:T(8,128)(2,1)S(1)}, bf16[384,256]{1,0:T(8,128)(2,1)}, u32[]{:S(2)}, u32[]{:S(2)}) collective-permute-start(bf16[384,256]{1,0:T(8,128)(2,1)S(1)} %collective-permute-done.7.rest_7_), channel_id=1, source_target_pairs={{0,1},{1,0},{2,3},{3,2},{4,5},{5,4},{6,7},{7,6},{8,9},{9,8},{10,11... | collective-permute-start | bytes 589832 | tf_op jit(solution)/shard_map/ppermute | solution.py:27
  122.5 12.1 %collective-permute-start.18 = (bf16[16,128,128]{2,1,0:T(8,128)(2,1)S(1)}, bf16[16,128,128]{2,1,0:T(8,128)(2,1)S(1)}, u32[]{:S(2)}, u32[]{:S(2)}) collective-permute-start(bf16[16,128,128]{2,1,0:T(8,128)(2,1)S(1)} %all_to_all.21.rest_0_), channel_id=1, source_target_pairs={{0,2},{1,3},{2,4},{3,5},{4,6},{5,7},{6,0},{7,1},{8,10},{9,11},{10,... | collective-permute-start | bytes 1572872 | tf_op jit(solution)/shard_map/ppermute | solution.py:27
  123.1 12.2 %collective-permute-start.19 = (bf16[16,128,128]{2,1,0:T(8,128)(2,1)S(1)}, bf16[16,128,128]{2,1,0:T(8,128)(2,1)S(1)}, u32[]{:S(2)}, u32[]{:S(2)}) collective-permute-start(bf16[16,128,128]{2,1,0:T(8,128)(2,1)S(1)} %all_to_all.21.rest_0_), channel_id=1, source_target_pairs={{0,6},{1,7},{2,0},{3,1},{4,2},{5,3},{6,4},{7,5},{8,14},{9,15},{10,... | collective-permute-start | bytes 1572872 | tf_op jit(solution)/shard_map/ppermute | solution.py:27
  125.2 12.3 %collective-permute-start.20 = (bf16[16,128,128]{2,1,0:T(8,128)(2,1)S(1)}, bf16[16,128,128]{2,1,0:T(8,128)(2,1)S(1)}, u32[]{:S(2)}, u32[]{:S(2)}) collective-permute-start(bf16[16,128,128]{2,1,0:T(8,128)(2,1)S(1)} %all_to_all.21.rest_0_), channel_id=1, source_target_pairs={{0,24},{1,25},{2,26},{3,27},{4,28},{5,29},{6,30},{7,31},{8,16},{9,... | collective-permute-start | bytes 1572872 | tf_op jit(solution)/shard_map/ppermute | solution.py:40
  126.3 11.2 %collective-permute-start.21 = (bf16[16,128,128]{2,1,0:T(8,128)(2,1)S(1)}, bf16[16,128,128]{2,1,0:T(8,128)(2,1)S(1)}, u32[]{:S(2)}, u32[]{:S(2)}) collective-permute-start(bf16[16,128,128]{2,1,0:T(8,128)(2,1)S(1)} %all_to_all.21.rest_0_), channel_id=1, source_target_pairs={{0,1},{1,0},{2,3},{3,2},{4,5},{5,4},{6,7},{7,6},{8,9},{9,8},{10,11... | collective-permute-start | bytes 1572872 | tf_op jit(solution)/shard_map/ppermute | solution.py:27
  134.6 7.5 %collective-permute-start.22 = (bf16[8,128,128]{2,1,0:T(8,128)(2,1)S(1)}, bf16[8,128,128]{2,1,0:T(8,128)(2,1)S(1)}, u32[]{:S(2)}, u32[]{:S(2)}) collective-permute-start(bf16[8,128,128]{2,1,0:T(8,128)(2,1)S(1)} %slice.22), channel_id=1, source_target_pairs={{0,2},{1,3},{2,4},{3,5},{4,6},{5,7},{6,0},{7,1},{8,10},{9,11},{10,... | collective-permute-start | bytes 786440 | tf_op jit(solution)/shard_map/ppermute | solution.py:27
  137.5 7.3 %collective-permute-start.26 = (bf16[16,128,128]{2,1,0:T(8,128)(2,1)S(1)}, bf16[16,128,128]{2,1,0:T(8,128)(2,1)S(1)}, u32[]{:S(2)}, u32[]{:S(2)}) collective-permute-start(bf16[16,128,128]{2,1,0:T(8,128)(2,1)S(1)} %collective-permute-done.20.rest_3_), channel_id=1, source_target_pairs={{0,1},{1,0},{2,3},{3,2},{4,5},{5,4},{6,7},{7,6},{8,9},{9,8},{10,11... | collective-permute-start | bytes 1572872 | tf_op jit(solution)/shard_map/ppermute | solution.py:27
  142.1 11.1 %collective-permute-start.27 = (bf16[16,128,128]{2,1,0:T(8,128)(2,1)S(1)}, bf16[16,128,128]{2,1,0:T(8,128)(2,1)}, u32[]{:S(2)}, u32[]{:S(2)}) collective-permute-start(bf16[16,128,128]{2,1,0:T(8,128)(2,1)S(1)} %collective-permute-done.20.rest_3_), channel_id=1, source_target_pairs={{0,2},{1,3},{2,4},{3,5},{4,6},{5,7},{6,0},{7,1},{8,10},{9,11},{10,... | collective-permute-start | bytes 1572872 | tf_op jit(solution)/shard_map/ppermute | solution.py:27
  142.1 15.6 %collective-permute-start.28 = (bf16[16,128,128]{2,1,0:T(8,128)(2,1)S(1)}, bf16[16,128,128]{2,1,0:T(8,128)(2,1)}, u32[]{:S(2)}, u32[]{:S(2)}) collective-permute-start(bf16[16,128,128]{2,1,0:T(8,128)(2,1)S(1)} %collective-permute-done.20.rest_3_), channel_id=1, source_target_pairs={{0,6},{1,7},{2,0},{3,1},{4,2},{5,3},{6,4},{7,5},{8,14},{9,15},{10,... | collective-permute-start | bytes 1572872 | tf_op jit(solution)/shard_map/ppermute | solution.py:27
  144.8 12.9 %collective-permute-start.29 = (bf16[8,128,128]{2,1,0:T(8,128)(2,1)S(1)}, bf16[8,128,128]{2,1,0:T(8,128)(2,1)}, u32[]{:S(2)}, u32[]{:S(2)}) collective-permute-start(bf16[8,128,128]{2,1,0:T(8,128)(2,1)S(1)} %collective-permute-done.22.rest_4_), channel_id=1, source_target_pairs={{0,24},{1,25},{2,26},{3,27},{4,28},{5,29},{6,30},{7,31},{8,16},{9,... | collective-permute-start | bytes 786440 | tf_op jit(solution)/shard_map/ppermute | solution.py:40
  146.1 12.2 %collective-permute-start.30 = (bf16[8,128,128]{2,1,0:T(8,128)(2,1)}, bf16[8,128,128]{2,1,0:T(8,128)(2,1)}, u32[]{:S(2)}, u32[]{:S(2)}) collective-permute-start(bf16[8,128,128]{2,1,0:T(8,128)(2,1)} %collective-permute-done.23.rest_5_), channel_id=1, source_target_pairs={{0,24},{1,25},{2,26},{3,27},{4,28},{5,29},{6,30},{7,31},{8,16},{9,... | collective-permute-start | bytes 786440 | tf_op jit(solution)/shard_map/ppermute | solution.py:40
  147.6 13.0 %collective-permute-start.31 = (bf16[8,128,128]{2,1,0:T(8,128)(2,1)S(1)}, bf16[8,128,128]{2,1,0:T(8,128)(2,1)S(1)}, u32[]{:S(2)}, u32[]{:S(2)}) collective-permute-start(bf16[8,128,128]{2,1,0:T(8,128)(2,1)S(1)} %collective-permute-done.22.rest_4_), channel_id=1, source_target_pairs={{0,1},{1,0},{2,3},{3,2},{4,5},{5,4},{6,7},{7,6},{8,9},{9,8},{10,11... | collective-permute-start | bytes 786440 | tf_op jit(solution)/shard_map/ppermute | solution.py:27
  153.2 10.6 %collective-permute-start.33 = (bf16[16,128,128]{2,1,0:T(8,128)(2,1)}, bf16[16,128,128]{2,1,0:T(8,128)(2,1)}, u32[]{:S(2)}, u32[]{:S(2)}) collective-permute-start(bf16[16,128,128]{2,1,0:T(8,128)(2,1)} %collective-permute-done.27.rest_6_), channel_id=1, source_target_pairs={{0,1},{1,0},{2,3},{3,2},{4,5},{5,4},{6,7},{7,6},{8,9},{9,8},{10,11... | collective-permute-start | bytes 1572872 | tf_op jit(solution)/shard_map/ppermute | solution.py:27
  196.6 15.9 %collective-permute-start.38 = (bf16[8,256,384]{2,1,0:T(8,128)(2,1)}, bf16[8,256,384]{2,1,0:T(8,128)(2,1)}, u32[]{:S(2)}, u32[]{:S(2)}) collective-permute-start(bf16[8,256,384]{2,1,0:T(8,128)(2,1)} %get-tuple-element.38), channel_id=1, source_target_pairs={{0,1},{1,0},{2,3},{3,2},{4,5},{5,4},{6,7},{7,6},{8,9},{9,8},{10,11... | collective-permute-start | bytes 4718600 | tf_op jit(solution)/shard_map/ppermute | solution.py:27
  197.1 15.4 %all-to-all-start.2 = ((bf16[8,256,128]{2,1,0:T(8,128)(2,1)}), bf16[8,256,128]{2,1,0:T(8,128)(2,1)S(1)}, u32[]{:S(2)}, u32[]{:S(2)}) async-start(bf16[8,256,128]{2,1,0:T(8,128)(2,1)} %add_convert_fusion.1), calls=%async_computation.2 | async-start | bytes 1048576 | tf_op jit(solution)/shard_map/all_to_all | solution.py:109
  200.7 46.6 %all-gather.11.cloned.1.call-start = ((), (), s32[]{:S(2)}) async-start(), calls=%async_computation.6 | async-start | bytes 1769472 | tf_op jit(solution)/shard_map/all_gather | solution.py:99
  (44 other events, 629.4 us)
Sparse Core Ops, SparseCore 0:
  13.5 40.6 all-gather.6
  71.7 58.0 all-gather.8
  203.3 34.6 all-gather.10
where the time goes:
time: 265 us; the launch traced here: 261 us
  blocking collectives  78.6 us (30%)
  starting transfers between devices  76.4 us (29%)
  Pallas kernels  41.9 us (16%)
  waiting for transfers between devices  32 us (12%)
  between operations  14.5 us (5%)
  other arithmetic  11.9 us (4%)
  local copies, waits for them, and re-layouts  5.59 us (2%)
    ppermute x37, starting transfers between devices, hop(): return lax.ppermute(block, axis, route)  68.7 us
    all_to_all x1, blocking collectives, gather_section(): lax.all_to_all(jnp.broadcast_to(block[None], (16,) + block.shape), 'secti...  30.2 us
    all_to_all x1, blocking collectives, among_chips(): lax.all_to_all(chunks, 'fsdp', 0, 0, tiled=True, axis_index_groups=chips)  30.1 us
    pallas_call x1, Pallas kernels, chain_call(): pl.pallas_call(functools.partial(chain, width), out_shape=(jax.ShapeDtype...  21.6 us
    ppermute x37, waiting for transfers between devices, hop(): return lax.ppermute(block, axis, route)  20.2 us
    all_to_all x1, blocking collectives, on_device(): lax.all_to_all(chosen.reshape(groups, rank, rank), 'fsdp', 0, 0, tiled=True)  18.3 us
    all_to_all x1, waiting for transfers between devices, among_chips(): lax.all_to_all(chunks, 'fsdp', 0, 0, tiled=True, axis_index_groups=chips)  11 us
    pallas_call x1, Pallas kernels, on_device(): pl.pallas_call(project, out_shape=jax.ShapeDtypeStruct((tokens, 3 * rank)...  7.79 us
  transfers between devices with their start and end apart: 44, of which 9 were waited for; matrix products, arithmetic and copies ran while one was open for 4% of the time, Pallas kernels for 3%

commit v1 on v0

--- a/solution.py
+++ b/solution.py
@@ -127,11 +127,11 @@
     out_ref[:, 2 * rank :] = dot(yv_ref[...], w_ref[:, rank:], NN).astype(BF16)
 
 
-def chain(width, s_ref, place_ref, a_hbm, norm_ref, *rest):
+def chain(width, s_ref, place_ref, a_hbm, norm_ref, x_hbm, y_hbm, *rest):
     pieces = rest[:20]
-    pick_ref, keep_ref, send_ref = rest[20:23]
-    z_ref, a_ref, w_ref, lift_ref, act_ref, slope_ref, inv_ref = rest[23:30]
-    q_ref, p_ref, sq_ref, sums_ref, sem = rest[30:]
+    keep_ref, send_ref, keep_part, send_part = rest[20:24]
+    z_ref, a_ref, w_ref, lift_ref, act_ref, slope_ref, inv_ref = rest[24:31]
+    q_ref, p_ref, sq_ref, sums_ref, x_ref, y_ref, sem = rest[31:]
     layers = a_ref.shape[0]
     rank = z_ref.shape[2]
     cut = [slice(rank * i, rank * (i + 1)) for i in range(layers)]
@@ -152,6 +152,12 @@
             copy = pltpu.make_async_copy(piece, z_ref.at[some, span, :], sem.at[part, at])
             copy.start()
             copies.append(copy)
+    whole = [
+        pltpu.make_async_copy(x_hbm, x_ref, sem.at[parts, 1]),
+        pltpu.make_async_copy(y_hbm, y_ref, sem.at[parts, 2]),
+    ]
+    for copy in whole:
+        copy.start()
     first.wait()
     for s in range(layers):
         w_ref[s] = a_ref[s, :, cut[1]].astype(F32)
@@ -201,8 +207,6 @@
     here = pl.ds(pl.multiple_of(s_ref[0] * rank, rank), rank)
     p_t, q_t, sq_t = p_ref[:, here].T, q_ref[:, here].T, sq_ref[:, here].T
     both = jnp.concatenate([p_t, -sq_t], axis=0)
-    pick_ref[: 2 * rank] = both
-    pick_ref[2 * rank :] = q_t
     for j in range(layers):
 
         @pl.when(j < s_ref[0])
@@ -224,10 +228,23 @@
         def _():
             send_ref[j // 2] = sums_ref[...]
 
-
-def chain_call(width, here, place, projected, norm, table):
+    for copy in whole:
+        copy.wait()
+    half, _, piece = keep_part.shape
+    even_core = s_ref[1] == 0
+    for i in range(half):
+        span = slice(2 * piece * i, 2 * piece * (i + 1))
+        from_x = dot(both, x_ref[:, span], NN)
+        from_y = dot(q_t, y_ref[:, span], NN)
+        sums = jnp.concatenate([from_x[:rank], from_x[rank:] + from_y], axis=0).astype(BF16)
+        even, odd = sums[:, :piece], sums[:, piece:]
+        keep_part[i] = jnp.where(even_core, even, odd)
+        send_part[i] = jnp.where(even_core, odd, even)
+
+
+def chain_call(here, place, projected, norm, x, y, table):
     sections, tokens, wide = projected.shape
-    rank = wide // 3
+    rank, width, piece = wide // 3, x.shape[1], x.shape[1] // 16
     smem = pl.BlockSpec(memory_space=pltpu.SMEM)
     vmem = pl.BlockSpec(memory_space=pltpu.VMEM)
     in_hbm = pl.BlockSpec(memory_space=pltpu.HBM)
@@ -236,45 +253,26 @@
     return pl.pallas_call(
         functools.partial(chain, width),
         out_shape=(
-            jax.ShapeDtypeStruct((3 * rank, tokens), BF16),
             jax.ShapeDtypeStruct((8, 2 * rank, rank), BF16),
             jax.ShapeDtypeStruct((8, 2 * rank, rank), BF16),
+            jax.ShapeDtypeStruct((8, 2 * rank, piece), BF16),
+            jax.ShapeDtypeStruct((8, 2 * rank, piece), BF16),
         ),
-        in_specs=[smem, smem, in_hbm, vmem] + [in_hbm] * 20,
-        out_specs=(vmem,) * 3,
+        in_specs=[smem, smem, in_hbm, vmem] + [in_hbm] * 22,
+        out_specs=(vmem,) * 4,
         scratch_shapes=[pltpu.VMEM((sections, sections * rank, rank), BF16)]
         + [pltpu.VMEM((sections, tokens, wide), BF16)]
         + [big] * 5
         + [flat] * 3
-        + [pltpu.VMEM((2 * rank, rank), BF16), pltpu.SemaphoreType.DMA((5, 16))],
+        + [pltpu.VMEM((2 * rank, rank), BF16)]
+        + [pltpu.VMEM(x.shape, BF16)] * 2
+        + [pltpu.SemaphoreType.DMA((5, 16))],
         compiler_params=pltpu.CompilerParams(vmem_limit_bytes=57 * MIB),
         cost_estimate=pl.CostEstimate(
             flops=2 * 10**10, bytes_accessed=12 * MIB, transcendentals=10**6
         ),
         name="chain",
-    )(here, place, projected, norm, *table)
-
-
-def outer(s_ref, pick_ref, x_hbm, y_hbm, keep_ref, send_ref, x_ref, y_ref, sem):
-    rank = pick_ref.shape[0] // 3
-    half, _, piece = keep_ref.shape
-    first = s_ref[1] == 0
-    copies = []
-    for i in range(half):
-        span = pl.ds(2 * piece * i, 2 * piece)
-        for k, (far, near) in enumerate(((x_hbm, x_ref), (y_hbm, y_ref))):
-            copies.append(pltpu.make_async_copy(far.at[:, span], near.at[:, span], sem.at[k, i]))
-            copies[-1].start()
-    for i in range(half):
-        span = slice(2 * piece * i, 2 * piece * (i + 1))
-        copies[2 * i].wait()
-        copies[2 * i + 1].wait()
-        from_x = dot(pick_ref[: 2 * rank], x_ref[:, span], NN)
-        from_y = dot(pick_ref[2 * rank :], y_ref[:, span], NN)
-        both = jnp.concatenate([from_x[:rank], from_x[rank:] + from_y], axis=0).astype(BF16)
-        even, odd = both[:, :piece], both[:, piece:]
-        keep_ref[i] = jnp.where(first, even, odd)
-        send_ref[i] = jnp.where(first, odd, even)
+    )(here, place, projected, norm, x, y, *table)
 
 
 def finish(s_ref, part_ref, mate_ref, up_hbm, down_hbm, own_ref, gain_ref, *rest):
@@ -327,6 +325,7 @@
 
     scaled_down = (down.astype(F32) * gain_row[:, None]).astype(BF16)
     weights = jnp.concatenate([scaled_down, up.T], axis=1)
+
     up_all = along_z(along_y(up))
 
     projected = pl.pallas_call(
@@ -341,46 +340,33 @@
             pltpu.SemaphoreType.DMA((18,)),
         ],
         compiler_params=pltpu.CompilerParams(vmem_limit_bytes=57 * MIB),
+        cost_estimate=pl.CostEstimate(
+            flops=8 * 10**9, bytes_accessed=9 * MIB, transcendentals=0
+        ),
         name="project",
     )(place, x, y, *gather_pieces(weights))
-    up_all, projected, late = lax.optimization_barrier(
-        (up_all, projected, along_y(scaled_down))
+    up_all, pair, late = lax.optimization_barrier(
+        (up_all, along_y(projected), along_y(scaled_down))
     )
-    projected = along_z(along_y(projected))
+    projected = along_z(pair)
     norm = jnp.sum(jnp.square(x.astype(F32)), axis=1, keepdims=True)
 
     pairs = dot(up_all.reshape(sections * rank, piece), weights, NN)
     layer = lax.broadcasted_iota(jnp.int32, (sections * rank, 1), 0) // rank
     chosen = jnp.where(layer < s, pairs[:, :rank], pairs[:, rank:]).astype(BF16)
-    chosen = lax.all_to_all(chosen.reshape(groups, rank, rank), "fsdp", 0, 0, tiled=True)
+    chosen = chosen.reshape(groups, rank, rank)
+    chosen = lax.all_to_all(chosen, "fsdp", 0, 0, tiled=True)
     block = jnp.sum(chosen.astype(F32), axis=0).astype(BF16)
+    block, late = lax.optimization_barrier((block, late))
     table = gather_table(gather_section(block))
-    late, _ = lax.optimization_barrier((late, block))
     down_all = along_z(late)
 
-    pick, cross, cross_out = chain_call(width, here, place, projected, norm, table)
-    cross = add(cross, swap(cross_out))
-    cross, pick = lax.optimization_barrier((cross, pick))
-    cross = among_chips(cross)
-    half = groups // 2
-    part, part_out = pl.pallas_call(
-        outer,
-        out_shape=(jax.ShapeDtypeStruct((half, 2 * rank, piece), BF16),) * 2,
-        in_specs=[smem, vmem, in_hbm, in_hbm],
-        out_specs=(vmem,) * 2,
-        scratch_shapes=[
-            pltpu.VMEM(x.shape, BF16),
-            pltpu.VMEM(y.shape, BF16),
-            pltpu.SemaphoreType.DMA((2, half)),
-        ],
-        compiler_params=pltpu.CompilerParams(vmem_limit_bytes=57 * MIB),
-        cost_estimate=pl.CostEstimate(
-            flops=7 * 10**9, bytes_accessed=9 * MIB, transcendentals=0
-        ),
-        name="outer",
-    )(here, pick, x, y)
+    cross, cross_out, part, part_out = chain_call(here, place, projected, norm, x, y, table)
+    cross_got, part_out = lax.optimization_barrier((swap(cross_out), part_out))
+    cross = among_chips(add(cross, cross_got))
     part_got = swap(part_out)
     cross = jnp.sum(cross.astype(F32), axis=0).astype(BF16)
+    half = groups // 2
     cross = jnp.broadcast_to(cross[None], (half, 2 * rank, rank))
     part = among_chips(jnp.concatenate([add(part, part_got), cross], axis=2))
     mate = swap(part[:, :, piece:])

time: 265 us -> 259 us (0.977)
  Pallas kernels: 41.9 us -> 37.2 us
  waiting for transfers between devices: 32 us -> 28 us
    pallas_call x1 -> x0, Pallas kernels: 6.86 us -> none  [on_device(): pl.pallas_call(outer, out_shape=(jax.ShapeDtypeStruct((half, 2 * rank, pi...]
    ppermute x37, waiting for transfers between devices: 20.2 us -> 16.2 us  [hop(): return lax.ppermute(block, axis, route)]
  transfers between devices with their start and end apart: 44 -> 44, of which waited for: 9 -> 8; matrix products, arithmetic and copies ran while one was open for 4% -> 6% of each run, Pallas kernels for 3% -> 3%
where the time goes in v1:
time: 259 us; the launch traced here: 256 us
  blocking collectives  80.4 us (31%)
  starting transfers between devices  75.6 us (29%)
  Pallas kernels  37.2 us (14%)
  waiting for transfers between devices  28 us (11%)
  between operations  14.5 us (6%)
  other arithmetic  12 us (5%)
  local copies, waits for them, and re-layouts  5.86 us (2%)
    ppermute x37, starting transfers between devices, hop(): return lax.ppermute(block, axis, route)  68.6 us
    all_to_all x1, blocking collectives, gather_section(): lax.all_to_all(jnp.broadcast_to(block[None], (16,) + block.shape), 'secti...  30.1 us
    all_to_all x1, blocking collectives, among_chips(): lax.all_to_all(chunks, 'fsdp', 0, 0, tiled=True, axis_index_groups=chips)  30.1 us
    pallas_call x1, Pallas kernels, chain_call(): pl.pallas_call(functools.partial(chain, width), out_shape=(jax.ShapeDtype...  23.6 us
    all_to_all x1, blocking collectives, on_device(): chosen = lax.all_to_all(chosen, 'fsdp', 0, 0, tiled=True)  20.3 us
    ppermute x37, waiting for transfers between devices, hop(): return lax.ppermute(block, axis, route)  16.2 us
    all_to_all x1, waiting for transfers between devices, among_chips(): lax.all_to_all(chunks, 'fsdp', 0, 0, tiled=True, axis_index_groups=chips)  11 us
    pallas_call x1, Pallas kernels, on_device(): pl.pallas_call(project, out_shape=jax.ShapeDtypeStruct((tokens, 3 * rank)...  7.92 us
  transfers between devices with their start and end apart: 44, of which 8 were waited for; matrix products, arithmetic and copies ran while one was open for 6% of the time, Pallas kernels for 3%

profile of v1, /device:TPU:1, one launch (start us, length us, event | category | flops | bytes accessed | tf_op | source)
XLA Modules:
  0.0 255.8 jit_solution(11113628928789135829)
XLA Ops:
  8.2 2.2 collective-permute-start
  10.4 2.0 collective-permute-done
  15.2 3.2 %collective-permute-start.3 = (bf16[384,256]{1,0:T(8,128)(2,1)S(1)}, bf16[384,256]{1,0:T(8,128)(2,1)S(1)}, u32[]{:S(2)}, u32[]{:S(2)}) collective-permute-start(bf16[384,256]{1,0:T(8,128)(2,1)S(1)} %pad_maximum_fusion.3.rest_0_), channel_id=1, source_target_pairs={{0,8},{1,9},{2,10},{3,11},{4,12},{5,13},{6,14},{7,15},{8,0},{9,1},... | collective-permute-start | bytes 589832 | tf_op jit(solution)/shard_map/ppermute | solution.py:27
  21.0 2.7 %collective-permute-start.8 = (bf16[384,256]{1,0:T(8,128)(2,1)S(1)}, bf16[384,256]{1,0:T(8,128)(2,1)S(1)}, u32[]{:S(2)}, u32[]{:S(2)}) collective-permute-start(bf16[384,256]{1,0:T(8,128)(2,1)S(1)} %pad_maximum_fusion.3.rest_0_), channel_id=1, source_target_pairs={{0,1},{1,0},{2,3},{3,2},{4,5},{5,4},{6,7},{7,6},{8,9},{9,8},{10,11... | collective-permute-start | bytes 589832 | tf_op jit(solution)/shard_map/ppermute | solution.py:27
  25.2 3.1 %collective-permute-start.11 = (bf16[384,256]{1,0:T(8,128)(2,1)S(1)}, bf16[384,256]{1,0:T(8,128)(2,1)S(1)}, u32[]{:S(2)}, u32[]{:S(2)}) collective-permute-start(bf16[384,256]{1,0:T(8,128)(2,1)S(1)} %collective-permute-done.3.rest_3_), channel_id=1, source_target_pairs={{0,1},{1,0},{2,3},{3,2},{4,5},{5,4},{6,7},{7,6},{8,9},{9,8},{10,11... | collective-permute-start | bytes 589832 | tf_op jit(solution)/shard_map/ppermute | solution.py:27
  29.2 3.4 %collective-permute-start.7 = (bf16[384,256]{1,0:T(8,128)(2,1)S(1)}, bf16[384,256]{1,0:T(8,128)(2,1)S(1)}, u32[]{:S(2)}, u32[]{:S(2)}) collective-permute-start(bf16[384,256]{1,0:T(8,128)(2,1)S(1)} %collective-permute-done.6.rest_6_), channel_id=1, source_target_pairs={{0,6},{1,7},{2,0},{3,1},{4,2},{5,3},{6,4},{7,5},{8,14},{9,15},{10,... | collective-permute-start | bytes 589832 | tf_op jit(solution)/shard_map/ppermute | solution.py:27
  32.6 2.9 %collective-permute-start.10 = (bf16[384,256]{1,0:T(8,128)(2,1)S(1)}, bf16[384,256]{1,0:T(8,128)(2,1)S(1)}, u32[]{:S(2)}, u32[]{:S(2)}) collective-permute-start(bf16[384,256]{1,0:T(8,128)(2,1)S(1)} %collective-permute-done.2.rest_2_), channel_id=1, source_target_pairs={{0,1},{1,0},{2,3},{3,2},{4,5},{5,4},{6,7},{7,6},{8,9},{9,8},{10,11... | collective-permute-start | bytes 589832 | tf_op jit(solution)/shard_map/ppermute | solution.py:27
  35.6 2.1 collective-permute-start.14
  39.0 11.9 %collective-permute-start.17 = (bf16[384,128]{1,0:T(8,128)(2,1)S(1)}, bf16[384,128]{1,0:T(8,128)(2,1)S(1)}, u32[]{:S(2)}, u32[]{:S(2)}) collective-permute-start(bf16[384,128]{1,0:T(8,128)(2,1)S(1)} %multiply_convert_fusion), channel_id=1, source_target_pairs={{0,16},{16,0},{32,48},{48,32},{64,80},{80,64},{96,112},{112,96},{1... | collective-permute-start | bytes 294920 | tf_op jit(solution)/shard_map/ppermute | solution.py:27
  51.7 7.9 %project.1 = bf16[256,384]{1,0:T(8,128)(2,1)} custom-call(s32[16]{0:T(128)} %stack.106.place_ref, bf16[256,6144]{1,0:T(8,128)(2,1)} %bitcast.47, bf16[256,6144]{1,0:T(8,128)(2,1)} %bitcast.54, bf16[384,256]{1,0:T(8,128)(2,1)} %copy-done.6, bf16[384,256]{1,0:T(8,128)(2,1)} %copy-done.19, bf16[384,256]{1,0:T(8,128)(2,1)} %copy-done.20, ...), custom_call_target="tpu_custom_call" | custom-call | flops 8000000000 | bytes 9437184 | tf_op jit(solution)/shard_map/project/pallas_call | solution.py:331
  61.6 4.0 %collective-permute-done.16 = bf16[256,384]{1,0:T(8,128)(2,1)S(1)} collective-permute-done((bf16[256,384]{1,0:T(8,128)(2,1)}, bf16[256,384]{1,0:T(8,128)(2,1)S(1)}, u32[]{:S(2)}, u32[]{:S(2)}) %collective-permute-start.16) | collective-permute-done | bytes 196640 | tf_op jit(solution)/shard_map/ppermute | solution.py:27
  67.5 2.1 fusion.5
  70.0 20.3 %all_to_all.20 = bf16[16,128,128]{2,1,0:T(8,128)(2,1)} all-to-all(bf16[16,128,128]{2,1,0:T(8,128)(2,1)S(1)} %bitcast.49), channel_id=1, replica_groups=mesh['section'=16,'fsdp'=16] {'fsdp'}, dimensions={0} | all-to-all | bytes 1048576 | tf_op jit(solution)/shard_map/all_to_all | solution.py:358
  91.5 30.1 %all_to_all.21.rest_0_ = bf16[16,128,128]{2,1,0:T(8,128)(2,1)S(1)} all-to-all(bf16[16,128,128]{2,1,0:T(8,128)(2,1)S(1)} %broadcast_in_dim.33), channel_id=1, replica_groups=mesh['section'=16,'fsdp'=16] {'section'}, dimensions={0} | all-to-all | bytes 1048576 | tf_op jit(solution)/shard_map/all_to_all | solution.py:86
  122.1 2.2 collective-permute-start.19
  124.9 2.7 %collective-permute-start.21 = (bf16[16,128,128]{2,1,0:T(8,128)(2,1)S(1)}, bf16[16,128,128]{2,1,0:T(8,128)(2,1)S(1)}, u32[]{:S(2)}, u32[]{:S(2)}) collective-permute-start(bf16[16,128,128]{2,1,0:T(8,128)(2,1)S(1)} %all_to_all.21.rest_0_), channel_id=1, source_target_pairs={{0,1},{1,0},{2,3},{3,2},{4,5},{5,4},{6,7},{7,6},{8,9},{9,8},{10,11... | collective-permute-start | bytes 1572872 | tf_op jit(solution)/shard_map/ppermute | solution.py:27
  127.6 6.0 %collective-permute-done.18.rest_1_ = bf16[16,128,128]{2,1,0:T(8,128)(2,1)S(1)} collective-permute-done((bf16[16,128,128]{2,1,0:T(8,128)(2,1)S(1)}, bf16[16,128,128]{2,1,0:T(8,128)(2,1)S(1)}, u32[]{:S(2)}, u32[]{:S(2)}) %collective-permute-start.18) | collective-permute-done | bytes 524320 | tf_op jit(solution)/shard_map/ppermute | solution.py:27
  133.8 2.7 %collective-permute-start.23 = (bf16[8,128,128]{2,1,0:T(8,128)(2,1)S(1)}, bf16[8,128,128]{2,1,0:T(8,128)(2,1)}, u32[]{:S(2)}, u32[]{:S(2)}) collective-permute-start(bf16[8,128,128]{2,1,0:T(8,128)(2,1)S(1)} %slice.23), channel_id=1, source_target_pairs={{0,6},{1,7},{2,0},{3,1},{4,2},{5,3},{6,4},{7,5},{8,14},{9,15},{10,... | collective-permute-start | bytes 786440 | tf_op jit(solution)/shard_map/ppermute | solution.py:27
  136.6 4.2 %collective-permute-start.26 = (bf16[16,128,128]{2,1,0:T(8,128)(2,1)S(1)}, bf16[16,128,128]{2,1,0:T(8,128)(2,1)S(1)}, u32[]{:S(2)}, u32[]{:S(2)}) collective-permute-start(bf16[16,128,128]{2,1,0:T(8,128)(2,1)S(1)} %collective-permute-done.20.rest_3_), channel_id=1, source_target_pairs={{0,1},{1,0},{2,3},{3,2},{4,5},{5,4},{6,7},{7,6},{8,9},{9,8},{10,11... | collective-permute-start | bytes 1572872 | tf_op jit(solution)/shard_map/ppermute | solution.py:27
  141.3 2.7 %collective-permute-start.28 = (bf16[16,128,128]{2,1,0:T(8,128)(2,1)S(1)}, bf16[16,128,128]{2,1,0:T(8,128)(2,1)}, u32[]{:S(2)}, u32[]{:S(2)}) collective-permute-start(bf16[16,128,128]{2,1,0:T(8,128)(2,1)S(1)} %collective-permute-done.20.rest_3_), channel_id=1, source_target_pairs={{0,6},{1,7},{2,0},{3,1},{4,2},{5,3},{6,4},{7,5},{8,14},{9,15},{10,... | collective-permute-start | bytes 1572872 | tf_op jit(solution)/shard_map/ppermute | solution.py:27
  144.7 2.1 collective-permute-start.30
  146.8 4.9 %collective-permute-start.31 = (bf16[8,128,128]{2,1,0:T(8,128)(2,1)S(1)}, bf16[8,128,128]{2,1,0:T(8,128)(2,1)S(1)}, u32[]{:S(2)}, u32[]{:S(2)}) collective-permute-start(bf16[8,128,128]{2,1,0:T(8,128)(2,1)S(1)} %collective-permute-done.22.rest_4_), channel_id=1, source_target_pairs={{0,1},{1,0},{2,3},{3,2},{4,5},{5,4},{6,7},{7,6},{8,9},{9,8},{10,11... | collective-permute-start | bytes 786440 | tf_op jit(solution)/shard_map/ppermute | solution.py:27
  152.4 4.5 %collective-permute-start.33 = (bf16[16,128,128]{2,1,0:T(8,128)(2,1)}, bf16[16,128,128]{2,1,0:T(8,128)(2,1)}, u32[]{:S(2)}, u32[]{:S(2)}) collective-permute-start(bf16[16,128,128]{2,1,0:T(8,128)(2,1)} %collective-permute-done.27.rest_6_), channel_id=1, source_target_pairs={{0,1},{1,0},{2,3},{3,2},{4,5},{5,4},{6,7},{7,6},{8,9},{9,8},{10,11... | collective-permute-start | bytes 1572872 | tf_op jit(solution)/shard_map/ppermute | solution.py:27
  157.4 2.3 collective-permute-start.35
  163.1 23.6 %chain.1 = (bf16[8,256,128]{2,1,0:T(8,128)(2,1)}, bf16[8,256,128]{2,1,0:T(8,128)(2,1)}, bf16[8,256,384]{2,1,0:T(8,128)(2,1)}, bf16[8,256,384]{2,1,0:T(8,128)(2,1)}) custom-call(s32[2]{0:T(128)} %pad_add_fusion.s_ref, s32[16]{0:T(128)} %stack.106.place_ref, bf16[16,256,384]{2,1,0:T(8,128)(2,1)} %all-gather.9.cloned.1.call-done.a_hbm, ...), custom_call_target="tpu_custom_call" | custom-call | flops 20000000000 | bytes 12582912 | tf_op jit(solution)/shard_map/chain/pallas_call | solution.py:253
  189.5 2.0 add_convert_fusion.1
  191.5 3.5 %all-to-all-start.2 = ((bf16[8,256,128]{2,1,0:T(8,128)(2,1)}), bf16[8,256,128]{2,1,0:T(8,128)(2,1)S(1)}, u32[]{:S(2)}, u32[]{:S(2)}) async-start(bf16[8,256,128]{2,1,0:T(8,128)(2,1)} %add_convert_fusion.1), calls=%async_computation.2 | async-start | bytes 1048576 | tf_op jit(solution)/shard_map/all_to_all | solution.py:109
  195.7 11.0 %all-to-all-done.2 = bf16[8,256,128]{2,1,0:T(8,128)(2,1)S(1)} async-done(((bf16[8,256,128]{2,1,0:T(8,128)(2,1)}), bf16[8,256,128]{2,1,0:T(8,128)(2,1)S(1)}, u32[]{:S(2)}, u32[]{:S(2)}) %all-to-all-start.2) | async-done | bytes 524320 | tf_op jit(solution)/shard_map/all_to_all | solution.py:109
  206.8 1.9 add_convert_fusion
  209.0 30.1 %all_to_all.22.part_ref = bf16[8,256,512]{2,1,0:T(8,128)(2,1)S(1)} all-to-all(bf16[8,256,512]{2,1,0:T(8,128)(2,1)S(1)} %pad_maximum_fusion), channel_id=1, replica_groups={{0,2,4,6,8,10,12,14},{1,3,5,7,9,11,13,15},{16,18,20,22,24,26,28,30},{17..., dimensions={0} | all-to-all | bytes 4194304 | tf_op jit(solution)/shard_map/all_to_all | solution.py:109
  239.1 1.9 collective-permute-start.39
  243.4 5.7 %finish.1 = (f32[384,128]{1,0:T(8,128)}, f32[1,384]{1,0:T(1,128)}, f32[128,384]{1,0:T(8,128)}) custom-call(s32[2]{0:T(128)} %pad_add_fusion.s_ref, bf16[8,256,512]{2,1,0:T(8,128)(2,1)} %copy-done, bf16[8,256,128]{2,1,0:T(8,128)(2,1)} %copy-done.5, bf16[16,128,384]{2,1,0:T(8,128)(2,1)} %all-gather.7.cloned.1.call-done.up_hbm, ...), custom_call_target="tpu_custom_call" | custom-call | tf_op jit(solution)/shard_map/finish/pallas_call | solution.py:374
  (160 shorter events, 29.4 us)
Async XLA Ops:
  7.2 60.3 %all-gather.7.cloned.1.call-start = ((), (), s32[]{:S(2)}) async-start(), calls=%async_computation.4 | async-start | bytes 1769472 | tf_op jit(solution)/shard_map/all_gather | solution.py:99
  13.3 149.8 %all-gather.9.cloned.1.call-start = ((), (), s32[]{:S(2)}) async-start(), calls=%async_computation.5 | async-start | bytes 3538944 | tf_op jit(solution)/shard_map/all_gather | solution.py:99
  15.2 8.5 %collective-permute-start.3 = (bf16[384,256]{1,0:T(8,128)(2,1)S(1)}, bf16[384,256]{1,0:T(8,128)(2,1)S(1)}, u32[]{:S(2)}, u32[]{:S(2)}) collective-permute-start(bf16[384,256]{1,0:T(8,128)(2,1)S(1)} %pad_maximum_fusion.3.rest_0_), channel_id=1, source_target_pairs={{0,8},{1,9},{2,10},{3,11},{4,12},{5,13},{6,14},{7,15},{8,0},{9,1},... | collective-permute-start | bytes 589832 | tf_op jit(solution)/shard_map/ppermute | solution.py:27
  18.3 6.8 %collective-permute-start.1 = (bf16[384,256]{1,0:T(8,128)(2,1)S(1)}, bf16[384,256]{1,0:T(8,128)(2,1)S(1)}, u32[]{:S(2)}, u32[]{:S(2)}) collective-permute-start(bf16[384,256]{1,0:T(8,128)(2,1)S(1)} %pad_maximum_fusion.3.rest_0_), channel_id=1, source_target_pairs={{0,2},{1,3},{2,4},{3,5},{4,6},{5,7},{6,0},{7,1},{8,10},{9,11},{10,... | collective-permute-start | bytes 589832 | tf_op jit(solution)/shard_map/ppermute | solution.py:27
  21.0 7.4 %collective-permute-start.8 = (bf16[384,256]{1,0:T(8,128)(2,1)S(1)}, bf16[384,256]{1,0:T(8,128)(2,1)S(1)}, u32[]{:S(2)}, u32[]{:S(2)}) collective-permute-start(bf16[384,256]{1,0:T(8,128)(2,1)S(1)} %pad_maximum_fusion.3.rest_0_), channel_id=1, source_target_pairs={{0,1},{1,0},{2,3},{3,2},{4,5},{5,4},{6,7},{7,6},{8,9},{9,8},{10,11... | collective-permute-start | bytes 589832 | tf_op jit(solution)/shard_map/ppermute | solution.py:27
  24.9 7.7 %collective-permute-start.5 = (bf16[384,256]{1,0:T(8,128)(2,1)S(1)}, bf16[384,256]{1,0:T(8,128)(2,1)S(1)}, u32[]{:S(2)}, u32[]{:S(2)}) collective-permute-start(bf16[384,256]{1,0:T(8,128)(2,1)S(1)} %collective-permute-done.3.rest_3_), channel_id=1, source_target_pairs={{0,2},{1,3},{2,4},{3,5},{4,6},{5,7},{6,0},{7,1},{8,10},{9,11},{10,... | collective-permute-start | bytes 589832 | tf_op jit(solution)/shard_map/ppermute | solution.py:27
  25.1 10.4 %collective-permute-start.4 = (bf16[384,256]{1,0:T(8,128)(2,1)S(1)}, bf16[384,256]{1,0:T(8,128)(2,1)S(1)}, u32[]{:S(2)}, u32[]{:S(2)}) collective-permute-start(bf16[384,256]{1,0:T(8,128)(2,1)S(1)} %collective-permute-done.1.rest_1_), channel_id=1, source_target_pairs={{0,2},{1,3},{2,4},{3,5},{4,6},{5,7},{6,0},{7,1},{8,10},{9,11},{10,... | collective-permute-start | bytes 589832 | tf_op jit(solution)/shard_map/ppermute | solution.py:27
  25.2 12.5 %collective-permute-start.11 = (bf16[384,256]{1,0:T(8,128)(2,1)S(1)}, bf16[384,256]{1,0:T(8,128)(2,1)S(1)}, u32[]{:S(2)}, u32[]{:S(2)}) collective-permute-start(bf16[384,256]{1,0:T(8,128)(2,1)S(1)} %collective-permute-done.3.rest_3_), channel_id=1, source_target_pairs={{0,1},{1,0},{2,3},{3,2},{4,5},{5,4},{6,7},{7,6},{8,9},{9,8},{10,11... | collective-permute-start | bytes 589832 | tf_op jit(solution)/shard_map/ppermute | solution.py:27
  28.4 9.4 %collective-permute-start.9 = (bf16[384,256]{1,0:T(8,128)(2,1)S(1)}, bf16[384,256]{1,0:T(8,128)(2,1)S(1)}, u32[]{:S(2)}, u32[]{:S(2)}) collective-permute-start(bf16[384,256]{1,0:T(8,128)(2,1)S(1)} %collective-permute-done.1.rest_1_), channel_id=1, source_target_pairs={{0,1},{1,0},{2,3},{3,2},{4,5},{5,4},{6,7},{7,6},{8,9},{9,8},{10,11... | collective-permute-start | bytes 589832 | tf_op jit(solution)/shard_map/ppermute | solution.py:27
  29.2 9.0 %collective-permute-start.7 = (bf16[384,256]{1,0:T(8,128)(2,1)S(1)}, bf16[384,256]{1,0:T(8,128)(2,1)S(1)}, u32[]{:S(2)}, u32[]{:S(2)}) collective-permute-start(bf16[384,256]{1,0:T(8,128)(2,1)S(1)} %collective-permute-done.6.rest_6_), channel_id=1, source_target_pairs={{0,6},{1,7},{2,0},{3,1},{4,2},{5,3},{6,4},{7,5},{8,14},{9,15},{10,... | collective-permute-start | bytes 589832 | tf_op jit(solution)/shard_map/ppermute | solution.py:27
  32.6 6.3 %collective-permute-start.10 = (bf16[384,256]{1,0:T(8,128)(2,1)S(1)}, bf16[384,256]{1,0:T(8,128)(2,1)S(1)}, u32[]{:S(2)}, u32[]{:S(2)}) collective-permute-start(bf16[384,256]{1,0:T(8,128)(2,1)S(1)} %collective-permute-done.2.rest_2_), channel_id=1, source_target_pairs={{0,1},{1,0},{2,3},{3,2},{4,5},{5,4},{6,7},{7,6},{8,9},{9,8},{10,11... | collective-permute-start | bytes 589832 | tf_op jit(solution)/shard_map/ppermute | solution.py:27
  35.6 15.2 %collective-permute-start.14 = (bf16[384,256]{1,0:T(8,128)(2,1)S(1)}, bf16[384,256]{1,0:T(8,128)(2,1)S(1)}, u32[]{:S(2)}, u32[]{:S(2)}) collective-permute-start(bf16[384,256]{1,0:T(8,128)(2,1)S(1)} %collective-permute-done.6.rest_6_), channel_id=1, source_target_pairs={{0,1},{1,0},{2,3},{3,2},{4,5},{5,4},{6,7},{7,6},{8,9},{9,8},{10,11... | collective-permute-start | bytes 589832 | tf_op jit(solution)/shard_map/ppermute | solution.py:27
  37.7 13.1 %collective-permute-start.13 = (bf16[384,256]{1,0:T(8,128)(2,1)S(1)}, bf16[384,256]{1,0:T(8,128)(2,1)S(1)}, u32[]{:S(2)}, u32[]{:S(2)}) collective-permute-start(bf16[384,256]{1,0:T(8,128)(2,1)S(1)} %collective-permute-done.5.rest_5_), channel_id=1, source_target_pairs={{0,1},{1,0},{2,3},{3,2},{4,5},{5,4},{6,7},{7,6},{8,9},{9,8},{10,11... | collective-permute-start | bytes 589832 | tf_op jit(solution)/shard_map/ppermute | solution.py:27
  37.8 13.0 %collective-permute-start.12 = (bf16[384,256]{1,0:T(8,128)(2,1)S(1)}, bf16[384,256]{1,0:T(8,128)(2,1)S(1)}, u32[]{:S(2)}, u32[]{:S(2)}) collective-permute-start(bf16[384,256]{1,0:T(8,128)(2,1)S(1)} %collective-permute-done.4.rest_4_), channel_id=1, source_target_pairs={{0,1},{1,0},{2,3},{3,2},{4,5},{5,4},{6,7},{7,6},{8,9},{9,8},{10,11... | collective-permute-start | bytes 589832 | tf_op jit(solution)/shard_map/ppermute | solution.py:27
  38.2 12.6 %collective-permute-start.15 = (bf16[384,256]{1,0:T(8,128)(2,1)S(1)}, bf16[384,256]{1,0:T(8,128)(2,1)S(1)}, u32[]{:S(2)}, u32[]{:S(2)}) collective-permute-start(bf16[384,256]{1,0:T(8,128)(2,1)S(1)} %collective-permute-done.7.rest_7_), channel_id=1, source_target_pairs={{0,1},{1,0},{2,3},{3,2},{4,5},{5,4},{6,7},{7,6},{8,9},{9,8},{10,11... | collective-permute-start | bytes 589832 | tf_op jit(solution)/shard_map/ppermute | solution.py:27
  39.0 21.8 %collective-permute-start.17 = (bf16[384,128]{1,0:T(8,128)(2,1)S(1)}, bf16[384,128]{1,0:T(8,128)(2,1)S(1)}, u32[]{:S(2)}, u32[]{:S(2)}) collective-permute-start(bf16[384,128]{1,0:T(8,128)(2,1)S(1)} %multiply_convert_fusion), channel_id=1, source_target_pairs={{0,16},{16,0},{32,48},{48,32},{64,80},{80,64},{96,112},{112,96},{1... | collective-permute-start | bytes 294920 | tf_op jit(solution)/shard_map/ppermute | solution.py:27
  121.6 12.0 %collective-permute-start.18 = (bf16[16,128,128]{2,1,0:T(8,128)(2,1)S(1)}, bf16[16,128,128]{2,1,0:T(8,128)(2,1)S(1)}, u32[]{:S(2)}, u32[]{:S(2)}) collective-permute-start(bf16[16,128,128]{2,1,0:T(8,128)(2,1)S(1)} %all_to_all.21.rest_0_), channel_id=1, source_target_pairs={{0,2},{1,3},{2,4},{3,5},{4,6},{5,7},{6,0},{7,1},{8,10},{9,11},{10,... | collective-permute-start | bytes 1572872 | tf_op jit(solution)/shard_map/ppermute | solution.py:27
  122.1 11.7 %collective-permute-start.19 = (bf16[16,128,128]{2,1,0:T(8,128)(2,1)S(1)}, bf16[16,128,128]{2,1,0:T(8,128)(2,1)S(1)}, u32[]{:S(2)}, u32[]{:S(2)}) collective-permute-start(bf16[16,128,128]{2,1,0:T(8,128)(2,1)S(1)} %all_to_all.21.rest_0_), channel_id=1, source_target_pairs={{0,6},{1,7},{2,0},{3,1},{4,2},{5,3},{6,4},{7,5},{8,14},{9,15},{10,... | collective-permute-start | bytes 1572872 | tf_op jit(solution)/shard_map/ppermute | solution.py:27
  124.3 12.2 %collective-permute-start.20 = (bf16[16,128,128]{2,1,0:T(8,128)(2,1)S(1)}, bf16[16,128,128]{2,1,0:T(8,128)(2,1)S(1)}, u32[]{:S(2)}, u32[]{:S(2)}) collective-permute-start(bf16[16,128,128]{2,1,0:T(8,128)(2,1)S(1)} %all_to_all.21.rest_0_), channel_id=1, source_target_pairs={{0,24},{1,25},{2,26},{3,27},{4,28},{5,29},{6,30},{7,31},{8,16},{9,... | collective-permute-start | bytes 1572872 | tf_op jit(solution)/shard_map/ppermute | solution.py:40
  124.9 11.6 %collective-permute-start.21 = (bf16[16,128,128]{2,1,0:T(8,128)(2,1)S(1)}, bf16[16,128,128]{2,1,0:T(8,128)(2,1)S(1)}, u32[]{:S(2)}, u32[]{:S(2)}) collective-permute-start(bf16[16,128,128]{2,1,0:T(8,128)(2,1)S(1)} %all_to_all.21.rest_0_), channel_id=1, source_target_pairs={{0,1},{1,0},{2,3},{3,2},{4,5},{5,4},{6,7},{7,6},{8,9},{9,8},{10,11... | collective-permute-start | bytes 1572872 | tf_op jit(solution)/shard_map/ppermute | solution.py:27
  133.7 7.6 %collective-permute-start.22 = (bf16[8,128,128]{2,1,0:T(8,128)(2,1)S(1)}, bf16[8,128,128]{2,1,0:T(8,128)(2,1)S(1)}, u32[]{:S(2)}, u32[]{:S(2)}) collective-permute-start(bf16[8,128,128]{2,1,0:T(8,128)(2,1)S(1)} %slice.22), channel_id=1, source_target_pairs={{0,2},{1,3},{2,4},{3,5},{4,6},{5,7},{6,0},{7,1},{8,10},{9,11},{10,... | collective-permute-start | bytes 786440 | tf_op jit(solution)/shard_map/ppermute | solution.py:27
  133.8 7.4 %collective-permute-start.23 = (bf16[8,128,128]{2,1,0:T(8,128)(2,1)S(1)}, bf16[8,128,128]{2,1,0:T(8,128)(2,1)}, u32[]{:S(2)}, u32[]{:S(2)}) collective-permute-start(bf16[8,128,128]{2,1,0:T(8,128)(2,1)S(1)} %slice.23), channel_id=1, source_target_pairs={{0,6},{1,7},{2,0},{3,1},{4,2},{5,3},{6,4},{7,5},{8,14},{9,15},{10,... | collective-permute-start | bytes 786440 | tf_op jit(solution)/shard_map/ppermute | solution.py:27
  136.6 7.4 %collective-permute-start.26 = (bf16[16,128,128]{2,1,0:T(8,128)(2,1)S(1)}, bf16[16,128,128]{2,1,0:T(8,128)(2,1)S(1)}, u32[]{:S(2)}, u32[]{:S(2)}) collective-permute-start(bf16[16,128,128]{2,1,0:T(8,128)(2,1)S(1)} %collective-permute-done.20.rest_3_), channel_id=1, source_target_pairs={{0,1},{1,0},{2,3},{3,2},{4,5},{5,4},{6,7},{7,6},{8,9},{9,8},{10,11... | collective-permute-start | bytes 1572872 | tf_op jit(solution)/shard_map/ppermute | solution.py:27
  141.3 11.1 %collective-permute-start.27 = (bf16[16,128,128]{2,1,0:T(8,128)(2,1)S(1)}, bf16[16,128,128]{2,1,0:T(8,128)(2,1)}, u32[]{:S(2)}, u32[]{:S(2)}) collective-permute-start(bf16[16,128,128]{2,1,0:T(8,128)(2,1)S(1)} %collective-permute-done.20.rest_3_), channel_id=1, source_target_pairs={{0,2},{1,3},{2,4},{3,5},{4,6},{5,7},{6,0},{7,1},{8,10},{9,11},{10,... | collective-permute-start | bytes 1572872 | tf_op jit(solution)/shard_map/ppermute | solution.py:27
  141.3 15.6 %collective-permute-start.28 = (bf16[16,128,128]{2,1,0:T(8,128)(2,1)S(1)}, bf16[16,128,128]{2,1,0:T(8,128)(2,1)}, u32[]{:S(2)}, u32[]{:S(2)}) collective-permute-start(bf16[16,128,128]{2,1,0:T(8,128)(2,1)S(1)} %collective-permute-done.20.rest_3_), channel_id=1, source_target_pairs={{0,6},{1,7},{2,0},{3,1},{4,2},{5,3},{6,4},{7,5},{8,14},{9,15},{10,... | collective-permute-start | bytes 1572872 | tf_op jit(solution)/shard_map/ppermute | solution.py:27
  144.0 12.9 %collective-permute-start.29 = (bf16[8,128,128]{2,1,0:T(8,128)(2,1)S(1)}, bf16[8,128,128]{2,1,0:T(8,128)(2,1)S(1)}, u32[]{:S(2)}, u32[]{:S(2)}) collective-permute-start(bf16[8,128,128]{2,1,0:T(8,128)(2,1)S(1)} %collective-permute-done.22.rest_4_), channel_id=1, source_target_pairs={{0,24},{1,25},{2,26},{3,27},{4,28},{5,29},{6,30},{7,31},{8,16},{9,... | collective-permute-start | bytes 786440 | tf_op jit(solution)/shard_map/ppermute | solution.py:40
  144.7 12.8 %collective-permute-start.30 = (bf16[8,128,128]{2,1,0:T(8,128)(2,1)}, bf16[8,128,128]{2,1,0:T(8,128)(2,1)}, u32[]{:S(2)}, u32[]{:S(2)}) collective-permute-start(bf16[8,128,128]{2,1,0:T(8,128)(2,1)} %collective-permute-done.23.rest_5_), channel_id=1, source_target_pairs={{0,24},{1,25},{2,26},{3,27},{4,28},{5,29},{6,30},{7,31},{8,16},{9,... | collective-permute-start | bytes 786440 | tf_op jit(solution)/shard_map/ppermute | solution.py:40
  146.8 13.0 %collective-permute-start.31 = (bf16[8,128,128]{2,1,0:T(8,128)(2,1)S(1)}, bf16[8,128,128]{2,1,0:T(8,128)(2,1)S(1)}, u32[]{:S(2)}, u32[]{:S(2)}) collective-permute-start(bf16[8,128,128]{2,1,0:T(8,128)(2,1)S(1)} %collective-permute-done.22.rest_4_), channel_id=1, source_target_pairs={{0,1},{1,0},{2,3},{3,2},{4,5},{5,4},{6,7},{7,6},{8,9},{9,8},{10,11... | collective-permute-start | bytes 786440 | tf_op jit(solution)/shard_map/ppermute | solution.py:27
  152.4 10.7 %collective-permute-start.33 = (bf16[16,128,128]{2,1,0:T(8,128)(2,1)}, bf16[16,128,128]{2,1,0:T(8,128)(2,1)}, u32[]{:S(2)}, u32[]{:S(2)}) collective-permute-start(bf16[16,128,128]{2,1,0:T(8,128)(2,1)} %collective-permute-done.27.rest_6_), channel_id=1, source_target_pairs={{0,1},{1,0},{2,3},{3,2},{4,5},{5,4},{6,7},{7,6},{8,9},{9,8},{10,11... | collective-permute-start | bytes 1572872 | tf_op jit(solution)/shard_map/ppermute | solution.py:27
  189.1 17.7 %collective-permute-start.38 = (bf16[8,256,384]{2,1,0:T(8,128)(2,1)}, bf16[8,256,384]{2,1,0:T(8,128)(2,1)}, u32[]{:S(2)}, u32[]{:S(2)}) collective-permute-start(bf16[8,256,384]{2,1,0:T(8,128)(2,1)} %get-tuple-element.38), channel_id=1, source_target_pairs={{0,1},{1,0},{2,3},{3,2},{4,5},{5,4},{6,7},{7,6},{8,9},{9,8},{10,11... | collective-permute-start | bytes 4718600 | tf_op jit(solution)/shard_map/ppermute | solution.py:27
  191.5 15.2 %all-to-all-start.2 = ((bf16[8,256,128]{2,1,0:T(8,128)(2,1)}), bf16[8,256,128]{2,1,0:T(8,128)(2,1)S(1)}, u32[]{:S(2)}, u32[]{:S(2)}) async-start(bf16[8,256,128]{2,1,0:T(8,128)(2,1)} %add_convert_fusion.1), calls=%async_computation.2 | async-start | bytes 1048576 | tf_op jit(solution)/shard_map/all_to_all | solution.py:109
  195.0 46.6 %all-gather.11.cloned.1.call-start = ((), (), s32[]{:S(2)}) async-start(), calls=%async_computation.6 | async-start | bytes 1769472 | tf_op jit(solution)/shard_map/all_gather | solution.py:99
  (45 other events, 597.2 us)
Sparse Core Ops, SparseCore 0:
  13.5 40.1 all-gather.6
  67.6 60.0 all-gather.8
  198.2 34.2 all-gather.10

commit v2 on v1

--- a/solution.py
+++ b/solution.py
@@ -131,7 +131,7 @@
     pieces = rest[:20]
     keep_ref, send_ref, keep_part, send_part = rest[20:24]
     z_ref, a_ref, w_ref, lift_ref, act_ref, slope_ref, inv_ref = rest[24:31]
-    q_ref, p_ref, sq_ref, sums_ref, x_ref, y_ref, sem = rest[31:]
+    q_ref, p_ref, sq_ref, x_ref, y_ref, sem = rest[31:]
     layers = a_ref.shape[0]
     rank = z_ref.shape[2]
     cut = [slice(rank * i, rank * (i + 1)) for i in range(layers)]
@@ -207,31 +207,24 @@
     here = pl.ds(pl.multiple_of(s_ref[0] * rank, rank), rank)
     p_t, q_t, sq_t = p_ref[:, here].T, q_ref[:, here].T, sq_ref[:, here].T
     both = jnp.concatenate([p_t, -sq_t], axis=0)
-    for j in range(layers):
-
-        @pl.when(j < s_ref[0])
-        def _():
-            sums_ref[...] = dot(both, q_ref[:, cut[j]], NN).astype(BF16)
-
-        @pl.when(j >= s_ref[0])
-        def _():
-            first = dot(q_t, p_ref[:, cut[j]], NN)
-            first = jnp.where(j == s_ref[0], 0.0, first)
-            sums_ref[:rank] = first.astype(BF16)
-            sums_ref[rank:] = (-dot(q_t, sq_ref[:, cut[j]], NN)).astype(BF16)
-
-        @pl.when(s_ref[1] == j % 2)
-        def _():
-            keep_ref[j // 2] = sums_ref[...]
-
-        @pl.when(s_ref[1] != j % 2)
-        def _():
-            send_ref[j // 2] = sums_ref[...]
+    even_core = s_ref[1] == 0
+    for i in range(layers // 2):
+        span = slice(2 * rank * i, 2 * rank * (i + 1))
+        before = dot(both, q_ref[:, span], NN)
+        after = dot(q_t, p_ref[:, span], NN)
+        scaled = -dot(q_t, sq_ref[:, span], NN)
+        found = []
+        for k in range(2):
+            j, some = 2 * i + k, slice(rank * k, rank * (k + 1))
+            later = jnp.where(j == s_ref[0], 0.0, after[:, some])
+            later = jnp.concatenate([later, scaled[:, some]], axis=0)
+            found.append(jnp.where(j < s_ref[0], before[:, some], later).astype(BF16))
+        keep_ref[i] = jnp.where(even_core, found[0], found[1])
+        send_ref[i] = jnp.where(even_core, found[1], found[0])
 
     for copy in whole:
         copy.wait()
     half, _, piece = keep_part.shape
-    even_core = s_ref[1] == 0
     for i in range(half):
         span = slice(2 * piece * i, 2 * piece * (i + 1))
         from_x = dot(both, x_ref[:, span], NN)
@@ -264,7 +257,6 @@
         + [pltpu.VMEM((sections, tokens, wide), BF16)]
         + [big] * 5
         + [flat] * 3
-        + [pltpu.VMEM((2 * rank, rank), BF16)]
         + [pltpu.VMEM(x.shape, BF16)] * 2
         + [pltpu.SemaphoreType.DMA((5, 16))],
         compiler_params=pltpu.CompilerParams(vmem_limit_bytes=57 * MIB),

time: 259 us -> 254 us (0.981)
  starting transfers between devices: 75.6 us -> 72.5 us
  Pallas kernels: 37.2 us -> 34.5 us
    ppermute x37, starting transfers between devices: 68.6 us -> 65.5 us  [hop(): return lax.ppermute(block, axis, route)]
    pallas_call x1, Pallas kernels: 23.6 us -> 20.9 us  [chain_call(): pl.pallas_call(functools.partial(chain, width), out_shape=(jax.ShapeDtype...]
  transfers between devices with their start and end apart: 44 -> 44, of which waited for: 8 -> 9; matrix products, arithmetic and copies ran while one was open for 6% -> 6% of each run, Pallas kernels for 3% -> 3%
where the time goes in v2:
time: 254 us; the launch traced here: 250 us
  blocking collectives  80.4 us (32%)
  starting transfers between devices  72.5 us (29%)
  Pallas kernels  34.5 us (14%)
  waiting for transfers between devices  28.1 us (11%)
  between operations  14.5 us (6%)
  other arithmetic  12 us (5%)
  local copies, waits for them, and re-layouts  5.84 us (2%)
    ppermute x37, starting transfers between devices, hop(): return lax.ppermute(block, axis, route)  65.5 us
    all_to_all x1, blocking collectives, among_chips(): lax.all_to_all(chunks, 'fsdp', 0, 0, tiled=True, axis_index_groups=chips)  30.1 us
    all_to_all x1, blocking collectives, gather_section(): lax.all_to_all(jnp.broadcast_to(block[None], (16,) + block.shape), 'secti...  29.8 us
    pallas_call x1, Pallas kernels, chain_call(): pl.pallas_call(functools.partial(chain, width), out_shape=(jax.ShapeDtype...  20.9 us
    all_to_all x1, blocking collectives, on_device(): chosen = lax.all_to_all(chosen, 'fsdp', 0, 0, tiled=True)  20.5 us
    ppermute x37, waiting for transfers between devices, hop(): return lax.ppermute(block, axis, route)  16.3 us
    all_to_all x1, waiting for transfers between devices, among_chips(): lax.all_to_all(chunks, 'fsdp', 0, 0, tiled=True, axis_index_groups=chips)  11 us
    pallas_call x1, Pallas kernels, on_device(): pl.pallas_call(project, out_shape=jax.ShapeDtypeStruct((tokens, 3 * rank)...  7.96 us
  transfers between devices with their start and end apart: 44, of which 9 were waited for; matrix products, arithmetic and copies ran while one was open for 6% of the time, Pallas kernels for 3%

profile of v2, /device:TPU:1, one launch (start us, length us, event | category | flops | bytes accessed | tf_op | source)
XLA Modules:
  0.0 250.0 jit_solution(17053418212454848055)
XLA Ops:
  8.2 2.2 collective-permute-start
  10.4 2.0 collective-permute-done
  15.2 3.2 %collective-permute-start.3 = (bf16[384,256]{1,0:T(8,128)(2,1)S(1)}, bf16[384,256]{1,0:T(8,128)(2,1)S(1)}, u32[]{:S(2)}, u32[]{:S(2)}) collective-permute-start(bf16[384,256]{1,0:T(8,128)(2,1)S(1)} %pad_maximum_fusion.3.rest_0_), channel_id=1, source_target_pairs={{0,8},{1,9},{2,10},{3,11},{4,12},{5,13},{6,14},{7,15},{8,0},{9,1},... | collective-permute-start | bytes 589832 | tf_op jit(solution)/shard_map/ppermute | solution.py:27
  21.0 2.7 %collective-permute-start.8 = (bf16[384,256]{1,0:T(8,128)(2,1)S(1)}, bf16[384,256]{1,0:T(8,128)(2,1)S(1)}, u32[]{:S(2)}, u32[]{:S(2)}) collective-permute-start(bf16[384,256]{1,0:T(8,128)(2,1)S(1)} %pad_maximum_fusion.3.rest_0_), channel_id=1, source_target_pairs={{0,1},{1,0},{2,3},{3,2},{4,5},{5,4},{6,7},{7,6},{8,9},{9,8},{10,11... | collective-permute-start | bytes 589832 | tf_op jit(solution)/shard_map/ppermute | solution.py:27
  25.2 3.1 %collective-permute-start.11 = (bf16[384,256]{1,0:T(8,128)(2,1)S(1)}, bf16[384,256]{1,0:T(8,128)(2,1)S(1)}, u32[]{:S(2)}, u32[]{:S(2)}) collective-permute-start(bf16[384,256]{1,0:T(8,128)(2,1)S(1)} %collective-permute-done.3.rest_3_), channel_id=1, source_target_pairs={{0,1},{1,0},{2,3},{3,2},{4,5},{5,4},{6,7},{7,6},{8,9},{9,8},{10,11... | collective-permute-start | bytes 589832 | tf_op jit(solution)/shard_map/ppermute | solution.py:27
  29.2 3.4 %collective-permute-start.7 = (bf16[384,256]{1,0:T(8,128)(2,1)S(1)}, bf16[384,256]{1,0:T(8,128)(2,1)S(1)}, u32[]{:S(2)}, u32[]{:S(2)}) collective-permute-start(bf16[384,256]{1,0:T(8,128)(2,1)S(1)} %collective-permute-done.6.rest_6_), channel_id=1, source_target_pairs={{0,6},{1,7},{2,0},{3,1},{4,2},{5,3},{6,4},{7,5},{8,14},{9,15},{10,... | collective-permute-start | bytes 589832 | tf_op jit(solution)/shard_map/ppermute | solution.py:27
  32.6 2.9 %collective-permute-start.10 = (bf16[384,256]{1,0:T(8,128)(2,1)S(1)}, bf16[384,256]{1,0:T(8,128)(2,1)S(1)}, u32[]{:S(2)}, u32[]{:S(2)}) collective-permute-start(bf16[384,256]{1,0:T(8,128)(2,1)S(1)} %collective-permute-done.2.rest_2_), channel_id=1, source_target_pairs={{0,1},{1,0},{2,3},{3,2},{4,5},{5,4},{6,7},{7,6},{8,9},{9,8},{10,11... | collective-permute-start | bytes 589832 | tf_op jit(solution)/shard_map/ppermute | solution.py:27
  35.6 2.1 collective-permute-start.14
  40.5 8.0 %project.1 = bf16[256,384]{1,0:T(8,128)(2,1)} custom-call(s32[16]{0:T(128)} %stack.106.place_ref, bf16[256,6144]{1,0:T(8,128)(2,1)} %bitcast.47, bf16[256,6144]{1,0:T(8,128)(2,1)} %bitcast.54, bf16[384,256]{1,0:T(8,128)(2,1)} %copy-done.6, bf16[384,256]{1,0:T(8,128)(2,1)} %copy-done.19, bf16[384,256]{1,0:T(8,128)(2,1)} %copy-done.20, ...), custom_call_target="tpu_custom_call" | custom-call | flops 8000000000 | bytes 9437184 | tf_op jit(solution)/shard_map/project/pallas_call | solution.py:323
  50.4 4.1 %collective-permute-done.16 = bf16[256,384]{1,0:T(8,128)(2,1)S(1)} collective-permute-done((bf16[256,384]{1,0:T(8,128)(2,1)}, bf16[256,384]{1,0:T(8,128)(2,1)S(1)}, u32[]{:S(2)}, u32[]{:S(2)}) %collective-permute-start.16) | collective-permute-done | bytes 196640 | tf_op jit(solution)/shard_map/ppermute | solution.py:27
  56.3 2.1 fusion.5
  58.9 20.5 %all_to_all.20 = bf16[16,128,128]{2,1,0:T(8,128)(2,1)} all-to-all(bf16[16,128,128]{2,1,0:T(8,128)(2,1)S(1)} %bitcast.49), channel_id=1, replica_groups=mesh['section'=16,'fsdp'=16] {'fsdp'}, dimensions={0} | all-to-all | bytes 1048576 | tf_op jit(solution)/shard_map/all_to_all | solution.py:350
  80.7 29.8 %all_to_all.21.rest_0_ = bf16[16,128,128]{2,1,0:T(8,128)(2,1)S(1)} all-to-all(bf16[16,128,128]{2,1,0:T(8,128)(2,1)S(1)} %broadcast_in_dim.33), channel_id=1, replica_groups=mesh['section'=16,'fsdp'=16] {'section'}, dimensions={0} | all-to-all | bytes 1048576 | tf_op jit(solution)/shard_map/all_to_all | solution.py:86
  110.9 2.2 collective-permute-start.19
  113.7 2.7 %collective-permute-start.21 = (bf16[16,128,128]{2,1,0:T(8,128)(2,1)S(1)}, bf16[16,128,128]{2,1,0:T(8,128)(2,1)S(1)}, u32[]{:S(2)}, u32[]{:S(2)}) collective-permute-start(bf16[16,128,128]{2,1,0:T(8,128)(2,1)S(1)} %all_to_all.21.rest_0_), channel_id=1, source_target_pairs={{0,1},{1,0},{2,3},{3,2},{4,5},{5,4},{6,7},{7,6},{8,9},{9,8},{10,11... | collective-permute-start | bytes 1572872 | tf_op jit(solution)/shard_map/ppermute | solution.py:27
  116.5 6.0 %collective-permute-done.18.rest_1_ = bf16[16,128,128]{2,1,0:T(8,128)(2,1)S(1)} collective-permute-done((bf16[16,128,128]{2,1,0:T(8,128)(2,1)S(1)}, bf16[16,128,128]{2,1,0:T(8,128)(2,1)S(1)}, u32[]{:S(2)}, u32[]{:S(2)}) %collective-permute-start.18) | collective-permute-done | bytes 524320 | tf_op jit(solution)/shard_map/ppermute | solution.py:27
  122.7 2.7 %collective-permute-start.23 = (bf16[8,128,128]{2,1,0:T(8,128)(2,1)S(1)}, bf16[8,128,128]{2,1,0:T(8,128)(2,1)}, u32[]{:S(2)}, u32[]{:S(2)}) collective-permute-start(bf16[8,128,128]{2,1,0:T(8,128)(2,1)S(1)} %slice.23), channel_id=1, source_target_pairs={{0,6},{1,7},{2,0},{3,1},{4,2},{5,3},{6,4},{7,5},{8,14},{9,15},{10,... | collective-permute-start | bytes 786440 | tf_op jit(solution)/shard_map/ppermute | solution.py:27
  125.4 4.2 %collective-permute-start.26 = (bf16[16,128,128]{2,1,0:T(8,128)(2,1)S(1)}, bf16[16,128,128]{2,1,0:T(8,128)(2,1)S(1)}, u32[]{:S(2)}, u32[]{:S(2)}) collective-permute-start(bf16[16,128,128]{2,1,0:T(8,128)(2,1)S(1)} %collective-permute-done.20.rest_3_), channel_id=1, source_target_pairs={{0,1},{1,0},{2,3},{3,2},{4,5},{5,4},{6,7},{7,6},{8,9},{9,8},{10,11... | collective-permute-start | bytes 1572872 | tf_op jit(solution)/shard_map/ppermute | solution.py:27
  130.1 2.7 %collective-permute-start.28 = (bf16[16,128,128]{2,1,0:T(8,128)(2,1)S(1)}, bf16[16,128,128]{2,1,0:T(8,128)(2,1)}, u32[]{:S(2)}, u32[]{:S(2)}) collective-permute-start(bf16[16,128,128]{2,1,0:T(8,128)(2,1)S(1)} %collective-permute-done.20.rest_3_), channel_id=1, source_target_pairs={{0,6},{1,7},{2,0},{3,1},{4,2},{5,3},{6,4},{7,5},{8,14},{9,15},{10,... | collective-permute-start | bytes 1572872 | tf_op jit(solution)/shard_map/ppermute | solution.py:27
  133.5 2.1 collective-permute-start.30
  135.6 4.9 %collective-permute-start.31 = (bf16[8,128,128]{2,1,0:T(8,128)(2,1)S(1)}, bf16[8,128,128]{2,1,0:T(8,128)(2,1)S(1)}, u32[]{:S(2)}, u32[]{:S(2)}) collective-permute-start(bf16[8,128,128]{2,1,0:T(8,128)(2,1)S(1)} %collective-permute-done.22.rest_4_), channel_id=1, source_target_pairs={{0,1},{1,0},{2,3},{3,2},{4,5},{5,4},{6,7},{7,6},{8,9},{9,8},{10,11... | collective-permute-start | bytes 786440 | tf_op jit(solution)/shard_map/ppermute | solution.py:27
  141.2 4.5 %collective-permute-start.33 = (bf16[16,128,128]{2,1,0:T(8,128)(2,1)}, bf16[16,128,128]{2,1,0:T(8,128)(2,1)}, u32[]{:S(2)}, u32[]{:S(2)}) collective-permute-start(bf16[16,128,128]{2,1,0:T(8,128)(2,1)} %collective-permute-done.27.rest_6_), channel_id=1, source_target_pairs={{0,1},{1,0},{2,3},{3,2},{4,5},{5,4},{6,7},{7,6},{8,9},{9,8},{10,11... | collective-permute-start | bytes 1572872 | tf_op jit(solution)/shard_map/ppermute | solution.py:27
  146.3 2.3 collective-permute-start.35
  149.3 8.5 %collective-permute-start.36 = (bf16[8,128,128]{2,1,0:T(8,128)(2,1)}, bf16[8,128,128]{2,1,0:T(8,128)(2,1)}, u32[]{:S(2)}, u32[]{:S(2)}) collective-permute-start(bf16[8,128,128]{2,1,0:T(8,128)(2,1)} %collective-permute-done.30.rest_9_), channel_id=1, source_target_pairs={{0,1},{1,0},{2,3},{3,2},{4,5},{5,4},{6,7},{7,6},{8,9},{9,8},{10,11... | collective-permute-start | bytes 786440 | tf_op jit(solution)/shard_map/ppermute | solution.py:27
  160.1 20.9 %chain.1 = (bf16[8,256,128]{2,1,0:T(8,128)(2,1)}, bf16[8,256,128]{2,1,0:T(8,128)(2,1)}, bf16[8,256,384]{2,1,0:T(8,128)(2,1)}, bf16[8,256,384]{2,1,0:T(8,128)(2,1)}) custom-call(s32[2]{0:T(128)} %pad_add_fusion.s_ref, s32[16]{0:T(128)} %stack.106.place_ref, bf16[16,256,384]{2,1,0:T(8,128)(2,1)} %all-gather.9.cloned.1.call-done.a_hbm, ...), custom_call_target="tpu_custom_call" | custom-call | flops 20000000000 | bytes 12582912 | tf_op jit(solution)/shard_map/chain/pallas_call | solution.py:246
  183.7 2.0 add_convert_fusion.1
  185.7 3.5 %all-to-all-start.2 = ((bf16[8,256,128]{2,1,0:T(8,128)(2,1)}), bf16[8,256,128]{2,1,0:T(8,128)(2,1)S(1)}, u32[]{:S(2)}, u32[]{:S(2)}) async-start(bf16[8,256,128]{2,1,0:T(8,128)(2,1)} %add_convert_fusion.1), calls=%async_computation.2 | async-start | bytes 1048576 | tf_op jit(solution)/shard_map/all_to_all | solution.py:109
  189.9 11.0 %all-to-all-done.2 = bf16[8,256,128]{2,1,0:T(8,128)(2,1)S(1)} async-done(((bf16[8,256,128]{2,1,0:T(8,128)(2,1)}), bf16[8,256,128]{2,1,0:T(8,128)(2,1)S(1)}, u32[]{:S(2)}, u32[]{:S(2)}) %all-to-all-start.2) | async-done | bytes 524320 | tf_op jit(solution)/shard_map/all_to_all | solution.py:109
  201.0 1.9 add_convert_fusion
  203.2 30.1 %all_to_all.22.part_ref = bf16[8,256,512]{2,1,0:T(8,128)(2,1)S(1)} all-to-all(bf16[8,256,512]{2,1,0:T(8,128)(2,1)S(1)} %pad_maximum_fusion), channel_id=1, replica_groups={{0,2,4,6,8,10,12,14},{1,3,5,7,9,11,13,15},{16,18,20,22,24,26,28,30},{17..., dimensions={0} | all-to-all | bytes 4194304 | tf_op jit(solution)/shard_map/all_to_all | solution.py:109
  233.3 1.9 collective-permute-start.39
  237.6 5.7 %finish.1 = (f32[384,128]{1,0:T(8,128)}, f32[1,384]{1,0:T(1,128)}, f32[128,384]{1,0:T(8,128)}) custom-call(s32[2]{0:T(128)} %pad_add_fusion.s_ref, bf16[8,256,512]{2,1,0:T(8,128)(2,1)} %copy-done, bf16[8,256,128]{2,1,0:T(8,128)(2,1)} %copy-done.5, bf16[16,128,384]{2,1,0:T(8,128)(2,1)} %all-gather.7.cloned.1.call-done.up_hbm, ...), custom_call_target="tpu_custom_call" | custom-call | tf_op jit(solution)/shard_map/finish/pallas_call | solution.py:366
  (160 shorter events, 29.6 us)
Async XLA Ops:
  7.2 49.1 %all-gather.7.cloned.1.call-start = ((), (), s32[]{:S(2)}) async-start(), calls=%async_computation.4 | async-start | bytes 1769472 | tf_op jit(solution)/shard_map/all_gather | solution.py:99
  13.3 146.7 %all-gather.9.cloned.1.call-start = ((), (), s32[]{:S(2)}) async-start(), calls=%async_computation.5 | async-start | bytes 3538944 | tf_op jit(solution)/shard_map/all_gather | solution.py:99
  15.2 8.5 %collective-permute-start.3 = (bf16[384,256]{1,0:T(8,128)(2,1)S(1)}, bf16[384,256]{1,0:T(8,128)(2,1)S(1)}, u32[]{:S(2)}, u32[]{:S(2)}) collective-permute-start(bf16[384,256]{1,0:T(8,128)(2,1)S(1)} %pad_maximum_fusion.3.rest_0_), channel_id=1, source_target_pairs={{0,8},{1,9},{2,10},{3,11},{4,12},{5,13},{6,14},{7,15},{8,0},{9,1},... | collective-permute-start | bytes 589832 | tf_op jit(solution)/shard_map/ppermute | solution.py:27
  18.3 6.8 %collective-permute-start.1 = (bf16[384,256]{1,0:T(8,128)(2,1)S(1)}, bf16[384,256]{1,0:T(8,128)(2,1)S(1)}, u32[]{:S(2)}, u32[]{:S(2)}) collective-permute-start(bf16[384,256]{1,0:T(8,128)(2,1)S(1)} %pad_maximum_fusion.3.rest_0_), channel_id=1, source_target_pairs={{0,2},{1,3},{2,4},{3,5},{4,6},{5,7},{6,0},{7,1},{8,10},{9,11},{10,... | collective-permute-start | bytes 589832 | tf_op jit(solution)/shard_map/ppermute | solution.py:27
  21.0 7.4 %collective-permute-start.8 = (bf16[384,256]{1,0:T(8,128)(2,1)S(1)}, bf16[384,256]{1,0:T(8,128)(2,1)S(1)}, u32[]{:S(2)}, u32[]{:S(2)}) collective-permute-start(bf16[384,256]{1,0:T(8,128)(2,1)S(1)} %pad_maximum_fusion.3.rest_0_), channel_id=1, source_target_pairs={{0,1},{1,0},{2,3},{3,2},{4,5},{5,4},{6,7},{7,6},{8,9},{9,8},{10,11... | collective-permute-start | bytes 589832 | tf_op jit(solution)/shard_map/ppermute | solution.py:27
  24.9 7.7 %collective-permute-start.5 = (bf16[384,256]{1,0:T(8,128)(2,1)S(1)}, bf16[384,256]{1,0:T(8,128)(2,1)S(1)}, u32[]{:S(2)}, u32[]{:S(2)}) collective-permute-start(bf16[384,256]{1,0:T(8,128)(2,1)S(1)} %collective-permute-done.3.rest_3_), channel_id=1, source_target_pairs={{0,2},{1,3},{2,4},{3,5},{4,6},{5,7},{6,0},{7,1},{8,10},{9,11},{10,... | collective-permute-start | bytes 589832 | tf_op jit(solution)/shard_map/ppermute | solution.py:27
  25.1 10.4 %collective-permute-start.4 = (bf16[384,256]{1,0:T(8,128)(2,1)S(1)}, bf16[384,256]{1,0:T(8,128)(2,1)S(1)}, u32[]{:S(2)}, u32[]{:S(2)}) collective-permute-start(bf16[384,256]{1,0:T(8,128)(2,1)S(1)} %collective-permute-done.1.rest_1_), channel_id=1, source_target_pairs={{0,2},{1,3},{2,4},{3,5},{4,6},{5,7},{6,0},{7,1},{8,10},{9,11},{10,... | collective-permute-start | bytes 589832 | tf_op jit(solution)/shard_map/ppermute | solution.py:27
  25.2 12.5 %collective-permute-start.11 = (bf16[384,256]{1,0:T(8,128)(2,1)S(1)}, bf16[384,256]{1,0:T(8,128)(2,1)S(1)}, u32[]{:S(2)}, u32[]{:S(2)}) collective-permute-start(bf16[384,256]{1,0:T(8,128)(2,1)S(1)} %collective-permute-done.3.rest_3_), channel_id=1, source_target_pairs={{0,1},{1,0},{2,3},{3,2},{4,5},{5,4},{6,7},{7,6},{8,9},{9,8},{10,11... | collective-permute-start | bytes 589832 | tf_op jit(solution)/shard_map/ppermute | solution.py:27
  28.4 9.4 %collective-permute-start.9 = (bf16[384,256]{1,0:T(8,128)(2,1)S(1)}, bf16[384,256]{1,0:T(8,128)(2,1)S(1)}, u32[]{:S(2)}, u32[]{:S(2)}) collective-permute-start(bf16[384,256]{1,0:T(8,128)(2,1)S(1)} %collective-permute-done.1.rest_1_), channel_id=1, source_target_pairs={{0,1},{1,0},{2,3},{3,2},{4,5},{5,4},{6,7},{7,6},{8,9},{9,8},{10,11... | collective-permute-start | bytes 589832 | tf_op jit(solution)/shard_map/ppermute | solution.py:27
  29.2 9.0 %collective-permute-start.7 = (bf16[384,256]{1,0:T(8,128)(2,1)S(1)}, bf16[384,256]{1,0:T(8,128)(2,1)S(1)}, u32[]{:S(2)}, u32[]{:S(2)}) collective-permute-start(bf16[384,256]{1,0:T(8,128)(2,1)S(1)} %collective-permute-done.6.rest_6_), channel_id=1, source_target_pairs={{0,6},{1,7},{2,0},{3,1},{4,2},{5,3},{6,4},{7,5},{8,14},{9,15},{10,... | collective-permute-start | bytes 589832 | tf_op jit(solution)/shard_map/ppermute | solution.py:27
  32.6 6.3 %collective-permute-start.10 = (bf16[384,256]{1,0:T(8,128)(2,1)S(1)}, bf16[384,256]{1,0:T(8,128)(2,1)S(1)}, u32[]{:S(2)}, u32[]{:S(2)}) collective-permute-start(bf16[384,256]{1,0:T(8,128)(2,1)S(1)} %collective-permute-done.2.rest_2_), channel_id=1, source_target_pairs={{0,1},{1,0},{2,3},{3,2},{4,5},{5,4},{6,7},{7,6},{8,9},{9,8},{10,11... | collective-permute-start | bytes 589832 | tf_op jit(solution)/shard_map/ppermute | solution.py:27
  39.0 10.6 %collective-permute-start.17 = (bf16[384,128]{1,0:T(8,128)(2,1)S(1)}, bf16[384,128]{1,0:T(8,128)(2,1)S(1)}, u32[]{:S(2)}, u32[]{:S(2)}) collective-permute-start(bf16[384,128]{1,0:T(8,128)(2,1)S(1)} %multiply_convert_fusion), channel_id=1, source_target_pairs={{0,16},{16,0},{32,48},{48,32},{64,80},{80,64},{96,112},{112,96},{1... | collective-permute-start | bytes 294920 | tf_op jit(solution)/shard_map/ppermute | solution.py:27
  110.5 12.0 %collective-permute-start.18 = (bf16[16,128,128]{2,1,0:T(8,128)(2,1)S(1)}, bf16[16,128,128]{2,1,0:T(8,128)(2,1)S(1)}, u32[]{:S(2)}, u32[]{:S(2)}) collective-permute-start(bf16[16,128,128]{2,1,0:T(8,128)(2,1)S(1)} %all_to_all.21.rest_0_), channel_id=1, source_target_pairs={{0,2},{1,3},{2,4},{3,5},{4,6},{5,7},{6,0},{7,1},{8,10},{9,11},{10,... | collective-permute-start | bytes 1572872 | tf_op jit(solution)/shard_map/ppermute | solution.py:27
  110.9 11.7 %collective-permute-start.19 = (bf16[16,128,128]{2,1,0:T(8,128)(2,1)S(1)}, bf16[16,128,128]{2,1,0:T(8,128)(2,1)S(1)}, u32[]{:S(2)}, u32[]{:S(2)}) collective-permute-start(bf16[16,128,128]{2,1,0:T(8,128)(2,1)S(1)} %all_to_all.21.rest_0_), channel_id=1, source_target_pairs={{0,6},{1,7},{2,0},{3,1},{4,2},{5,3},{6,4},{7,5},{8,14},{9,15},{10,... | collective-permute-start | bytes 1572872 | tf_op jit(solution)/shard_map/ppermute | solution.py:27
  113.1 12.2 %collective-permute-start.20 = (bf16[16,128,128]{2,1,0:T(8,128)(2,1)S(1)}, bf16[16,128,128]{2,1,0:T(8,128)(2,1)S(1)}, u32[]{:S(2)}, u32[]{:S(2)}) collective-permute-start(bf16[16,128,128]{2,1,0:T(8,128)(2,1)S(1)} %all_to_all.21.rest_0_), channel_id=1, source_target_pairs={{0,24},{1,25},{2,26},{3,27},{4,28},{5,29},{6,30},{7,31},{8,16},{9,... | collective-permute-start | bytes 1572872 | tf_op jit(solution)/shard_map/ppermute | solution.py:40
  113.7 11.7 %collective-permute-start.21 = (bf16[16,128,128]{2,1,0:T(8,128)(2,1)S(1)}, bf16[16,128,128]{2,1,0:T(8,128)(2,1)S(1)}, u32[]{:S(2)}, u32[]{:S(2)}) collective-permute-start(bf16[16,128,128]{2,1,0:T(8,128)(2,1)S(1)} %all_to_all.21.rest_0_), channel_id=1, source_target_pairs={{0,1},{1,0},{2,3},{3,2},{4,5},{5,4},{6,7},{7,6},{8,9},{9,8},{10,11... | collective-permute-start | bytes 1572872 | tf_op jit(solution)/shard_map/ppermute | solution.py:27
  122.5 7.6 %collective-permute-start.22 = (bf16[8,128,128]{2,1,0:T(8,128)(2,1)S(1)}, bf16[8,128,128]{2,1,0:T(8,128)(2,1)S(1)}, u32[]{:S(2)}, u32[]{:S(2)}) collective-permute-start(bf16[8,128,128]{2,1,0:T(8,128)(2,1)S(1)} %slice.22), channel_id=1, source_target_pairs={{0,2},{1,3},{2,4},{3,5},{4,6},{5,7},{6,0},{7,1},{8,10},{9,11},{10,... | collective-permute-start | bytes 786440 | tf_op jit(solution)/shard_map/ppermute | solution.py:27
  122.7 7.4 %collective-permute-start.23 = (bf16[8,128,128]{2,1,0:T(8,128)(2,1)S(1)}, bf16[8,128,128]{2,1,0:T(8,128)(2,1)}, u32[]{:S(2)}, u32[]{:S(2)}) collective-permute-start(bf16[8,128,128]{2,1,0:T(8,128)(2,1)S(1)} %slice.23), channel_id=1, source_target_pairs={{0,6},{1,7},{2,0},{3,1},{4,2},{5,3},{6,4},{7,5},{8,14},{9,15},{10,... | collective-permute-start | bytes 786440 | tf_op jit(solution)/shard_map/ppermute | solution.py:27
  125.4 7.4 %collective-permute-start.26 = (bf16[16,128,128]{2,1,0:T(8,128)(2,1)S(1)}, bf16[16,128,128]{2,1,0:T(8,128)(2,1)S(1)}, u32[]{:S(2)}, u32[]{:S(2)}) collective-permute-start(bf16[16,128,128]{2,1,0:T(8,128)(2,1)S(1)} %collective-permute-done.20.rest_3_), channel_id=1, source_target_pairs={{0,1},{1,0},{2,3},{3,2},{4,5},{5,4},{6,7},{7,6},{8,9},{9,8},{10,11... | collective-permute-start | bytes 1572872 | tf_op jit(solution)/shard_map/ppermute | solution.py:27
  130.1 11.1 %collective-permute-start.27 = (bf16[16,128,128]{2,1,0:T(8,128)(2,1)S(1)}, bf16[16,128,128]{2,1,0:T(8,128)(2,1)}, u32[]{:S(2)}, u32[]{:S(2)}) collective-permute-start(bf16[16,128,128]{2,1,0:T(8,128)(2,1)S(1)} %collective-permute-done.20.rest_3_), channel_id=1, source_target_pairs={{0,2},{1,3},{2,4},{3,5},{4,6},{5,7},{6,0},{7,1},{8,10},{9,11},{10,... | collective-permute-start | bytes 1572872 | tf_op jit(solution)/shard_map/ppermute | solution.py:27
  130.1 15.6 %collective-permute-start.28 = (bf16[16,128,128]{2,1,0:T(8,128)(2,1)S(1)}, bf16[16,128,128]{2,1,0:T(8,128)(2,1)}, u32[]{:S(2)}, u32[]{:S(2)}) collective-permute-start(bf16[16,128,128]{2,1,0:T(8,128)(2,1)S(1)} %collective-permute-done.20.rest_3_), channel_id=1, source_target_pairs={{0,6},{1,7},{2,0},{3,1},{4,2},{5,3},{6,4},{7,5},{8,14},{9,15},{10,... | collective-permute-start | bytes 1572872 | tf_op jit(solution)/shard_map/ppermute | solution.py:27
  132.8 12.9 %collective-permute-start.29 = (bf16[8,128,128]{2,1,0:T(8,128)(2,1)S(1)}, bf16[8,128,128]{2,1,0:T(8,128)(2,1)S(1)}, u32[]{:S(2)}, u32[]{:S(2)}) collective-permute-start(bf16[8,128,128]{2,1,0:T(8,128)(2,1)S(1)} %collective-permute-done.22.rest_4_), channel_id=1, source_target_pairs={{0,24},{1,25},{2,26},{3,27},{4,28},{5,29},{6,30},{7,31},{8,16},{9,... | collective-permute-start | bytes 786440 | tf_op jit(solution)/shard_map/ppermute | solution.py:40
  133.5 12.8 %collective-permute-start.30 = (bf16[8,128,128]{2,1,0:T(8,128)(2,1)}, bf16[8,128,128]{2,1,0:T(8,128)(2,1)}, u32[]{:S(2)}, u32[]{:S(2)}) collective-permute-start(bf16[8,128,128]{2,1,0:T(8,128)(2,1)} %collective-permute-done.23.rest_5_), channel_id=1, source_target_pairs={{0,24},{1,25},{2,26},{3,27},{4,28},{5,29},{6,30},{7,31},{8,16},{9,... | collective-permute-start | bytes 786440 | tf_op jit(solution)/shard_map/ppermute | solution.py:40
  135.6 13.0 %collective-permute-start.31 = (bf16[8,128,128]{2,1,0:T(8,128)(2,1)S(1)}, bf16[8,128,128]{2,1,0:T(8,128)(2,1)S(1)}, u32[]{:S(2)}, u32[]{:S(2)}) collective-permute-start(bf16[8,128,128]{2,1,0:T(8,128)(2,1)S(1)} %collective-permute-done.22.rest_4_), channel_id=1, source_target_pairs={{0,1},{1,0},{2,3},{3,2},{4,5},{5,4},{6,7},{7,6},{8,9},{9,8},{10,11... | collective-permute-start | bytes 786440 | tf_op jit(solution)/shard_map/ppermute | solution.py:27
  141.2 18.8 %collective-permute-start.33 = (bf16[16,128,128]{2,1,0:T(8,128)(2,1)}, bf16[16,128,128]{2,1,0:T(8,128)(2,1)}, u32[]{:S(2)}, u32[]{:S(2)}) collective-permute-start(bf16[16,128,128]{2,1,0:T(8,128)(2,1)} %collective-permute-done.27.rest_6_), channel_id=1, source_target_pairs={{0,1},{1,0},{2,3},{3,2},{4,5},{5,4},{6,7},{7,6},{8,9},{9,8},{10,11... | collective-permute-start | bytes 1572872 | tf_op jit(solution)/shard_map/ppermute | solution.py:27
  145.7 14.3 %collective-permute-start.34 = (bf16[16,128,128]{2,1,0:T(8,128)(2,1)}, bf16[16,128,128]{2,1,0:T(8,128)(2,1)}, u32[]{:S(2)}, u32[]{:S(2)}) collective-permute-start(bf16[16,128,128]{2,1,0:T(8,128)(2,1)} %collective-permute-done.28.rest_7_), channel_id=1, source_target_pairs={{0,1},{1,0},{2,3},{3,2},{4,5},{5,4},{6,7},{7,6},{8,9},{9,8},{10,11... | collective-permute-start | bytes 1572872 | tf_op jit(solution)/shard_map/ppermute | solution.py:27
  145.8 14.2 %collective-permute-start.32 = (bf16[8,128,128]{2,1,0:T(8,128)(2,1)}, bf16[8,128,128]{2,1,0:T(8,128)(2,1)}, u32[]{:S(2)}, u32[]{:S(2)}) collective-permute-start(bf16[8,128,128]{2,1,0:T(8,128)(2,1)} %collective-permute-done.23.rest_5_), channel_id=1, source_target_pairs={{0,1},{1,0},{2,3},{3,2},{4,5},{5,4},{6,7},{7,6},{8,9},{9,8},{10,11... | collective-permute-start | bytes 786440 | tf_op jit(solution)/shard_map/ppermute | solution.py:27
  146.3 13.7 %collective-permute-start.35 = (bf16[8,128,128]{2,1,0:T(8,128)(2,1)S(1)}, bf16[8,128,128]{2,1,0:T(8,128)(2,1)}, u32[]{:S(2)}, u32[]{:S(2)}) collective-permute-start(bf16[8,128,128]{2,1,0:T(8,128)(2,1)S(1)} %collective-permute-done.29.rest_8_), channel_id=1, source_target_pairs={{0,1},{1,0},{2,3},{3,2},{4,5},{5,4},{6,7},{7,6},{8,9},{9,8},{10,11... | collective-permute-start | bytes 786440 | tf_op jit(solution)/shard_map/ppermute | solution.py:27
  149.3 10.7 %collective-permute-start.36 = (bf16[8,128,128]{2,1,0:T(8,128)(2,1)}, bf16[8,128,128]{2,1,0:T(8,128)(2,1)}, u32[]{:S(2)}, u32[]{:S(2)}) collective-permute-start(bf16[8,128,128]{2,1,0:T(8,128)(2,1)} %collective-permute-done.30.rest_9_), channel_id=1, source_target_pairs={{0,1},{1,0},{2,3},{3,2},{4,5},{5,4},{6,7},{7,6},{8,9},{9,8},{10,11... | collective-permute-start | bytes 786440 | tf_op jit(solution)/shard_map/ppermute | solution.py:27
  183.3 17.7 %collective-permute-start.38 = (bf16[8,256,384]{2,1,0:T(8,128)(2,1)}, bf16[8,256,384]{2,1,0:T(8,128)(2,1)}, u32[]{:S(2)}, u32[]{:S(2)}) collective-permute-start(bf16[8,256,384]{2,1,0:T(8,128)(2,1)} %get-tuple-element.38), channel_id=1, source_target_pairs={{0,1},{1,0},{2,3},{3,2},{4,5},{5,4},{6,7},{7,6},{8,9},{9,8},{10,11... | collective-permute-start | bytes 4718600 | tf_op jit(solution)/shard_map/ppermute | solution.py:27
  185.7 15.2 %all-to-all-start.2 = ((bf16[8,256,128]{2,1,0:T(8,128)(2,1)}), bf16[8,256,128]{2,1,0:T(8,128)(2,1)S(1)}, u32[]{:S(2)}, u32[]{:S(2)}) async-start(bf16[8,256,128]{2,1,0:T(8,128)(2,1)} %add_convert_fusion.1), calls=%async_computation.2 | async-start | bytes 1048576 | tf_op jit(solution)/shard_map/all_to_all | solution.py:109
  189.2 46.7 %all-gather.11.cloned.1.call-start = ((), (), s32[]{:S(2)}) async-start(), calls=%async_computation.6 | async-start | bytes 1769472 | tf_op jit(solution)/shard_map/all_gather | solution.py:99
  (45 other events, 467.8 us)
Sparse Core Ops, SparseCore 0:
  13.5 40.1 all-gather.6
  56.4 60.0 all-gather.8
  192.4 34.3 all-gather.10

commit v3 on v2

--- a/solution.py
+++ b/solution.py
@@ -52,7 +52,7 @@
     return near + [swap(piece) for piece in near]
 
 
-def gather_table(slab):
+def gather_table(slab, norm):
     half = slab.shape[0] // 2
     slab_swap = swap(slab)
     left = hop(slab, "fsdp", 2, 4, 1)
@@ -60,7 +60,7 @@
     other = across(slab)
     far_a = hop(left[:half], "fsdp", 2, 4, 1)
     far_b = hop(right[half:], "fsdp", 2, 4, -1)
-    other, slab_swap = lax.optimization_barrier((other, slab_swap))
+    other, slab_swap, norm = lax.optimization_barrier((other, slab_swap, norm))
     other_left = hop(other, "fsdp", 2, 4, 1)
     other_right = hop(other, "fsdp", 2, 4, -1)
     early = [swap(left), swap(right), swap(other)]
@@ -68,7 +68,7 @@
     other_far = [across(far_a), across(far_b)]
     near = [slab, left, right, other, far_a, far_b, other_left, other_right] + other_far
     late = [swap(piece) for piece in near[4:]]
-    return near + [slab_swap] + early + late
+    return near + [slab_swap] + early + late, norm
 
 
 def places():
@@ -79,6 +79,7 @@
     for c in (core, 1 - core):
         for i, o in steps:
             found.append(jnp.where(i == 0, y, 1 - y) * 8 + ((x + o) % 4) * 2 + c)
+    found += [lax.axis_index("section"), core]
     return jnp.stack(found).astype(jnp.int32)
 
 
@@ -204,10 +205,10 @@
                 lift_ref[k] += back[:, cut[k]]
         mean = jnp.sum(grad * act_ref[s] * inverse * inverse, axis=1, keepdims=True) * scale
         shrink = shrink + mean
-    here = pl.ds(pl.multiple_of(s_ref[0] * rank, rank), rank)
+    here = pl.ds(pl.multiple_of(s_ref[16] * rank, rank), rank)
     p_t, q_t, sq_t = p_ref[:, here].T, q_ref[:, here].T, sq_ref[:, here].T
     both = jnp.concatenate([p_t, -sq_t], axis=0)
-    even_core = s_ref[1] == 0
+    even_core = s_ref[17] == 0
     for i in range(layers // 2):
         span = slice(2 * rank * i, 2 * rank * (i + 1))
         before = dot(both, q_ref[:, span], NN)
@@ -216,9 +217,9 @@
         found = []
         for k in range(2):
             j, some = 2 * i + k, slice(rank * k, rank * (k + 1))
-            later = jnp.where(j == s_ref[0], 0.0, after[:, some])
+            later = jnp.where(j == s_ref[16], 0.0, after[:, some])
             later = jnp.concatenate([later, scaled[:, some]], axis=0)
-            found.append(jnp.where(j < s_ref[0], before[:, some], later).astype(BF16))
+            found.append(jnp.where(j < s_ref[16], before[:, some], later).astype(BF16))
         keep_ref[i] = jnp.where(even_core, found[0], found[1])
         send_ref[i] = jnp.where(even_core, found[1], found[0])
 
@@ -235,7 +236,7 @@
         send_part[i] = jnp.where(even_core, odd, even)
 
 
-def chain_call(here, place, projected, norm, x, y, table):
+def chain_call(place, projected, norm, x, y, table):
     sections, tokens, wide = projected.shape
     rank, width, piece = wide // 3, x.shape[1], x.shape[1] // 16
     smem = pl.BlockSpec(memory_space=pltpu.SMEM)
@@ -264,7 +265,7 @@
             flops=2 * 10**10, bytes_accessed=12 * MIB, transcendentals=10**6
         ),
         name="chain",
-    )(here, place, projected, norm, x, y, *table)
+    )(place, place, projected, norm, x, y, *table)
 
 
 def finish(s_ref, part_ref, mate_ref, up_hbm, down_hbm, own_ref, gain_ref, *rest):
@@ -279,15 +280,15 @@
     held = part_ref[0, :, :piece].astype(F32)
     for k in range(1, part_ref.shape[0]):
         held = held + part_ref[k, :, :piece].astype(F32)
-    first = s_ref[1] == 0
+    first = s_ref[17] == 0
     zero = jnp.zeros((rank, rank), BF16)
     masked, after = [], []
     for j in range(layers):
         ours, theirs = part_ref[j // 2, :, piece:], mate_ref[j // 2]
         sums = jnp.where(first == (j % 2 == 0), ours, theirs)
-        before = jnp.where(j < s_ref[0], sums[:rank], zero)
+        before = jnp.where(j < s_ref[16], sums[:rank], zero)
         masked.append(jnp.concatenate([before, sums[rank:]], axis=0))
-        after.append(jnp.where(j > s_ref[0], sums[:rank], zero))
+        after.append(jnp.where(j > s_ref[16], sums[:rank], zero))
     for copy in copies:
         copy.wait()
     held = held + dot(jnp.concatenate(masked, axis=1), up_ref[...].reshape(-1, piece), NN)
@@ -296,14 +297,13 @@
         held_up = held_up + dot(after[k], down_ref[k], NT)
     up_out[...] = held_up
     held_down = held[:rank]
-    down_out[...] = (held_down * gain_ref[...]).T
+    down_out[...] = (held_down * gain_ref[...].astype(F32)).T
     gain_out[...] = jnp.sum(own_ref[...].astype(F32).T * held_down, axis=0, keepdims=True)
 
 
 def on_device(inputs, out_grad, down_proj, gain, up_proj):
     sections, groups = lax.axis_size("section"), lax.axis_size("fsdp")
     s = lax.axis_index("section")
-    here = jnp.stack([s, lax.axis_index("fsdp") % 2]).astype(jnp.int32)
     place = places()
     width = inputs.shape[2]
     x = inputs.reshape(-1, width)
@@ -350,10 +350,10 @@
     chosen = lax.all_to_all(chosen, "fsdp", 0, 0, tiled=True)
     block = jnp.sum(chosen.astype(F32), axis=0).astype(BF16)
     block, late = lax.optimization_barrier((block, late))
-    table = gather_table(gather_section(block))
+    table, norm = gather_table(gather_section(block), norm)
     down_all = along_z(late)
 
-    cross, cross_out, part, part_out = chain_call(here, place, projected, norm, x, y, table)
+    cross, cross_out, part, part_out = chain_call(place, projected, norm, x, y, table)
     cross_got, part_out = lax.optimization_barrier((swap(cross_out), part_out))
     cross = among_chips(add(cross, cross_got))
     part_got = swap(part_out)
@@ -379,7 +379,7 @@
         ],
         compiler_params=pltpu.CompilerParams(vmem_limit_bytes=57 * MIB),
         name="finish",
-    )(here, part, mate, up_all, down_all, down, gain_row[None])
+    )(place, part, mate, up_all, down_all, down, gain)
     return (grad_down[None], grad_gain, grad_up[None])
 
 

time: 254 us -> 257 us (1.012)
  waiting for transfers between devices: 28.1 us -> 37.3 us
  starting transfers between devices: 72.5 us -> 65.1 us
    ppermute x37, waiting for transfers between devices: 16.3 us -> 25.6 us  [hop(): return lax.ppermute(block, axis, route)]
    ppermute x37, starting transfers between devices: 65.5 us -> 57.2 us  [hop(): return lax.ppermute(block, axis, route)]
where the time goes in v3:
time: 257 us; the launch traced here: 252 us
  blocking collectives  80.5 us (31%)
  starting transfers between devices  65.1 us (25%)
  waiting for transfers between devices  37.3 us (15%)
  Pallas kernels  34.5 us (13%)
  between operations  14.4 us (6%)
  other arithmetic  10.8 us (4%)
  local copies, waits for them, and re-layouts  7.51 us (3%)
    ppermute x37, starting transfers between devices, hop(): return lax.ppermute(block, axis, route)  57.2 us
    all_to_all x1, blocking collectives, among_chips(): lax.all_to_all(chunks, 'fsdp', 0, 0, tiled=True, axis_index_groups=chips)  30.1 us
    all_to_all x1, blocking collectives, gather_section(): lax.all_to_all(jnp.broadcast_to(block[None], (16,) + block.shape), 'secti...  30 us
    ppermute x37, waiting for transfers between devices, hop(): return lax.ppermute(block, axis, route)  25.6 us
    pallas_call x1, Pallas kernels, chain_call(): pl.pallas_call(functools.partial(chain, width), out_shape=(jax.ShapeDtype...  20.9 us
    all_to_all x1, blocking collectives, on_device(): chosen = lax.all_to_all(chosen, 'fsdp', 0, 0, tiled=True)  20.4 us
    all_to_all x1, waiting for transfers between devices, among_chips(): lax.all_to_all(chunks, 'fsdp', 0, 0, tiled=True, axis_index_groups=chips)  11 us
    pallas_call x1, Pallas kernels, on_device(): pl.pallas_call(project, out_shape=jax.ShapeDtypeStruct((tokens, 3 * rank)...  7.96 us
  transfers between devices with their start and end apart: 44, of which 9 were waited for; matrix products, arithmetic and copies ran while one was open for 6% of the time, Pallas kernels for 3%

profile of v3, /device:TPU:1, one launch (start us, length us, event | category | flops | bytes accessed | tf_op | source)
XLA Modules:
  0.0 252.3 jit_solution(14372159628587468639)
XLA Ops:
  8.2 2.2 collective-permute-start
  10.4 2.0 collective-permute-done
  15.2 3.2 %collective-permute-start.3 = (bf16[384,256]{1,0:T(8,128)(2,1)S(1)}, bf16[384,256]{1,0:T(8,128)(2,1)S(1)}, u32[]{:S(2)}, u32[]{:S(2)}) collective-permute-start(bf16[384,256]{1,0:T(8,128)(2,1)S(1)} %pad_maximum_fusion.3.rest_0_), channel_id=1, source_target_pairs={{0,8},{1,9},{2,10},{3,11},{4,12},{5,13},{6,14},{7,15},{8,0},{9,1},... | collective-permute-start | bytes 589832 | tf_op jit(solution)/shard_map/ppermute | solution.py:27
  21.0 2.7 %collective-permute-start.8 = (bf16[384,256]{1,0:T(8,128)(2,1)S(1)}, bf16[384,256]{1,0:T(8,128)(2,1)S(1)}, u32[]{:S(2)}, u32[]{:S(2)}) collective-permute-start(bf16[384,256]{1,0:T(8,128)(2,1)S(1)} %pad_maximum_fusion.3.rest_0_), channel_id=1, source_target_pairs={{0,1},{1,0},{2,3},{3,2},{4,5},{5,4},{6,7},{7,6},{8,9},{9,8},{10,11... | collective-permute-start | bytes 589832 | tf_op jit(solution)/shard_map/ppermute | solution.py:27
  25.2 3.1 %collective-permute-start.11 = (bf16[384,256]{1,0:T(8,128)(2,1)S(1)}, bf16[384,256]{1,0:T(8,128)(2,1)S(1)}, u32[]{:S(2)}, u32[]{:S(2)}) collective-permute-start(bf16[384,256]{1,0:T(8,128)(2,1)S(1)} %collective-permute-done.3.rest_3_), channel_id=1, source_target_pairs={{0,1},{1,0},{2,3},{3,2},{4,5},{5,4},{6,7},{7,6},{8,9},{9,8},{10,11... | collective-permute-start | bytes 589832 | tf_op jit(solution)/shard_map/ppermute | solution.py:27
  29.2 3.4 %collective-permute-start.7 = (bf16[384,256]{1,0:T(8,128)(2,1)S(1)}, bf16[384,256]{1,0:T(8,128)(2,1)S(1)}, u32[]{:S(2)}, u32[]{:S(2)}) collective-permute-start(bf16[384,256]{1,0:T(8,128)(2,1)S(1)} %collective-permute-done.6.rest_6_), channel_id=1, source_target_pairs={{0,6},{1,7},{2,0},{3,1},{4,2},{5,3},{6,4},{7,5},{8,14},{9,15},{10,... | collective-permute-start | bytes 589832 | tf_op jit(solution)/shard_map/ppermute | solution.py:27
  32.6 2.9 %collective-permute-start.10 = (bf16[384,256]{1,0:T(8,128)(2,1)S(1)}, bf16[384,256]{1,0:T(8,128)(2,1)S(1)}, u32[]{:S(2)}, u32[]{:S(2)}) collective-permute-start(bf16[384,256]{1,0:T(8,128)(2,1)S(1)} %collective-permute-done.2.rest_2_), channel_id=1, source_target_pairs={{0,1},{1,0},{2,3},{3,2},{4,5},{5,4},{6,7},{7,6},{8,9},{9,8},{10,11... | collective-permute-start | bytes 589832 | tf_op jit(solution)/shard_map/ppermute | solution.py:27
  35.6 2.1 collective-permute-start.14
  40.6 8.0 %project.1 = bf16[256,384]{1,0:T(8,128)(2,1)} custom-call(s32[18]{0:T(128)} %stack.102.place_ref.s_ref, bf16[256,6144]{1,0:T(8,128)(2,1)} %bitcast.47, bf16[256,6144]{1,0:T(8,128)(2,1)} %bitcast.54, bf16[384,256]{1,0:T(8,128)(2,1)} %copy-done.5, bf16[384,256]{1,0:T(8,128)(2,1)} %copy-done.16, bf16[384,256]{1,0:T(8,128)(2,1)} %copy-done.17, ...), custom_call_target="tpu_custom_call" | custom-call | flops 8000000000 | bytes 9437184 | tf_op jit(solution)/shard_map/project/pallas_call | solution.py:323
  50.5 4.1 %collective-permute-done.16 = bf16[256,384]{1,0:T(8,128)(2,1)S(1)} collective-permute-done((bf16[256,384]{1,0:T(8,128)(2,1)}, bf16[256,384]{1,0:T(8,128)(2,1)S(1)}, u32[]{:S(2)}, u32[]{:S(2)}) %collective-permute-start.16) | collective-permute-done | bytes 196640 | tf_op jit(solution)/shard_map/ppermute | solution.py:27
  56.4 2.1 fusion.5
  59.0 20.4 %all_to_all.20 = bf16[16,128,128]{2,1,0:T(8,128)(2,1)} all-to-all(bf16[16,128,128]{2,1,0:T(8,128)(2,1)S(1)} %bitcast.49), channel_id=1, replica_groups=mesh['section'=16,'fsdp'=16] {'fsdp'}, dimensions={0} | all-to-all | bytes 1048576 | tf_op jit(solution)/shard_map/all_to_all | solution.py:350
  80.7 30.0 %all_to_all.21.rest_0_ = bf16[16,128,128]{2,1,0:T(8,128)(2,1)} all-to-all(bf16[16,128,128]{2,1,0:T(8,128)(2,1)S(1)} %broadcast_in_dim.31), channel_id=1, replica_groups=mesh['section'=16,'fsdp'=16] {'section'}, dimensions={0} | all-to-all | bytes 1048576 | tf_op jit(solution)/shard_map/all_to_all | solution.py:87
  111.1 2.2 collective-permute-start.21
  113.9 2.7 %collective-permute-start.19 = (bf16[16,128,128]{2,1,0:T(8,128)(2,1)}, bf16[16,128,128]{2,1,0:T(8,128)(2,1)}, u32[]{:S(2)}, u32[]{:S(2)}) collective-permute-start(bf16[16,128,128]{2,1,0:T(8,128)(2,1)} %all_to_all.21.rest_0_), channel_id=1, source_target_pairs={{0,1},{1,0},{2,3},{3,2},{4,5},{5,4},{6,7},{7,6},{8,9},{9,8},{10,11... | collective-permute-start | bytes 1572872 | tf_op jit(solution)/shard_map/ppermute | solution.py:27
  116.6 6.4 %collective-permute-done.20.rest_1_ = bf16[16,128,128]{2,1,0:T(8,128)(2,1)S(1)} collective-permute-done((bf16[16,128,128]{2,1,0:T(8,128)(2,1)}, bf16[16,128,128]{2,1,0:T(8,128)(2,1)S(1)}, u32[]{:S(2)}, u32[]{:S(2)}) %collective-permute-start.20) | collective-permute-done | bytes 524320 | tf_op jit(solution)/shard_map/ppermute | solution.py:27
  125.3 2.6 %collective-permute-start.23 = (bf16[8,128,128]{2,1,0:T(8,128)(2,1)}, bf16[8,128,128]{2,1,0:T(8,128)(2,1)}, u32[]{:S(2)}, u32[]{:S(2)}) collective-permute-start(bf16[8,128,128]{2,1,0:T(8,128)(2,1)} %slice.23), channel_id=1, source_target_pairs={{0,6},{1,7},{2,0},{3,1},{4,2},{5,3},{6,4},{7,5},{8,14},{9,15},{10,... | collective-permute-start | bytes 786440 | tf_op jit(solution)/shard_map/ppermute | solution.py:27
  128.8 3.4 %collective-permute-start.26 = (bf16[16,128,128]{2,1,0:T(8,128)(2,1)}, bf16[16,128,128]{2,1,0:T(8,128)(2,1)S(1)}, u32[]{:S(2)}, u32[]{:S(2)}) collective-permute-start(bf16[16,128,128]{2,1,0:T(8,128)(2,1)} %collective-permute-done.18.rest_3_), channel_id=1, source_target_pairs={{0,1},{1,0},{2,3},{3,2},{4,5},{5,4},{6,7},{7,6},{8,9},{9,8},{10,11... | collective-permute-start | bytes 1572872 | tf_op jit(solution)/shard_map/ppermute | solution.py:27
  132.7 2.7 %collective-permute-start.28 = (bf16[16,128,128]{2,1,0:T(8,128)(2,1)}, bf16[16,128,128]{2,1,0:T(8,128)(2,1)S(1)}, u32[]{:S(2)}, u32[]{:S(2)}) collective-permute-start(bf16[16,128,128]{2,1,0:T(8,128)(2,1)} %collective-permute-done.18.rest_3_), channel_id=1, source_target_pairs={{0,6},{1,7},{2,0},{3,1},{4,2},{5,3},{6,4},{7,5},{8,14},{9,15},{10,... | collective-permute-start | bytes 1572872 | tf_op jit(solution)/shard_map/ppermute | solution.py:27
  136.1 2.1 collective-permute-start.30
  138.2 7.8 %collective-permute-done.27.rest_6_ = bf16[16,128,128]{2,1,0:T(8,128)(2,1)S(1)} collective-permute-done((bf16[16,128,128]{2,1,0:T(8,128)(2,1)}, bf16[16,128,128]{2,1,0:T(8,128)(2,1)S(1)}, u32[]{:S(2)}, u32[]{:S(2)}) %collective-permute-start.27) | collective-permute-done | bytes 524320 | tf_op jit(solution)/shard_map/ppermute | solution.py:27
  146.0 2.4 collective-permute-start.33
  149.1 2.3 collective-permute-start.35
  151.4 8.6 %collective-permute-start.36 = (bf16[8,128,128]{2,1,0:T(8,128)(2,1)}, bf16[8,128,128]{2,1,0:T(8,128)(2,1)}, u32[]{:S(2)}, u32[]{:S(2)}) collective-permute-start(bf16[8,128,128]{2,1,0:T(8,128)(2,1)} %collective-permute-done.30.rest_9_), channel_id=1, source_target_pairs={{0,1},{1,0},{2,3},{3,2},{4,5},{5,4},{6,7},{7,6},{8,9},{9,8},{10,11... | collective-permute-start | bytes 786440 | tf_op jit(solution)/shard_map/ppermute | solution.py:27
  161.8 20.9 %chain.1 = (bf16[8,256,128]{2,1,0:T(8,128)(2,1)}, bf16[8,256,128]{2,1,0:T(8,128)(2,1)}, bf16[8,256,384]{2,1,0:T(8,128)(2,1)}, bf16[8,256,384]{2,1,0:T(8,128)(2,1)}) custom-call(s32[18]{0:T(128)} %stack.102.place_ref.s_ref, s32[18]{0:T(128)} %stack.102.place_ref.s_ref, bf16[16,256,384]{2,1,0:T(8,128)(2,1)} %all-gather.9.cloned.1.call-done.a_hbm, ...), custom_call_target="tpu_custom_call" | custom-call | flops 20000000000 | bytes 12582912 | tf_op jit(solution)/shard_map/chain/pallas_call | solution.py:247
  182.9 2.0 collective-permute-done.37
  185.1 2.0 add_convert_fusion.1
  187.0 4.5 %all-to-all-start.2 = ((bf16[8,256,128]{2,1,0:T(8,128)(2,1)}), bf16[8,256,128]{2,1,0:T(8,128)(2,1)S(1)}, u32[]{:S(2)}, u32[]{:S(2)}) async-start(bf16[8,256,128]{2,1,0:T(8,128)(2,1)} %add_convert_fusion.1), calls=%async_computation.2 | async-start | bytes 1048576 | tf_op jit(solution)/shard_map/all_to_all | solution.py:110
  192.3 11.0 %all-to-all-done.2 = bf16[8,256,128]{2,1,0:T(8,128)(2,1)S(1)} async-done(((bf16[8,256,128]{2,1,0:T(8,128)(2,1)}), bf16[8,256,128]{2,1,0:T(8,128)(2,1)S(1)}, u32[]{:S(2)}, u32[]{:S(2)}) %all-to-all-start.2) | async-done | bytes 524320 | tf_op jit(solution)/shard_map/all_to_all | solution.py:110
  203.4 1.9 add_convert_fusion
  205.5 30.1 %all_to_all.22.part_ref = bf16[8,256,512]{2,1,0:T(8,128)(2,1)S(1)} all-to-all(bf16[8,256,512]{2,1,0:T(8,128)(2,1)S(1)} %pad_maximum_fusion), channel_id=1, replica_groups={{0,2,4,6,8,10,12,14},{1,3,5,7,9,11,13,15},{16,18,20,22,24,26,28,30},{17..., dimensions={0} | all-to-all | bytes 4194304 | tf_op jit(solution)/shard_map/all_to_all | solution.py:110
  239.9 5.7 %finish.1 = (f32[384,128]{1,0:T(8,128)}, f32[1,384]{1,0:T(1,128)}, f32[128,384]{1,0:T(8,128)}) custom-call(s32[18]{0:T(128)} %stack.102.place_ref.s_ref, bf16[8,256,512]{2,1,0:T(8,128)(2,1)} %copy-done, bf16[8,256,128]{2,1,0:T(8,128)(2,1)} %copy-done.4, bf16[16,128,384]{2,1,0:T(8,128)(2,1)} %all-gather.7.cloned.1.call-done.up_hbm, ...), custom_call_target="tpu_custom_call" | custom-call | tf_op jit(solution)/shard_map/finish/pallas_call | solution.py:366
  (153 shorter events, 30.5 us)
Async XLA Ops:
  7.2 49.2 %all-gather.7.cloned.1.call-start = ((), (), s32[]{:S(2)}) async-start(), calls=%async_computation.4 | async-start | bytes 1769472 | tf_op jit(solution)/shard_map/all_gather | solution.py:100
  13.4 148.4 %all-gather.9.cloned.1.call-start = ((), (), s32[]{:S(2)}) async-start(), calls=%async_computation.5 | async-start | bytes 3538944 | tf_op jit(solution)/shard_map/all_gather | solution.py:100
  15.2 8.5 %collective-permute-start.3 = (bf16[384,256]{1,0:T(8,128)(2,1)S(1)}, bf16[384,256]{1,0:T(8,128)(2,1)S(1)}, u32[]{:S(2)}, u32[]{:S(2)}) collective-permute-start(bf16[384,256]{1,0:T(8,128)(2,1)S(1)} %pad_maximum_fusion.3.rest_0_), channel_id=1, source_target_pairs={{0,8},{1,9},{2,10},{3,11},{4,12},{5,13},{6,14},{7,15},{8,0},{9,1},... | collective-permute-start | bytes 589832 | tf_op jit(solution)/shard_map/ppermute | solution.py:27
  18.3 6.8 %collective-permute-start.1 = (bf16[384,256]{1,0:T(8,128)(2,1)S(1)}, bf16[384,256]{1,0:T(8,128)(2,1)S(1)}, u32[]{:S(2)}, u32[]{:S(2)}) collective-permute-start(bf16[384,256]{1,0:T(8,128)(2,1)S(1)} %pad_maximum_fusion.3.rest_0_), channel_id=1, source_target_pairs={{0,2},{1,3},{2,4},{3,5},{4,6},{5,7},{6,0},{7,1},{8,10},{9,11},{10,... | collective-permute-start | bytes 589832 | tf_op jit(solution)/shard_map/ppermute | solution.py:27
  21.0 7.4 %collective-permute-start.8 = (bf16[384,256]{1,0:T(8,128)(2,1)S(1)}, bf16[384,256]{1,0:T(8,128)(2,1)S(1)}, u32[]{:S(2)}, u32[]{:S(2)}) collective-permute-start(bf16[384,256]{1,0:T(8,128)(2,1)S(1)} %pad_maximum_fusion.3.rest_0_), channel_id=1, source_target_pairs={{0,1},{1,0},{2,3},{3,2},{4,5},{5,4},{6,7},{7,6},{8,9},{9,8},{10,11... | collective-permute-start | bytes 589832 | tf_op jit(solution)/shard_map/ppermute | solution.py:27
  24.9 7.7 %collective-permute-start.5 = (bf16[384,256]{1,0:T(8,128)(2,1)S(1)}, bf16[384,256]{1,0:T(8,128)(2,1)S(1)}, u32[]{:S(2)}, u32[]{:S(2)}) collective-permute-start(bf16[384,256]{1,0:T(8,128)(2,1)S(1)} %collective-permute-done.3.rest_3_), channel_id=1, source_target_pairs={{0,2},{1,3},{2,4},{3,5},{4,6},{5,7},{6,0},{7,1},{8,10},{9,11},{10,... | collective-permute-start | bytes 589832 | tf_op jit(solution)/shard_map/ppermute | solution.py:27
  25.1 10.4 %collective-permute-start.4 = (bf16[384,256]{1,0:T(8,128)(2,1)S(1)}, bf16[384,256]{1,0:T(8,128)(2,1)S(1)}, u32[]{:S(2)}, u32[]{:S(2)}) collective-permute-start(bf16[384,256]{1,0:T(8,128)(2,1)S(1)} %collective-permute-done.1.rest_1_), channel_id=1, source_target_pairs={{0,2},{1,3},{2,4},{3,5},{4,6},{5,7},{6,0},{7,1},{8,10},{9,11},{10,... | collective-permute-start | bytes 589832 | tf_op jit(solution)/shard_map/ppermute | solution.py:27
  25.2 12.5 %collective-permute-start.11 = (bf16[384,256]{1,0:T(8,128)(2,1)S(1)}, bf16[384,256]{1,0:T(8,128)(2,1)S(1)}, u32[]{:S(2)}, u32[]{:S(2)}) collective-permute-start(bf16[384,256]{1,0:T(8,128)(2,1)S(1)} %collective-permute-done.3.rest_3_), channel_id=1, source_target_pairs={{0,1},{1,0},{2,3},{3,2},{4,5},{5,4},{6,7},{7,6},{8,9},{9,8},{10,11... | collective-permute-start | bytes 589832 | tf_op jit(solution)/shard_map/ppermute | solution.py:27
  28.4 9.4 %collective-permute-start.9 = (bf16[384,256]{1,0:T(8,128)(2,1)S(1)}, bf16[384,256]{1,0:T(8,128)(2,1)S(1)}, u32[]{:S(2)}, u32[]{:S(2)}) collective-permute-start(bf16[384,256]{1,0:T(8,128)(2,1)S(1)} %collective-permute-done.1.rest_1_), channel_id=1, source_target_pairs={{0,1},{1,0},{2,3},{3,2},{4,5},{5,4},{6,7},{7,6},{8,9},{9,8},{10,11... | collective-permute-start | bytes 589832 | tf_op jit(solution)/shard_map/ppermute | solution.py:27
  29.2 9.0 %collective-permute-start.7 = (bf16[384,256]{1,0:T(8,128)(2,1)S(1)}, bf16[384,256]{1,0:T(8,128)(2,1)S(1)}, u32[]{:S(2)}, u32[]{:S(2)}) collective-permute-start(bf16[384,256]{1,0:T(8,128)(2,1)S(1)} %collective-permute-done.6.rest_6_), channel_id=1, source_target_pairs={{0,6},{1,7},{2,0},{3,1},{4,2},{5,3},{6,4},{7,5},{8,14},{9,15},{10,... | collective-permute-start | bytes 589832 | tf_op jit(solution)/shard_map/ppermute | solution.py:27
  32.6 6.4 %collective-permute-start.10 = (bf16[384,256]{1,0:T(8,128)(2,1)S(1)}, bf16[384,256]{1,0:T(8,128)(2,1)S(1)}, u32[]{:S(2)}, u32[]{:S(2)}) collective-permute-start(bf16[384,256]{1,0:T(8,128)(2,1)S(1)} %collective-permute-done.2.rest_2_), channel_id=1, source_target_pairs={{0,1},{1,0},{2,3},{3,2},{4,5},{5,4},{6,7},{7,6},{8,9},{9,8},{10,11... | collective-permute-start | bytes 589832 | tf_op jit(solution)/shard_map/ppermute | solution.py:27
  39.0 10.7 %collective-permute-start.17 = (bf16[384,128]{1,0:T(8,128)(2,1)S(1)}, bf16[384,128]{1,0:T(8,128)(2,1)S(1)}, u32[]{:S(2)}, u32[]{:S(2)}) collective-permute-start(bf16[384,128]{1,0:T(8,128)(2,1)S(1)} %multiply_convert_fusion), channel_id=1, source_target_pairs={{0,16},{16,0},{32,48},{48,32},{64,80},{80,64},{96,112},{112,96},{1... | collective-permute-start | bytes 294920 | tf_op jit(solution)/shard_map/ppermute | solution.py:27
  48.5 6.1 %collective-permute-start.16 = (bf16[256,384]{1,0:T(8,128)(2,1)}, bf16[256,384]{1,0:T(8,128)(2,1)S(1)}, u32[]{:S(2)}, u32[]{:S(2)}) collective-permute-start(bf16[256,384]{1,0:T(8,128)(2,1)} %project.1), channel_id=1, source_target_pairs={{0,16},{16,0},{32,48},{48,32},{64,80},{80,64},{96,112},{112,96},{1... | collective-permute-start | bytes 589832 | tf_op jit(solution)/shard_map/ppermute | solution.py:27
  110.6 12.3 %collective-permute-start.20 = (bf16[16,128,128]{2,1,0:T(8,128)(2,1)}, bf16[16,128,128]{2,1,0:T(8,128)(2,1)S(1)}, u32[]{:S(2)}, u32[]{:S(2)}) collective-permute-start(bf16[16,128,128]{2,1,0:T(8,128)(2,1)} %all_to_all.21.rest_0_), channel_id=1, source_target_pairs={{0,2},{1,3},{2,4},{3,5},{4,6},{5,7},{6,0},{7,1},{8,10},{9,11},{10,... | collective-permute-start | bytes 1572872 | tf_op jit(solution)/shard_map/ppermute | solution.py:27
  111.1 12.7 %collective-permute-start.21 = (bf16[16,128,128]{2,1,0:T(8,128)(2,1)}, bf16[16,128,128]{2,1,0:T(8,128)(2,1)S(1)}, u32[]{:S(2)}, u32[]{:S(2)}) collective-permute-start(bf16[16,128,128]{2,1,0:T(8,128)(2,1)} %all_to_all.21.rest_0_), channel_id=1, source_target_pairs={{0,6},{1,7},{2,0},{3,1},{4,2},{5,3},{6,4},{7,5},{8,14},{9,15},{10,... | collective-permute-start | bytes 1572872 | tf_op jit(solution)/shard_map/ppermute | solution.py:27
  113.3 15.4 %collective-permute-start.18 = (bf16[16,128,128]{2,1,0:T(8,128)(2,1)}, bf16[16,128,128]{2,1,0:T(8,128)(2,1)}, u32[]{:S(2)}, u32[]{:S(2)}) collective-permute-start(bf16[16,128,128]{2,1,0:T(8,128)(2,1)} %all_to_all.21.rest_0_), channel_id=1, source_target_pairs={{0,24},{1,25},{2,26},{3,27},{4,28},{5,29},{6,30},{7,31},{8,16},{9,... | collective-permute-start | bytes 1572872 | tf_op jit(solution)/shard_map/ppermute | solution.py:40
  113.9 14.9 %collective-permute-start.19 = (bf16[16,128,128]{2,1,0:T(8,128)(2,1)}, bf16[16,128,128]{2,1,0:T(8,128)(2,1)}, u32[]{:S(2)}, u32[]{:S(2)}) collective-permute-start(bf16[16,128,128]{2,1,0:T(8,128)(2,1)} %all_to_all.21.rest_0_), channel_id=1, source_target_pairs={{0,1},{1,0},{2,3},{3,2},{4,5},{5,4},{6,7},{7,6},{8,9},{9,8},{10,11... | collective-permute-start | bytes 1572872 | tf_op jit(solution)/shard_map/ppermute | solution.py:27
  123.0 9.7 %collective-permute-start.22 = (bf16[8,128,128]{2,1,0:T(8,128)(2,1)S(1)}, bf16[8,128,128]{2,1,0:T(8,128)(2,1)}, u32[]{:S(2)}, u32[]{:S(2)}) collective-permute-start(bf16[8,128,128]{2,1,0:T(8,128)(2,1)S(1)} %slice.22), channel_id=1, source_target_pairs={{0,2},{1,3},{2,4},{3,5},{4,6},{5,7},{6,0},{7,1},{8,10},{9,11},{10,... | collective-permute-start | bytes 786440 | tf_op jit(solution)/shard_map/ppermute | solution.py:27
  125.3 7.4 %collective-permute-start.23 = (bf16[8,128,128]{2,1,0:T(8,128)(2,1)}, bf16[8,128,128]{2,1,0:T(8,128)(2,1)}, u32[]{:S(2)}, u32[]{:S(2)}) collective-permute-start(bf16[8,128,128]{2,1,0:T(8,128)(2,1)} %slice.23), channel_id=1, source_target_pairs={{0,6},{1,7},{2,0},{3,1},{4,2},{5,3},{6,4},{7,5},{8,14},{9,15},{10,... | collective-permute-start | bytes 786440 | tf_op jit(solution)/shard_map/ppermute | solution.py:27
  128.8 6.6 %collective-permute-start.26 = (bf16[16,128,128]{2,1,0:T(8,128)(2,1)}, bf16[16,128,128]{2,1,0:T(8,128)(2,1)S(1)}, u32[]{:S(2)}, u32[]{:S(2)}) collective-permute-start(bf16[16,128,128]{2,1,0:T(8,128)(2,1)} %collective-permute-done.18.rest_3_), channel_id=1, source_target_pairs={{0,1},{1,0},{2,3},{3,2},{4,5},{5,4},{6,7},{7,6},{8,9},{9,8},{10,11... | collective-permute-start | bytes 1572872 | tf_op jit(solution)/shard_map/ppermute | solution.py:27
  132.7 13.3 %collective-permute-start.27 = (bf16[16,128,128]{2,1,0:T(8,128)(2,1)}, bf16[16,128,128]{2,1,0:T(8,128)(2,1)S(1)}, u32[]{:S(2)}, u32[]{:S(2)}) collective-permute-start(bf16[16,128,128]{2,1,0:T(8,128)(2,1)} %collective-permute-done.18.rest_3_), channel_id=1, source_target_pairs={{0,2},{1,3},{2,4},{3,5},{4,6},{5,7},{6,0},{7,1},{8,10},{9,11},{10,... | collective-permute-start | bytes 1572872 | tf_op jit(solution)/shard_map/ppermute | solution.py:27
  132.7 15.8 %collective-permute-start.28 = (bf16[16,128,128]{2,1,0:T(8,128)(2,1)}, bf16[16,128,128]{2,1,0:T(8,128)(2,1)S(1)}, u32[]{:S(2)}, u32[]{:S(2)}) collective-permute-start(bf16[16,128,128]{2,1,0:T(8,128)(2,1)} %collective-permute-done.18.rest_3_), channel_id=1, source_target_pairs={{0,6},{1,7},{2,0},{3,1},{4,2},{5,3},{6,4},{7,5},{8,14},{9,15},{10,... | collective-permute-start | bytes 1572872 | tf_op jit(solution)/shard_map/ppermute | solution.py:27
  135.4 13.5 %collective-permute-start.29 = (bf16[8,128,128]{2,1,0:T(8,128)(2,1)}, bf16[8,128,128]{2,1,0:T(8,128)(2,1)S(1)}, u32[]{:S(2)}, u32[]{:S(2)}) collective-permute-start(bf16[8,128,128]{2,1,0:T(8,128)(2,1)} %collective-permute-done.22.rest_4_), channel_id=1, source_target_pairs={{0,24},{1,25},{2,26},{3,27},{4,28},{5,29},{6,30},{7,31},{8,16},{9,... | collective-permute-start | bytes 786440 | tf_op jit(solution)/shard_map/ppermute | solution.py:40
  136.1 13.0 %collective-permute-start.30 = (bf16[8,128,128]{2,1,0:T(8,128)(2,1)}, bf16[8,128,128]{2,1,0:T(8,128)(2,1)}, u32[]{:S(2)}, u32[]{:S(2)}) collective-permute-start(bf16[8,128,128]{2,1,0:T(8,128)(2,1)} %collective-permute-done.23.rest_5_), channel_id=1, source_target_pairs={{0,24},{1,25},{2,26},{3,27},{4,28},{5,29},{6,30},{7,31},{8,16},{9,... | collective-permute-start | bytes 786440 | tf_op jit(solution)/shard_map/ppermute | solution.py:40
  146.0 14.7 %collective-permute-start.33 = (bf16[16,128,128]{2,1,0:T(8,128)(2,1)S(1)}, bf16[16,128,128]{2,1,0:T(8,128)(2,1)S(1)}, u32[]{:S(2)}, u32[]{:S(2)}) collective-permute-start(bf16[16,128,128]{2,1,0:T(8,128)(2,1)S(1)} %collective-permute-done.27.rest_6_), channel_id=1, source_target_pairs={{0,1},{1,0},{2,3},{3,2},{4,5},{5,4},{6,7},{7,6},{8,9},{9,8},{10,11... | collective-permute-start | bytes 1572872 | tf_op jit(solution)/shard_map/ppermute | solution.py:27
  148.4 12.3 %collective-permute-start.34 = (bf16[16,128,128]{2,1,0:T(8,128)(2,1)S(1)}, bf16[16,128,128]{2,1,0:T(8,128)(2,1)}, u32[]{:S(2)}, u32[]{:S(2)}) collective-permute-start(bf16[16,128,128]{2,1,0:T(8,128)(2,1)S(1)} %collective-permute-done.28.rest_7_), channel_id=1, source_target_pairs={{0,1},{1,0},{2,3},{3,2},{4,5},{5,4},{6,7},{7,6},{8,9},{9,8},{10,11... | collective-permute-start | bytes 1572872 | tf_op jit(solution)/shard_map/ppermute | solution.py:27
  149.0 11.8 %collective-permute-start.32 = (bf16[8,128,128]{2,1,0:T(8,128)(2,1)}, bf16[8,128,128]{2,1,0:T(8,128)(2,1)}, u32[]{:S(2)}, u32[]{:S(2)}) collective-permute-start(bf16[8,128,128]{2,1,0:T(8,128)(2,1)} %collective-permute-done.23.rest_5_), channel_id=1, source_target_pairs={{0,1},{1,0},{2,3},{3,2},{4,5},{5,4},{6,7},{7,6},{8,9},{9,8},{10,11... | collective-permute-start | bytes 786440 | tf_op jit(solution)/shard_map/ppermute | solution.py:27
  149.1 11.7 %collective-permute-start.35 = (bf16[8,128,128]{2,1,0:T(8,128)(2,1)S(1)}, bf16[8,128,128]{2,1,0:T(8,128)(2,1)}, u32[]{:S(2)}, u32[]{:S(2)}) collective-permute-start(bf16[8,128,128]{2,1,0:T(8,128)(2,1)S(1)} %collective-permute-done.29.rest_8_), channel_id=1, source_target_pairs={{0,1},{1,0},{2,3},{3,2},{4,5},{5,4},{6,7},{7,6},{8,9},{9,8},{10,11... | collective-permute-start | bytes 786440 | tf_op jit(solution)/shard_map/ppermute | solution.py:27
  151.4 10.4 %collective-permute-start.36 = (bf16[8,128,128]{2,1,0:T(8,128)(2,1)}, bf16[8,128,128]{2,1,0:T(8,128)(2,1)}, u32[]{:S(2)}, u32[]{:S(2)}) collective-permute-start(bf16[8,128,128]{2,1,0:T(8,128)(2,1)} %collective-permute-done.30.rest_9_), channel_id=1, source_target_pairs={{0,1},{1,0},{2,3},{3,2},{4,5},{5,4},{6,7},{7,6},{8,9},{9,8},{10,11... | collective-permute-start | bytes 786440 | tf_op jit(solution)/shard_map/ppermute | solution.py:27
  184.9 18.4 %collective-permute-start.38 = (bf16[8,256,384]{2,1,0:T(8,128)(2,1)}, bf16[8,256,384]{2,1,0:T(8,128)(2,1)}, u32[]{:S(2)}, u32[]{:S(2)}) collective-permute-start(bf16[8,256,384]{2,1,0:T(8,128)(2,1)} %get-tuple-element.40), channel_id=1, source_target_pairs={{0,1},{1,0},{2,3},{3,2},{4,5},{5,4},{6,7},{7,6},{8,9},{9,8},{10,11... | collective-permute-start | bytes 4718600 | tf_op jit(solution)/shard_map/ppermute | solution.py:27
  187.0 16.2 %all-to-all-start.2 = ((bf16[8,256,128]{2,1,0:T(8,128)(2,1)}), bf16[8,256,128]{2,1,0:T(8,128)(2,1)S(1)}, u32[]{:S(2)}, u32[]{:S(2)}) async-start(bf16[8,256,128]{2,1,0:T(8,128)(2,1)} %add_convert_fusion.1), calls=%async_computation.2 | async-start | bytes 1048576 | tf_op jit(solution)/shard_map/all_to_all | solution.py:110
  191.5 46.0 %all-gather.11.cloned.1.call-start = ((), (), s32[]{:S(2)}) async-start(), calls=%async_computation.6 | async-start | bytes 1769472 | tf_op jit(solution)/shard_map/all_gather | solution.py:100
  (42 other events, 379.1 us)
Sparse Core Ops, SparseCore 0:
  13.5 40.1 all-gather.6
  56.5 60.0 all-gather.8
  194.7 34.2 all-gather.10

commit v4 on v3

--- a/solution.py
+++ b/solution.py
@@ -52,7 +52,7 @@
     return near + [swap(piece) for piece in near]
 
 
-def gather_table(slab, norm):
+def gather_table(slab):
     half = slab.shape[0] // 2
     slab_swap = swap(slab)
     left = hop(slab, "fsdp", 2, 4, 1)
@@ -60,7 +60,7 @@
     other = across(slab)
     far_a = hop(left[:half], "fsdp", 2, 4, 1)
     far_b = hop(right[half:], "fsdp", 2, 4, -1)
-    other, slab_swap, norm = lax.optimization_barrier((other, slab_swap, norm))
+    other, slab_swap = lax.optimization_barrier((other, slab_swap))
     other_left = hop(other, "fsdp", 2, 4, 1)
     other_right = hop(other, "fsdp", 2, 4, -1)
     early = [swap(left), swap(right), swap(other)]
@@ -68,7 +68,7 @@
     other_far = [across(far_a), across(far_b)]
     near = [slab, left, right, other, far_a, far_b, other_left, other_right] + other_far
     late = [swap(piece) for piece in near[4:]]
-    return near + [slab_swap] + early + late, norm
+    return near + [slab_swap] + early + late
 
 
 def places():
@@ -350,7 +350,7 @@
     chosen = lax.all_to_all(chosen, "fsdp", 0, 0, tiled=True)
     block = jnp.sum(chosen.astype(F32), axis=0).astype(BF16)
     block, late = lax.optimization_barrier((block, late))
-    table, norm = gather_table(gather_section(block), norm)
+    table = gather_table(gather_section(block))
     down_all = along_z(late)
 
     cross, cross_out, part, part_out = chain_call(place, projected, norm, x, y, table)

time: 257 us -> 254 us (0.988)
  waiting for transfers between devices: 37.3 us -> 29.1 us
  starting transfers between devices: 65.1 us -> 72.1 us
    ppermute x37, waiting for transfers between devices: 25.6 us -> 17.4 us  [hop(): return lax.ppermute(block, axis, route)]
    ppermute x37, starting transfers between devices: 57.2 us -> 65.2 us  [hop(): return lax.ppermute(block, axis, route)]
  transfers between devices with their start and end apart: 44 -> 44, of which waited for: 9 -> 10; matrix products, arithmetic and copies ran while one was open for 6% -> 6% of each run, Pallas kernels for 3% -> 3%
where the time goes in v4:
time: 254 us; the launch traced here: 249 us
  blocking collectives  80.4 us (32%)
  starting transfers between devices  72.1 us (28%)
  Pallas kernels  34.5 us (14%)
  waiting for transfers between devices  29.1 us (11%)
  between operations  14.5 us (6%)
  other arithmetic  10.8 us (4%)
  local copies, waits for them, and re-layouts  5.81 us (2%)
    ppermute x37, starting transfers between devices, hop(): return lax.ppermute(block, axis, route)  65.2 us
    all_to_all x1, blocking collectives, among_chips(): lax.all_to_all(chunks, 'fsdp', 0, 0, tiled=True, axis_index_groups=chips)  30.1 us
    all_to_all x1, blocking collectives, gather_section(): lax.all_to_all(jnp.broadcast_to(block[None], (16,) + block.shape), 'secti...  29.8 us
    pallas_call x1, Pallas kernels, chain_call(): pl.pallas_call(functools.partial(chain, width), out_shape=(jax.ShapeDtype...  20.8 us
    all_to_all x1, blocking collectives, on_device(): chosen = lax.all_to_all(chosen, 'fsdp', 0, 0, tiled=True)  20.5 us
    ppermute x37, waiting for transfers between devices, hop(): return lax.ppermute(block, axis, route)  17.4 us
    all_to_all x1, waiting for transfers between devices, among_chips(): lax.all_to_all(chunks, 'fsdp', 0, 0, tiled=True, axis_index_groups=chips)  11 us
    pallas_call x1, Pallas kernels, on_device(): pl.pallas_call(project, out_shape=jax.ShapeDtypeStruct((tokens, 3 * rank)...  7.97 us
  transfers between devices with their start and end apart: 44, of which 10 were waited for; matrix products, arithmetic and copies ran while one was open for 6% of the time, Pallas kernels for 3%

profile of v4, /device:TPU:1, one launch (start us, length us, event | category | flops | bytes accessed | tf_op | source)
XLA Modules:
  0.0 249.3 jit_solution(13235785670757223052)
XLA Ops:
  8.2 2.2 collective-permute-start
  10.4 2.0 collective-permute-done
  15.1 3.2 %collective-permute-start.3 = (bf16[384,256]{1,0:T(8,128)(2,1)S(1)}, bf16[384,256]{1,0:T(8,128)(2,1)S(1)}, u32[]{:S(2)}, u32[]{:S(2)}) collective-permute-start(bf16[384,256]{1,0:T(8,128)(2,1)S(1)} %pad_maximum_fusion.3.rest_0_), channel_id=1, source_target_pairs={{0,8},{1,9},{2,10},{3,11},{4,12},{5,13},{6,14},{7,15},{8,0},{9,1},... | collective-permute-start | bytes 589832 | tf_op jit(solution)/shard_map/ppermute | solution.py:27
  21.0 2.7 %collective-permute-start.8 = (bf16[384,256]{1,0:T(8,128)(2,1)S(1)}, bf16[384,256]{1,0:T(8,128)(2,1)S(1)}, u32[]{:S(2)}, u32[]{:S(2)}) collective-permute-start(bf16[384,256]{1,0:T(8,128)(2,1)S(1)} %pad_maximum_fusion.3.rest_0_), channel_id=1, source_target_pairs={{0,1},{1,0},{2,3},{3,2},{4,5},{5,4},{6,7},{7,6},{8,9},{9,8},{10,11... | collective-permute-start | bytes 589832 | tf_op jit(solution)/shard_map/ppermute | solution.py:27
  25.2 3.1 %collective-permute-start.11 = (bf16[384,256]{1,0:T(8,128)(2,1)S(1)}, bf16[384,256]{1,0:T(8,128)(2,1)S(1)}, u32[]{:S(2)}, u32[]{:S(2)}) collective-permute-start(bf16[384,256]{1,0:T(8,128)(2,1)S(1)} %collective-permute-done.3.rest_3_), channel_id=1, source_target_pairs={{0,1},{1,0},{2,3},{3,2},{4,5},{5,4},{6,7},{7,6},{8,9},{9,8},{10,11... | collective-permute-start | bytes 589832 | tf_op jit(solution)/shard_map/ppermute | solution.py:27
  29.2 3.4 %collective-permute-start.7 = (bf16[384,256]{1,0:T(8,128)(2,1)S(1)}, bf16[384,256]{1,0:T(8,128)(2,1)S(1)}, u32[]{:S(2)}, u32[]{:S(2)}) collective-permute-start(bf16[384,256]{1,0:T(8,128)(2,1)S(1)} %collective-permute-done.6.rest_6_), channel_id=1, source_target_pairs={{0,6},{1,7},{2,0},{3,1},{4,2},{5,3},{6,4},{7,5},{8,14},{9,15},{10,... | collective-permute-start | bytes 589832 | tf_op jit(solution)/shard_map/ppermute | solution.py:27
  32.6 2.9 %collective-permute-start.10 = (bf16[384,256]{1,0:T(8,128)(2,1)S(1)}, bf16[384,256]{1,0:T(8,128)(2,1)S(1)}, u32[]{:S(2)}, u32[]{:S(2)}) collective-permute-start(bf16[384,256]{1,0:T(8,128)(2,1)S(1)} %collective-permute-done.2.rest_2_), channel_id=1, source_target_pairs={{0,1},{1,0},{2,3},{3,2},{4,5},{5,4},{6,7},{7,6},{8,9},{9,8},{10,11... | collective-permute-start | bytes 589832 | tf_op jit(solution)/shard_map/ppermute | solution.py:27
  35.6 2.1 collective-permute-start.14
  40.5 8.0 %project.1 = bf16[256,384]{1,0:T(8,128)(2,1)} custom-call(s32[18]{0:T(128)} %stack.102.place_ref.s_ref, bf16[256,6144]{1,0:T(8,128)(2,1)} %bitcast.47, bf16[256,6144]{1,0:T(8,128)(2,1)} %bitcast.54, bf16[384,256]{1,0:T(8,128)(2,1)} %copy-done.6, bf16[384,256]{1,0:T(8,128)(2,1)} %copy-done.18, bf16[384,256]{1,0:T(8,128)(2,1)} %copy-done.19, ...), custom_call_target="tpu_custom_call" | custom-call | flops 8000000000 | bytes 9437184 | tf_op jit(solution)/shard_map/project/pallas_call | solution.py:323
  50.4 4.1 %collective-permute-done.16 = bf16[256,384]{1,0:T(8,128)(2,1)S(1)} collective-permute-done((bf16[256,384]{1,0:T(8,128)(2,1)}, bf16[256,384]{1,0:T(8,128)(2,1)S(1)}, u32[]{:S(2)}, u32[]{:S(2)}) %collective-permute-start.16) | collective-permute-done | bytes 196640 | tf_op jit(solution)/shard_map/ppermute | solution.py:27
  56.3 2.1 fusion.5
  58.9 20.5 %all_to_all.20 = bf16[16,128,128]{2,1,0:T(8,128)(2,1)} all-to-all(bf16[16,128,128]{2,1,0:T(8,128)(2,1)S(1)} %bitcast.49), channel_id=1, replica_groups=mesh['section'=16,'fsdp'=16] {'fsdp'}, dimensions={0} | all-to-all | bytes 1048576 | tf_op jit(solution)/shard_map/all_to_all | solution.py:350
  80.6 29.8 %all_to_all.21.rest_0_ = bf16[16,128,128]{2,1,0:T(8,128)(2,1)S(1)} all-to-all(bf16[16,128,128]{2,1,0:T(8,128)(2,1)S(1)} %broadcast_in_dim.32), channel_id=1, replica_groups=mesh['section'=16,'fsdp'=16] {'section'}, dimensions={0} | all-to-all | bytes 1048576 | tf_op jit(solution)/shard_map/all_to_all | solution.py:87
  110.9 2.2 collective-permute-start.19
  113.7 2.7 %collective-permute-start.21 = (bf16[16,128,128]{2,1,0:T(8,128)(2,1)S(1)}, bf16[16,128,128]{2,1,0:T(8,128)(2,1)S(1)}, u32[]{:S(2)}, u32[]{:S(2)}) collective-permute-start(bf16[16,128,128]{2,1,0:T(8,128)(2,1)S(1)} %all_to_all.21.rest_0_), channel_id=1, source_target_pairs={{0,1},{1,0},{2,3},{3,2},{4,5},{5,4},{6,7},{7,6},{8,9},{9,8},{10,11... | collective-permute-start | bytes 1572872 | tf_op jit(solution)/shard_map/ppermute | solution.py:27
  116.4 6.0 %collective-permute-done.18.rest_1_ = bf16[16,128,128]{2,1,0:T(8,128)(2,1)S(1)} collective-permute-done((bf16[16,128,128]{2,1,0:T(8,128)(2,1)S(1)}, bf16[16,128,128]{2,1,0:T(8,128)(2,1)S(1)}, u32[]{:S(2)}, u32[]{:S(2)}) %collective-permute-start.18) | collective-permute-done | bytes 524320 | tf_op jit(solution)/shard_map/ppermute | solution.py:27
  122.7 2.7 %collective-permute-start.23 = (bf16[8,128,128]{2,1,0:T(8,128)(2,1)S(1)}, bf16[8,128,128]{2,1,0:T(8,128)(2,1)}, u32[]{:S(2)}, u32[]{:S(2)}) collective-permute-start(bf16[8,128,128]{2,1,0:T(8,128)(2,1)S(1)} %slice.23), channel_id=1, source_target_pairs={{0,6},{1,7},{2,0},{3,1},{4,2},{5,3},{6,4},{7,5},{8,14},{9,15},{10,... | collective-permute-start | bytes 786440 | tf_op jit(solution)/shard_map/ppermute | solution.py:27
  125.4 4.2 %collective-permute-start.26 = (bf16[16,128,128]{2,1,0:T(8,128)(2,1)S(1)}, bf16[16,128,128]{2,1,0:T(8,128)(2,1)S(1)}, u32[]{:S(2)}, u32[]{:S(2)}) collective-permute-start(bf16[16,128,128]{2,1,0:T(8,128)(2,1)S(1)} %collective-permute-done.20.rest_3_), channel_id=1, source_target_pairs={{0,1},{1,0},{2,3},{3,2},{4,5},{5,4},{6,7},{7,6},{8,9},{9,8},{10,11... | collective-permute-start | bytes 1572872 | tf_op jit(solution)/shard_map/ppermute | solution.py:27
  130.1 2.7 %collective-permute-start.28 = (bf16[16,128,128]{2,1,0:T(8,128)(2,1)S(1)}, bf16[16,128,128]{2,1,0:T(8,128)(2,1)}, u32[]{:S(2)}, u32[]{:S(2)}) collective-permute-start(bf16[16,128,128]{2,1,0:T(8,128)(2,1)S(1)} %collective-permute-done.20.rest_3_), channel_id=1, source_target_pairs={{0,6},{1,7},{2,0},{3,1},{4,2},{5,3},{6,4},{7,5},{8,14},{9,15},{10,... | collective-permute-start | bytes 1572872 | tf_op jit(solution)/shard_map/ppermute | solution.py:27
  133.5 2.1 collective-permute-start.30
  135.6 4.9 %collective-permute-start.31 = (bf16[8,128,128]{2,1,0:T(8,128)(2,1)S(1)}, bf16[8,128,128]{2,1,0:T(8,128)(2,1)S(1)}, u32[]{:S(2)}, u32[]{:S(2)}) collective-permute-start(bf16[8,128,128]{2,1,0:T(8,128)(2,1)S(1)} %collective-permute-done.22.rest_4_), channel_id=1, source_target_pairs={{0,1},{1,0},{2,3},{3,2},{4,5},{5,4},{6,7},{7,6},{8,9},{9,8},{10,11... | collective-permute-start | bytes 786440 | tf_op jit(solution)/shard_map/ppermute | solution.py:27
  141.2 4.5 %collective-permute-start.33 = (bf16[16,128,128]{2,1,0:T(8,128)(2,1)}, bf16[16,128,128]{2,1,0:T(8,128)(2,1)}, u32[]{:S(2)}, u32[]{:S(2)}) collective-permute-start(bf16[16,128,128]{2,1,0:T(8,128)(2,1)} %collective-permute-done.27.rest_6_), channel_id=1, source_target_pairs={{0,1},{1,0},{2,3},{3,2},{4,5},{5,4},{6,7},{7,6},{8,9},{9,8},{10,11... | collective-permute-start | bytes 1572872 | tf_op jit(solution)/shard_map/ppermute | solution.py:27
  146.3 2.3 collective-permute-start.35
  149.3 8.5 %collective-permute-start.36 = (bf16[8,128,128]{2,1,0:T(8,128)(2,1)}, bf16[8,128,128]{2,1,0:T(8,128)(2,1)}, u32[]{:S(2)}, u32[]{:S(2)}) collective-permute-start(bf16[8,128,128]{2,1,0:T(8,128)(2,1)} %collective-permute-done.30.rest_9_), channel_id=1, source_target_pairs={{0,1},{1,0},{2,3},{3,2},{4,5},{5,4},{6,7},{7,6},{8,9},{9,8},{10,11... | collective-permute-start | bytes 786440 | tf_op jit(solution)/shard_map/ppermute | solution.py:27
  159.7 20.8 %chain.1 = (bf16[8,256,128]{2,1,0:T(8,128)(2,1)}, bf16[8,256,128]{2,1,0:T(8,128)(2,1)}, bf16[8,256,384]{2,1,0:T(8,128)(2,1)}, bf16[8,256,384]{2,1,0:T(8,128)(2,1)}) custom-call(s32[18]{0:T(128)} %stack.102.place_ref.s_ref, s32[18]{0:T(128)} %stack.102.place_ref.s_ref, bf16[16,256,384]{2,1,0:T(8,128)(2,1)} %all-gather.9.cloned.1.call-done.a_hbm, ...), custom_call_target="tpu_custom_call" | custom-call | flops 20000000000 | bytes 12582912 | tf_op jit(solution)/shard_map/chain/pallas_call | solution.py:247
  180.9 1.9 collective-permute-done.37
  183.0 2.0 add_convert_fusion.1
  185.0 3.5 %all-to-all-start.2 = ((bf16[8,256,128]{2,1,0:T(8,128)(2,1)}), bf16[8,256,128]{2,1,0:T(8,128)(2,1)S(1)}, u32[]{:S(2)}, u32[]{:S(2)}) async-start(bf16[8,256,128]{2,1,0:T(8,128)(2,1)} %add_convert_fusion.1), calls=%async_computation.2 | async-start | bytes 1048576 | tf_op jit(solution)/shard_map/all_to_all | solution.py:110
  189.2 11.0 %all-to-all-done.2 = bf16[8,256,128]{2,1,0:T(8,128)(2,1)S(1)} async-done(((bf16[8,256,128]{2,1,0:T(8,128)(2,1)}), bf16[8,256,128]{2,1,0:T(8,128)(2,1)S(1)}, u32[]{:S(2)}, u32[]{:S(2)}) %all-to-all-start.2) | async-done | bytes 524320 | tf_op jit(solution)/shard_map/all_to_all | solution.py:110
  200.3 1.9 add_convert_fusion
  202.5 30.1 %all_to_all.22.part_ref = bf16[8,256,512]{2,1,0:T(8,128)(2,1)S(1)} all-to-all(bf16[8,256,512]{2,1,0:T(8,128)(2,1)S(1)} %pad_maximum_fusion), channel_id=1, replica_groups={{0,2,4,6,8,10,12,14},{1,3,5,7,9,11,13,15},{16,18,20,22,24,26,28,30},{17..., dimensions={0} | all-to-all | bytes 4194304 | tf_op jit(solution)/shard_map/all_to_all | solution.py:110
  236.9 5.7 %finish.1 = (f32[384,128]{1,0:T(8,128)}, f32[1,384]{1,0:T(1,128)}, f32[128,384]{1,0:T(8,128)}) custom-call(s32[18]{0:T(128)} %stack.102.place_ref.s_ref, bf16[8,256,512]{2,1,0:T(8,128)(2,1)} %copy-done, bf16[8,256,128]{2,1,0:T(8,128)(2,1)} %copy-done.5, bf16[16,128,384]{2,1,0:T(8,128)(2,1)} %all-gather.7.cloned.1.call-done.up_hbm, ...), custom_call_target="tpu_custom_call" | custom-call | tf_op jit(solution)/shard_map/finish/pallas_call | solution.py:366
  (156 shorter events, 29.0 us)
Async XLA Ops:
  7.2 49.1 %all-gather.7.cloned.1.call-start = ((), (), s32[]{:S(2)}) async-start(), calls=%async_computation.4 | async-start | bytes 1769472 | tf_op jit(solution)/shard_map/all_gather | solution.py:100
  13.3 146.3 %all-gather.9.cloned.1.call-start = ((), (), s32[]{:S(2)}) async-start(), calls=%async_computation.5 | async-start | bytes 3538944 | tf_op jit(solution)/shard_map/all_gather | solution.py:100
  15.1 8.5 %collective-permute-start.3 = (bf16[384,256]{1,0:T(8,128)(2,1)S(1)}, bf16[384,256]{1,0:T(8,128)(2,1)S(1)}, u32[]{:S(2)}, u32[]{:S(2)}) collective-permute-start(bf16[384,256]{1,0:T(8,128)(2,1)S(1)} %pad_maximum_fusion.3.rest_0_), channel_id=1, source_target_pairs={{0,8},{1,9},{2,10},{3,11},{4,12},{5,13},{6,14},{7,15},{8,0},{9,1},... | collective-permute-start | bytes 589832 | tf_op jit(solution)/shard_map/ppermute | solution.py:27
  18.3 6.8 %collective-permute-start.1 = (bf16[384,256]{1,0:T(8,128)(2,1)S(1)}, bf16[384,256]{1,0:T(8,128)(2,1)S(1)}, u32[]{:S(2)}, u32[]{:S(2)}) collective-permute-start(bf16[384,256]{1,0:T(8,128)(2,1)S(1)} %pad_maximum_fusion.3.rest_0_), channel_id=1, source_target_pairs={{0,2},{1,3},{2,4},{3,5},{4,6},{5,7},{6,0},{7,1},{8,10},{9,11},{10,... | collective-permute-start | bytes 589832 | tf_op jit(solution)/shard_map/ppermute | solution.py:27
  21.0 7.4 %collective-permute-start.8 = (bf16[384,256]{1,0:T(8,128)(2,1)S(1)}, bf16[384,256]{1,0:T(8,128)(2,1)S(1)}, u32[]{:S(2)}, u32[]{:S(2)}) collective-permute-start(bf16[384,256]{1,0:T(8,128)(2,1)S(1)} %pad_maximum_fusion.3.rest_0_), channel_id=1, source_target_pairs={{0,1},{1,0},{2,3},{3,2},{4,5},{5,4},{6,7},{7,6},{8,9},{9,8},{10,11... | collective-permute-start | bytes 589832 | tf_op jit(solution)/shard_map/ppermute | solution.py:27
  24.9 7.7 %collective-permute-start.5 = (bf16[384,256]{1,0:T(8,128)(2,1)S(1)}, bf16[384,256]{1,0:T(8,128)(2,1)S(1)}, u32[]{:S(2)}, u32[]{:S(2)}) collective-permute-start(bf16[384,256]{1,0:T(8,128)(2,1)S(1)} %collective-permute-done.3.rest_3_), channel_id=1, source_target_pairs={{0,2},{1,3},{2,4},{3,5},{4,6},{5,7},{6,0},{7,1},{8,10},{9,11},{10,... | collective-permute-start | bytes 589832 | tf_op jit(solution)/shard_map/ppermute | solution.py:27
  25.1 10.4 %collective-permute-start.4 = (bf16[384,256]{1,0:T(8,128)(2,1)S(1)}, bf16[384,256]{1,0:T(8,128)(2,1)S(1)}, u32[]{:S(2)}, u32[]{:S(2)}) collective-permute-start(bf16[384,256]{1,0:T(8,128)(2,1)S(1)} %collective-permute-done.1.rest_1_), channel_id=1, source_target_pairs={{0,2},{1,3},{2,4},{3,5},{4,6},{5,7},{6,0},{7,1},{8,10},{9,11},{10,... | collective-permute-start | bytes 589832 | tf_op jit(solution)/shard_map/ppermute | solution.py:27
  25.2 12.5 %collective-permute-start.11 = (bf16[384,256]{1,0:T(8,128)(2,1)S(1)}, bf16[384,256]{1,0:T(8,128)(2,1)S(1)}, u32[]{:S(2)}, u32[]{:S(2)}) collective-permute-start(bf16[384,256]{1,0:T(8,128)(2,1)S(1)} %collective-permute-done.3.rest_3_), channel_id=1, source_target_pairs={{0,1},{1,0},{2,3},{3,2},{4,5},{5,4},{6,7},{7,6},{8,9},{9,8},{10,11... | collective-permute-start | bytes 589832 | tf_op jit(solution)/shard_map/ppermute | solution.py:27
  28.4 9.4 %collective-permute-start.9 = (bf16[384,256]{1,0:T(8,128)(2,1)S(1)}, bf16[384,256]{1,0:T(8,128)(2,1)S(1)}, u32[]{:S(2)}, u32[]{:S(2)}) collective-permute-start(bf16[384,256]{1,0:T(8,128)(2,1)S(1)} %collective-permute-done.1.rest_1_), channel_id=1, source_target_pairs={{0,1},{1,0},{2,3},{3,2},{4,5},{5,4},{6,7},{7,6},{8,9},{9,8},{10,11... | collective-permute-start | bytes 589832 | tf_op jit(solution)/shard_map/ppermute | solution.py:27
  29.2 9.0 %collective-permute-start.7 = (bf16[384,256]{1,0:T(8,128)(2,1)S(1)}, bf16[384,256]{1,0:T(8,128)(2,1)S(1)}, u32[]{:S(2)}, u32[]{:S(2)}) collective-permute-start(bf16[384,256]{1,0:T(8,128)(2,1)S(1)} %collective-permute-done.6.rest_6_), channel_id=1, source_target_pairs={{0,6},{1,7},{2,0},{3,1},{4,2},{5,3},{6,4},{7,5},{8,14},{9,15},{10,... | collective-permute-start | bytes 589832 | tf_op jit(solution)/shard_map/ppermute | solution.py:27
  32.6 6.3 %collective-permute-start.10 = (bf16[384,256]{1,0:T(8,128)(2,1)S(1)}, bf16[384,256]{1,0:T(8,128)(2,1)S(1)}, u32[]{:S(2)}, u32[]{:S(2)}) collective-permute-start(bf16[384,256]{1,0:T(8,128)(2,1)S(1)} %collective-permute-done.2.rest_2_), channel_id=1, source_target_pairs={{0,1},{1,0},{2,3},{3,2},{4,5},{5,4},{6,7},{7,6},{8,9},{9,8},{10,11... | collective-permute-start | bytes 589832 | tf_op jit(solution)/shard_map/ppermute | solution.py:27
  38.9 10.6 %collective-permute-start.17 = (bf16[384,128]{1,0:T(8,128)(2,1)S(1)}, bf16[384,128]{1,0:T(8,128)(2,1)S(1)}, u32[]{:S(2)}, u32[]{:S(2)}) collective-permute-start(bf16[384,128]{1,0:T(8,128)(2,1)S(1)} %multiply_convert_fusion), channel_id=1, source_target_pairs={{0,16},{16,0},{32,48},{48,32},{64,80},{80,64},{96,112},{112,96},{1... | collective-permute-start | bytes 294920 | tf_op jit(solution)/shard_map/ppermute | solution.py:27
  110.5 12.0 %collective-permute-start.18 = (bf16[16,128,128]{2,1,0:T(8,128)(2,1)S(1)}, bf16[16,128,128]{2,1,0:T(8,128)(2,1)S(1)}, u32[]{:S(2)}, u32[]{:S(2)}) collective-permute-start(bf16[16,128,128]{2,1,0:T(8,128)(2,1)S(1)} %all_to_all.21.rest_0_), channel_id=1, source_target_pairs={{0,2},{1,3},{2,4},{3,5},{4,6},{5,7},{6,0},{7,1},{8,10},{9,11},{10,... | collective-permute-start | bytes 1572872 | tf_op jit(solution)/shard_map/ppermute | solution.py:27
  110.9 11.7 %collective-permute-start.19 = (bf16[16,128,128]{2,1,0:T(8,128)(2,1)S(1)}, bf16[16,128,128]{2,1,0:T(8,128)(2,1)S(1)}, u32[]{:S(2)}, u32[]{:S(2)}) collective-permute-start(bf16[16,128,128]{2,1,0:T(8,128)(2,1)S(1)} %all_to_all.21.rest_0_), channel_id=1, source_target_pairs={{0,6},{1,7},{2,0},{3,1},{4,2},{5,3},{6,4},{7,5},{8,14},{9,15},{10,... | collective-permute-start | bytes 1572872 | tf_op jit(solution)/shard_map/ppermute | solution.py:27
  113.1 12.2 %collective-permute-start.20 = (bf16[16,128,128]{2,1,0:T(8,128)(2,1)S(1)}, bf16[16,128,128]{2,1,0:T(8,128)(2,1)S(1)}, u32[]{:S(2)}, u32[]{:S(2)}) collective-permute-start(bf16[16,128,128]{2,1,0:T(8,128)(2,1)S(1)} %all_to_all.21.rest_0_), channel_id=1, source_target_pairs={{0,24},{1,25},{2,26},{3,27},{4,28},{5,29},{6,30},{7,31},{8,16},{9,... | collective-permute-start | bytes 1572872 | tf_op jit(solution)/shard_map/ppermute | solution.py:40
  113.7 11.7 %collective-permute-start.21 = (bf16[16,128,128]{2,1,0:T(8,128)(2,1)S(1)}, bf16[16,128,128]{2,1,0:T(8,128)(2,1)S(1)}, u32[]{:S(2)}, u32[]{:S(2)}) collective-permute-start(bf16[16,128,128]{2,1,0:T(8,128)(2,1)S(1)} %all_to_all.21.rest_0_), channel_id=1, source_target_pairs={{0,1},{1,0},{2,3},{3,2},{4,5},{5,4},{6,7},{7,6},{8,9},{9,8},{10,11... | collective-permute-start | bytes 1572872 | tf_op jit(solution)/shard_map/ppermute | solution.py:27
  122.5 7.6 %collective-permute-start.22 = (bf16[8,128,128]{2,1,0:T(8,128)(2,1)S(1)}, bf16[8,128,128]{2,1,0:T(8,128)(2,1)S(1)}, u32[]{:S(2)}, u32[]{:S(2)}) collective-permute-start(bf16[8,128,128]{2,1,0:T(8,128)(2,1)S(1)} %slice.22), channel_id=1, source_target_pairs={{0,2},{1,3},{2,4},{3,5},{4,6},{5,7},{6,0},{7,1},{8,10},{9,11},{10,... | collective-permute-start | bytes 786440 | tf_op jit(solution)/shard_map/ppermute | solution.py:27
  122.7 7.4 %collective-permute-start.23 = (bf16[8,128,128]{2,1,0:T(8,128)(2,1)S(1)}, bf16[8,128,128]{2,1,0:T(8,128)(2,1)}, u32[]{:S(2)}, u32[]{:S(2)}) collective-permute-start(bf16[8,128,128]{2,1,0:T(8,128)(2,1)S(1)} %slice.23), channel_id=1, source_target_pairs={{0,6},{1,7},{2,0},{3,1},{4,2},{5,3},{6,4},{7,5},{8,14},{9,15},{10,... | collective-permute-start | bytes 786440 | tf_op jit(solution)/shard_map/ppermute | solution.py:27
  125.4 7.4 %collective-permute-start.26 = (bf16[16,128,128]{2,1,0:T(8,128)(2,1)S(1)}, bf16[16,128,128]{2,1,0:T(8,128)(2,1)S(1)}, u32[]{:S(2)}, u32[]{:S(2)}) collective-permute-start(bf16[16,128,128]{2,1,0:T(8,128)(2,1)S(1)} %collective-permute-done.20.rest_3_), channel_id=1, source_target_pairs={{0,1},{1,0},{2,3},{3,2},{4,5},{5,4},{6,7},{7,6},{8,9},{9,8},{10,11... | collective-permute-start | bytes 1572872 | tf_op jit(solution)/shard_map/ppermute | solution.py:27
  130.1 11.1 %collective-permute-start.27 = (bf16[16,128,128]{2,1,0:T(8,128)(2,1)S(1)}, bf16[16,128,128]{2,1,0:T(8,128)(2,1)}, u32[]{:S(2)}, u32[]{:S(2)}) collective-permute-start(bf16[16,128,128]{2,1,0:T(8,128)(2,1)S(1)} %collective-permute-done.20.rest_3_), channel_id=1, source_target_pairs={{0,2},{1,3},{2,4},{3,5},{4,6},{5,7},{6,0},{7,1},{8,10},{9,11},{10,... | collective-permute-start | bytes 1572872 | tf_op jit(solution)/shard_map/ppermute | solution.py:27
  130.1 15.6 %collective-permute-start.28 = (bf16[16,128,128]{2,1,0:T(8,128)(2,1)S(1)}, bf16[16,128,128]{2,1,0:T(8,128)(2,1)}, u32[]{:S(2)}, u32[]{:S(2)}) collective-permute-start(bf16[16,128,128]{2,1,0:T(8,128)(2,1)S(1)} %collective-permute-done.20.rest_3_), channel_id=1, source_target_pairs={{0,6},{1,7},{2,0},{3,1},{4,2},{5,3},{6,4},{7,5},{8,14},{9,15},{10,... | collective-permute-start | bytes 1572872 | tf_op jit(solution)/shard_map/ppermute | solution.py:27
  132.8 12.9 %collective-permute-start.29 = (bf16[8,128,128]{2,1,0:T(8,128)(2,1)S(1)}, bf16[8,128,128]{2,1,0:T(8,128)(2,1)S(1)}, u32[]{:S(2)}, u32[]{:S(2)}) collective-permute-start(bf16[8,128,128]{2,1,0:T(8,128)(2,1)S(1)} %collective-permute-done.22.rest_4_), channel_id=1, source_target_pairs={{0,24},{1,25},{2,26},{3,27},{4,28},{5,29},{6,30},{7,31},{8,16},{9,... | collective-permute-start | bytes 786440 | tf_op jit(solution)/shard_map/ppermute | solution.py:40
  133.5 12.8 %collective-permute-start.30 = (bf16[8,128,128]{2,1,0:T(8,128)(2,1)}, bf16[8,128,128]{2,1,0:T(8,128)(2,1)}, u32[]{:S(2)}, u32[]{:S(2)}) collective-permute-start(bf16[8,128,128]{2,1,0:T(8,128)(2,1)} %collective-permute-done.23.rest_5_), channel_id=1, source_target_pairs={{0,24},{1,25},{2,26},{3,27},{4,28},{5,29},{6,30},{7,31},{8,16},{9,... | collective-permute-start | bytes 786440 | tf_op jit(solution)/shard_map/ppermute | solution.py:40
  135.6 13.0 %collective-permute-start.31 = (bf16[8,128,128]{2,1,0:T(8,128)(2,1)S(1)}, bf16[8,128,128]{2,1,0:T(8,128)(2,1)S(1)}, u32[]{:S(2)}, u32[]{:S(2)}) collective-permute-start(bf16[8,128,128]{2,1,0:T(8,128)(2,1)S(1)} %collective-permute-done.22.rest_4_), channel_id=1, source_target_pairs={{0,1},{1,0},{2,3},{3,2},{4,5},{5,4},{6,7},{7,6},{8,9},{9,8},{10,11... | collective-permute-start | bytes 786440 | tf_op jit(solution)/shard_map/ppermute | solution.py:27
  141.2 18.1 %collective-permute-start.33 = (bf16[16,128,128]{2,1,0:T(8,128)(2,1)}, bf16[16,128,128]{2,1,0:T(8,128)(2,1)}, u32[]{:S(2)}, u32[]{:S(2)}) collective-permute-start(bf16[16,128,128]{2,1,0:T(8,128)(2,1)} %collective-permute-done.27.rest_6_), channel_id=1, source_target_pairs={{0,1},{1,0},{2,3},{3,2},{4,5},{5,4},{6,7},{7,6},{8,9},{9,8},{10,11... | collective-permute-start | bytes 1572872 | tf_op jit(solution)/shard_map/ppermute | solution.py:27
  145.7 13.6 %collective-permute-start.34 = (bf16[16,128,128]{2,1,0:T(8,128)(2,1)}, bf16[16,128,128]{2,1,0:T(8,128)(2,1)}, u32[]{:S(2)}, u32[]{:S(2)}) collective-permute-start(bf16[16,128,128]{2,1,0:T(8,128)(2,1)} %collective-permute-done.28.rest_7_), channel_id=1, source_target_pairs={{0,1},{1,0},{2,3},{3,2},{4,5},{5,4},{6,7},{7,6},{8,9},{9,8},{10,11... | collective-permute-start | bytes 1572872 | tf_op jit(solution)/shard_map/ppermute | solution.py:27
  145.8 13.6 %collective-permute-start.32 = (bf16[8,128,128]{2,1,0:T(8,128)(2,1)}, bf16[8,128,128]{2,1,0:T(8,128)(2,1)}, u32[]{:S(2)}, u32[]{:S(2)}) collective-permute-start(bf16[8,128,128]{2,1,0:T(8,128)(2,1)} %collective-permute-done.23.rest_5_), channel_id=1, source_target_pairs={{0,1},{1,0},{2,3},{3,2},{4,5},{5,4},{6,7},{7,6},{8,9},{9,8},{10,11... | collective-permute-start | bytes 786440 | tf_op jit(solution)/shard_map/ppermute | solution.py:27
  146.3 13.1 %collective-permute-start.35 = (bf16[8,128,128]{2,1,0:T(8,128)(2,1)S(1)}, bf16[8,128,128]{2,1,0:T(8,128)(2,1)}, u32[]{:S(2)}, u32[]{:S(2)}) collective-permute-start(bf16[8,128,128]{2,1,0:T(8,128)(2,1)S(1)} %collective-permute-done.29.rest_8_), channel_id=1, source_target_pairs={{0,1},{1,0},{2,3},{3,2},{4,5},{5,4},{6,7},{7,6},{8,9},{9,8},{10,11... | collective-permute-start | bytes 786440 | tf_op jit(solution)/shard_map/ppermute | solution.py:27
  149.3 10.4 %collective-permute-start.36 = (bf16[8,128,128]{2,1,0:T(8,128)(2,1)}, bf16[8,128,128]{2,1,0:T(8,128)(2,1)}, u32[]{:S(2)}, u32[]{:S(2)}) collective-permute-start(bf16[8,128,128]{2,1,0:T(8,128)(2,1)} %collective-permute-done.30.rest_9_), channel_id=1, source_target_pairs={{0,1},{1,0},{2,3},{3,2},{4,5},{5,4},{6,7},{7,6},{8,9},{9,8},{10,11... | collective-permute-start | bytes 786440 | tf_op jit(solution)/shard_map/ppermute | solution.py:27
  182.7 17.6 %collective-permute-start.38 = (bf16[8,256,384]{2,1,0:T(8,128)(2,1)}, bf16[8,256,384]{2,1,0:T(8,128)(2,1)}, u32[]{:S(2)}, u32[]{:S(2)}) collective-permute-start(bf16[8,256,384]{2,1,0:T(8,128)(2,1)} %get-tuple-element.38), channel_id=1, source_target_pairs={{0,1},{1,0},{2,3},{3,2},{4,5},{5,4},{6,7},{7,6},{8,9},{9,8},{10,11... | collective-permute-start | bytes 4718600 | tf_op jit(solution)/shard_map/ppermute | solution.py:27
  185.0 15.2 %all-to-all-start.2 = ((bf16[8,256,128]{2,1,0:T(8,128)(2,1)}), bf16[8,256,128]{2,1,0:T(8,128)(2,1)S(1)}, u32[]{:S(2)}, u32[]{:S(2)}) async-start(bf16[8,256,128]{2,1,0:T(8,128)(2,1)} %add_convert_fusion.1), calls=%async_computation.2 | async-start | bytes 1048576 | tf_op jit(solution)/shard_map/all_to_all | solution.py:110
  188.5 46.0 %all-gather.11.cloned.1.call-start = ((), (), s32[]{:S(2)}) async-start(), calls=%async_computation.6 | async-start | bytes 1769472 | tf_op jit(solution)/shard_map/all_gather | solution.py:100
  (44 other events, 435.0 us)
Sparse Core Ops, SparseCore 0:
  13.5 40.4 all-gather.6
  56.4 60.0 all-gather.8
  191.7 34.5 all-gather.10
